TPU v7x, 128 devices: a whole 4x4x4 slice. The times are simulated.
128 devices in a mesh: rows: 4 (over x_lo, core), cols: 32 (over y, x_hi, z).
Axes of the slice: x: 4 (x_hi: 2, x_lo: 2; x = x_hi * 2 + x_lo), y: 4, z: 4, core: 2. Of those that a mesh axis runs over, the one named last changes fastest.
Arguments:
- image: bfloat16 [128, 2048, 128], P('rows', 'cols'), may hold values from -40 to 40
- cotangent: bfloat16 [128, 2048, 128], P('rows', 'cols'), may hold values from -6 to 6
- norm1_gain: float32 [128], replicated, may hold values from 0.1 to 1.9
- w_expand: float32 [128, 512], replicated, may hold values from -0.5 to 0.5
- dw_kernel: float32 [9, 512], replicated, may hold values from -2 to 2
- w_project: float32 [512, 128], replicated, may hold values from -0.25 to 0.25
- norm2_gain: float32 [128], replicated, may hold values from 0.1 to 1.9
- w_qkv: float32 [128, 384], replicated, may hold values from -0.5 to 0.5
- w_out: float32 [128, 128], replicated, may hold values from -0.5 to 0.5
- bias_table: float32 [4, 225], replicated, may hold values from -80 to 160
Outputs:
- block_out: bfloat16 [128, 2048, 128], P('rows', 'cols')
- grad_image: bfloat16 [128, 2048, 128], P('rows', 'cols')
- grad_gain1: float32 [128], replicated
- grad_expand: float32 [128, 512], replicated
- grad_kernel: float32 [9, 512], replicated
- grad_project: float32 [512, 128], replicated
- grad_gain2: float32 [128], replicated
- grad_qkv: float32 [128, 384], replicated
- grad_out: float32 [128, 128], replicated
- grad_bias: float32 [4, 225], replicated
All inputs are finite; a program needn't handle non-finite values.
Results may differ from a plain program's by a relative error of at most 0.019.
Values may be sent and summed in bfloat16 or wider, within the bound.
No kernel may reach another device: no remote copies, remote signals or barrier semaphores. Data moves between devices by JAX's collectives and lax.ppermute only.
A program may use at most 128 MiB of HBM per device.

v0:
```python
import math

import jax
import jax.numpy as jnp
from jax import lax
from jax.sharding import PartitionSpec as P

GRID = 8


epsilon = 1e-06
gelu_coef = math.sqrt(2.0 / math.pi)


def extended(block, sides, width):
    for axis, dim in sides:
        count = lax.axis_size(axis)
        forward = [(i, i + 1) for i in range(count - 1)]
        backward = [(target, source) for source, target in forward]
        low = lax.ppermute(
            lax.slice_in_dim(block, block.shape[dim] - width, None, axis=dim), axis, forward
        )
        high = lax.ppermute(lax.slice_in_dim(block, 0, width, axis=dim), axis, backward)
        block = jnp.concatenate([low, block, high], axis=dim)
    return block


def gelu_value(values):
    inner = gelu_coef * (values + 0.044715 * values * values * values)
    return 0.5 * values * (1.0 + jnp.tanh(inner))


def gelu_slope(values):
    tangent = jnp.tanh(gelu_coef * (values + 0.044715 * values * values * values))
    return 0.5 * (1.0 + tangent) + 0.5 * values * (1.0 - tangent * tangent) * gelu_coef * (
        1.0 + 0.134145 * values * values
    )


def expand_part(tokens, gain_vec, weight):
    values = tokens.astype(jnp.float32)
    inverse = lax.rsqrt(jnp.mean(values * values, axis=-1, keepdims=True) + epsilon)
    unit_form = values * inverse
    normed = (unit_form * gain_vec).astype(jnp.bfloat16)
    flat_rows = normed.reshape(-1, normed.shape[-1])
    before = jnp.dot(flat_rows, weight, preferred_element_type=jnp.float32)
    before = before.reshape(normed.shape[:-1] + (weight.shape[1],))
    return (inverse, unit_form, normed, before, gelu_value(before).astype(jnp.bfloat16))


def depthwise(padded, kernel, height, breadth):
    running = jnp.zeros((height, breadth, kernel.shape[1]), jnp.float32)
    for offset in range(9):
        window = padded[offset // 3 : offset // 3 + height, offset % 3 : offset % 3 + breadth]
        running = running + kernel[offset] * window.astype(jnp.float32)
    return running


def offsets_onehot():
    member_count = GRID * GRID
    span_size = 2 * GRID - 1
    pair_index = jnp.arange(member_count * member_count, dtype=jnp.int32)
    first_pos = pair_index // member_count
    second_pos = pair_index % member_count
    table_index = (first_pos // GRID - second_pos // GRID + GRID - 1) * span_size + (
        first_pos % GRID - second_pos % GRID + GRID - 1
    )
    return (
        table_index[:, None] == jnp.arange(span_size * span_size, dtype=jnp.int32)[None, :]
    ).astype(jnp.float32)


def grid_sizes(rows_tile, cols_tile):
    row_devs = lax.axis_size("rows")
    col_devs = lax.axis_size("cols")
    per_dev = GRID // row_devs
    block_rows = rows_tile // per_dev
    row_piece = block_rows // row_devs
    col_piece = cols_tile // col_devs
    col_group = col_devs // GRID
    return (row_devs, col_devs, per_dev, block_rows, row_piece, col_piece, col_group)


def window_layout(tokens):
    rows_tile, cols_tile, channels = tokens.shape
    row_devs, col_devs, per_dev, block_rows, row_piece, col_piece, col_group = grid_sizes(
        rows_tile, cols_tile
    )
    arrived = lax.all_to_all(
        lax.all_to_all(
            tokens.reshape(per_dev, block_rows, cols_tile, channels),
            "rows",
            split_axis=1,
            concat_axis=0,
            tiled=True,
        ),
        "cols",
        split_axis=2,
        concat_axis=0,
        tiled=True,
    )
    arrived = arrived.reshape(GRID, col_group, GRID, row_piece, col_piece, channels)
    arrived = arrived.transpose(1, 3, 4, 2, 0, 5)
    return arrived.reshape(-1, GRID * GRID, channels)


def token_layout(windows, rows_tile, cols_tile):
    channels = windows.shape[-1]
    row_devs, col_devs, per_dev, block_rows, row_piece, col_piece, col_group = grid_sizes(
        rows_tile, cols_tile
    )
    arranged = windows.reshape(col_group, row_piece, col_piece, GRID, GRID, channels).transpose(
        3, 1, 4, 0, 2, 5
    )
    arranged = arranged.reshape(GRID, row_piece, col_devs, col_piece, channels)
    arrived = lax.all_to_all(
        lax.all_to_all(arranged, "rows", split_axis=0, concat_axis=1, tiled=True),
        "cols",
        split_axis=2,
        concat_axis=3,
        tiled=True,
    )
    return arrived.reshape(rows_tile, cols_tile, channels)


def attend_forward(windows, weight, bias_full, head_count):
    window_count, member_count, channels = windows.shape
    head_size = channels // head_count
    mixture = jnp.dot(windows.reshape(-1, channels), weight, preferred_element_type=jnp.float32)
    mixture = mixture.reshape(window_count, member_count, 3, head_count, head_size)
    queries = (mixture[:, :, 0] * head_size ** (-0.5)).astype(jnp.bfloat16)
    key_vecs = mixture[:, :, 1].astype(jnp.bfloat16)
    value_vecs = mixture[:, :, 2].astype(jnp.bfloat16)
    scores = (
        jnp.einsum("wihd,wjhd->whij", queries, key_vecs, preferred_element_type=jnp.float32)
        + bias_full[None]
    )
    row_max = jnp.max(scores, axis=-1, keepdims=True)
    weights = jnp.exp(scores - row_max)
    probability = weights / jnp.sum(weights, axis=-1, keepdims=True)
    rounded = probability.astype(jnp.bfloat16)
    attended = jnp.einsum(
        "whij,wjhd->wihd", rounded, value_vecs, preferred_element_type=jnp.float32
    )
    attended = attended.astype(jnp.bfloat16).reshape(window_count, member_count, channels)
    return (attended, queries, key_vecs, value_vecs, probability, rounded)


def attend_backward(
    windows, grad_attended, weight, queries, key_vecs, value_vecs, probability, rounded, head_count
):
    window_count, member_count, channels = windows.shape
    head_size = channels // head_count
    grad_heads = grad_attended.reshape(window_count, member_count, head_count, head_size)
    grad_probs = jnp.einsum(
        "wihd,wjhd->whij", grad_heads, value_vecs, preferred_element_type=jnp.float32
    )
    grad_values = jnp.einsum(
        "whij,wihd->wjhd", rounded, grad_heads, preferred_element_type=jnp.float32
    )
    grad_scores = probability * (
        grad_probs - jnp.sum(probability * grad_probs, axis=-1, keepdims=True)
    )
    grad_round = grad_scores.astype(jnp.bfloat16)
    grad_queries = jnp.einsum(
        "whij,wjhd->wihd", grad_round, key_vecs, preferred_element_type=jnp.float32
    )
    grad_keys = jnp.einsum(
        "whij,wihd->wjhd", grad_round, queries, preferred_element_type=jnp.float32
    )
    grad_mixture = jnp.stack([grad_queries * head_size ** (-0.5), grad_keys, grad_values], axis=2)
    grad_mixture = grad_mixture.astype(jnp.bfloat16).reshape(-1, 3 * channels)
    grad_weight = jnp.dot(
        windows.reshape(-1, channels).T, grad_mixture, preferred_element_type=jnp.float32
    )
    grad_windows = jnp.dot(grad_mixture, weight.T, preferred_element_type=jnp.float32)
    grad_windows = grad_windows.astype(jnp.bfloat16).reshape(window_count, member_count, channels)
    return (grad_windows, grad_weight, jnp.sum(grad_scores, axis=0))


def per_device(
    image,
    cotangent,
    norm1_gain,
    w_expand,
    dw_kernel,
    w_project,
    norm2_gain,
    w_qkv,
    w_out,
    bias_table,
):
    rows_tile, cols_tile, channels = image.shape
    hidden_width = w_expand.shape[1]
    head_count = bias_table.shape[0]
    expand_half = w_expand.astype(jnp.bfloat16)
    project_half = w_project.astype(jnp.bfloat16)
    mixing_half = w_qkv.astype(jnp.bfloat16)
    output_half = w_out.astype(jnp.bfloat16)
    factor = 1.0 / math.sqrt(rows_tile * cols_tile * lax.axis_size("rows") * lax.axis_size("cols"))
    onehot = offsets_onehot()
    bias_full = jnp.dot(bias_table, onehot.T, precision=lax.Precision.HIGHEST).reshape(
        head_count, GRID * GRID, GRID * GRID
    )
    inverse_one, unit_one, normed_one, before_one, expanded = expand_part(
        image, norm1_gain, expand_half
    )
    expand_rim = extended(expanded, (("rows", 0), ("cols", 1)), 1)
    depth_before = depthwise(expand_rim, dw_kernel, rows_tile, cols_tile)
    depthed = gelu_value(depth_before).astype(jnp.bfloat16)
    projected = jnp.dot(
        depthed.reshape(-1, hidden_width), project_half, preferred_element_type=jnp.float32
    )
    middle = (image.astype(jnp.float32) + projected.reshape(rows_tile, cols_tile, channels)).astype(
        jnp.bfloat16
    )
    middle_values = middle.astype(jnp.float32)
    inverse_two = lax.rsqrt(
        jnp.mean(middle_values * middle_values, axis=-1, keepdims=True) + epsilon
    )
    unit_two = middle_values * inverse_two
    normed_two = (unit_two * norm2_gain).astype(jnp.bfloat16)
    windows_two = window_layout(normed_two)
    attended_win, queries, key_vecs, value_vecs, probability, rounded = attend_forward(
        windows_two, mixing_half, bias_full, head_count
    )
    attended = token_layout(attended_win, rows_tile, cols_tile)
    flat_attended = attended.reshape(-1, channels)
    flat_cot = cotangent.reshape(-1, channels)
    mixed_out = jnp.dot(flat_attended, output_half, preferred_element_type=jnp.float32).reshape(
        rows_tile, cols_tile, channels
    )
    block_out = (middle_values + mixed_out).astype(jnp.bfloat16)
    grad_out = jnp.dot(flat_attended.T, flat_cot, preferred_element_type=jnp.float32)
    grad_attended = jnp.dot(flat_cot, output_half.T, preferred_element_type=jnp.float32).astype(
        jnp.bfloat16
    )
    grad_attended = grad_attended.reshape(rows_tile, cols_tile, channels)
    grad_windows, grad_qkv, score_sums = attend_backward(
        windows_two,
        window_layout(grad_attended),
        mixing_half,
        queries,
        key_vecs,
        value_vecs,
        probability,
        rounded,
        head_count,
    )
    grad_bias = jnp.dot(score_sums.reshape(head_count, -1), onehot, precision=lax.Precision.HIGHEST)
    grad_normed_two = token_layout(grad_windows, rows_tile, cols_tile).astype(jnp.float32)
    grad_gain_two = jnp.sum(grad_normed_two * unit_two, axis=(0, 1))
    scaled_two = grad_normed_two * norm2_gain
    grad_middle = cotangent.astype(jnp.float32) + inverse_two * (
        scaled_two - unit_two * jnp.mean(scaled_two * unit_two, axis=-1, keepdims=True)
    )
    grad_middle = grad_middle.astype(jnp.bfloat16)
    grad_depthed = jnp.dot(
        grad_middle.reshape(-1, channels), project_half.T, preferred_element_type=jnp.float32
    )
    grad_depthed = grad_depthed.reshape(rows_tile, cols_tile, hidden_width)
    grad_before = (grad_depthed * gelu_slope(depth_before)).astype(jnp.bfloat16)
    grad_project = jnp.dot(
        depthed.reshape(-1, hidden_width).T,
        grad_middle.reshape(-1, channels),
        preferred_element_type=jnp.float32,
    )
    own_grad = grad_before.astype(jnp.float32)
    grad_kernel = jnp.stack(
        [
            jnp.sum(
                expand_rim[
                    offset // 3 : offset // 3 + rows_tile, offset % 3 : offset % 3 + cols_tile
                ].astype(jnp.float32)
                * own_grad,
                axis=(0, 1),
            )
            for offset in range(9)
        ]
    )
    grad_rim = extended(grad_before, (("rows", 0), ("cols", 1)), 1)
    grad_expanded = depthwise(grad_rim, dw_kernel[::-1], rows_tile, cols_tile)
    grad_expand_before = (grad_expanded * gelu_slope(before_one)).astype(jnp.bfloat16)
    grad_expand = jnp.dot(
        normed_one.reshape(-1, channels).T,
        grad_expand_before.reshape(-1, hidden_width),
        preferred_element_type=jnp.float32,
    )
    grad_normed_one = jnp.dot(
        grad_expand_before.reshape(-1, hidden_width),
        expand_half.T,
        preferred_element_type=jnp.float32,
    )
    grad_normed_one = grad_normed_one.reshape(rows_tile, cols_tile, channels)
    scaled_one = grad_normed_one * norm1_gain
    grad_gain_one = jnp.sum(grad_normed_one * unit_one, axis=(0, 1))
    grad_image = grad_middle.astype(jnp.float32) + inverse_one * (
        scaled_one - unit_one * jnp.mean(scaled_one * unit_one, axis=-1, keepdims=True)
    )
    grad_image = grad_image.astype(jnp.bfloat16)
    (
        grad_gain_one,
        grad_expand,
        grad_kernel,
        grad_project,
        grad_gain_two,
        grad_qkv,
        grad_out,
        grad_bias,
    ) = lax.psum(
        (
            grad_gain_one,
            grad_expand,
            grad_kernel,
            grad_project,
            grad_gain_two,
            grad_qkv,
            grad_out,
            grad_bias,
        ),
        ("rows", "cols"),
    )
    return (
        block_out,
        grad_image,
        grad_gain_one * factor,
        grad_expand * factor,
        grad_kernel * factor,
        grad_project * factor,
        grad_gain_two * factor,
        grad_qkv * factor,
        grad_out * factor,
        grad_bias * factor,
    )


def solution(mesh):
    return jax.shard_map(
        per_device,
        mesh=mesh,
        in_specs=(
            P("rows", "cols", None),
            P("rows", "cols", None),
            P(),
            P(),
            P(),
            P(),
            P(),
            P(),
            P(),
            P(),
        ),
        out_specs=(
            P("rows", "cols", None),
            P("rows", "cols", None),
            P(),
            P(),
            P(),
            P(),
            P(),
            P(),
            P(),
            P(),
        ),
        check_vma=False,
    )
```

profile of v0, /device:TPU:1, one launch (start us, length us, event | category | flops | bytes accessed | tf_op | source)
XLA Modules:
  0.0 474.7 jit_solution(16436239626289094855)
XLA Ops:
  7.2 1.4 fusion.65
  8.6 4.7 multiply_convert_fusion.1
  13.3 4.5 collective-permute-start
  17.9 1.9 collective-permute-start.1
  20.9 4.1 all-to-all-start.4
  25.2 3.5 collective-permute-start.2
  28.8 1.3 collective-permute-start.3
  30.5 4.2 collective-permute-done.3
  34.6 3.2 maximum_maximum_fusion
  37.9 7.6 %multiply_convert_fusion = (bf16[32,64,512]{2,1,0:T(8,128)(2,1)S(1)}, f32[32,64,512]{2,1,0:T(8,128)}) fusion(bf16[34,65,512]{2,1,0:T(8,128)(2,1)S(1)} %get-tuple-element.46, f32[512]{0:T(512)S(1)} %bitcast.193, bf16[1,64,512]{2,1,0:T(8,128)(2,1)S(1)} %collective-permute-done.1, bf16[32,64,512]{2,1,0:T(8,128)(2,1)S(1)} %copy-done.5, f32[512]{0:T(512)S(1)} %bitcast.195, ...), kind=kLoop, calls=%fused_computation.67 | loop fusion | flops 38797312 | bytes 21121024 | tf_op jit(solution)/shard_map/convert_element_type | solution.py:210
  45.5 1.4 copy-done.11
  48.9 4.5 all-to-all-start
  55.7 5.4 %all-to-all-done = bf16[2,16,64,128]{3,2,0,1:T(8,128)(2,1)} async-done(((bf16[2,16,64,128]{3,2,0,1:T(8,128)(2,1)}), bf16[2,16,64,128]{3,2,0,1:T(8,128)(2,1)}, u32[]{:S(2)}, u32[]{:S(2)}) %all-to-all-start) | async-done | bytes 524320 | tf_op jit(solution)/shard_map/all_to_all | solution.py:90
  61.1 12.4 %all-to-all-start.5 = ((bf16[8,4,64,128]{3,1,0,2:T(4,128)(2,1)}), bf16[8,4,64,128]{3,1,0,2:T(4,128)(2,1)}, u32[]{:S(2)}, u32[]{:S(2)}) async-start(bf16[8,4,64,128]{3,1,0,2:T(4,128)(2,1)} %copy.227), calls=%async_computation.5 | async-start | bytes 1048576 | tf_op jit(solution)/shard_map/all_to_all | solution.py:89
  75.8 8.4 %all-to-all-done.5 = bf16[8,4,64,128]{3,1,0,2:T(4,128)(2,1)} async-done(((bf16[8,4,64,128]{3,1,0,2:T(4,128)(2,1)}), bf16[8,4,64,128]{3,1,0,2:T(4,128)(2,1)}, u32[]{:S(2)}, u32[]{:S(2)}) %all-to-all-start.5) | async-done | bytes 524320 | tf_op jit(solution)/shard_map/all_to_all | solution.py:89
  84.2 4.9 %all-to-all-start.1 = ((bf16[8,4,64,128]{3,1,0,2:T(4,128)(2,1)}), bf16[8,4,64,128]{3,1,0,2:T(4,128)(2,1)}, u32[]{:S(2)}, u32[]{:S(2)}) async-start(bf16[8,4,64,128]{3,1,0,2:T(4,128)(2,1)} %copy.210), calls=%async_computation.1 | async-start | bytes 1048576 | tf_op jit(solution)/shard_map/all_to_all | solution.py:89
  89.3 2.2 convolution_bitcast_fusion
  92.8 1.4 copy.230
  94.3 4.0 reshape_reshape.21
  98.2 3.9 copy.231
  105.8 1.8 fusion.130
  108.8 1.5 fusion.53
  114.2 3.7 copy.236
  117.9 5.6 %convert_element_type.204 = bf16[2048,384]{0,1:T(8,128)(2,1)} reshape(bf16[32,64,3,4,32]{1,0,4,3,2:T(8,128)(2,1)} %copy.236) | data formatting | bytes 3145728 | tf_op jit(solution)/shard_map/convert_element_type | solution.py:172
  123.5 2.0 convolution_convert_fusion
  125.6 1.3 copy.238
  127.0 7.6 %all-to-all-start.6 = ((bf16[8,4,32,2,128]{4,3,2,1,0:T(2,128)(2,1)}), bf16[8,4,32,2,128]{4,3,2,1,0:T(2,128)(2,1)}, u32[]{:S(2)}, u32[]{:S(2)}) async-start(bf16[8,4,32,2,128]{4,3,2,1,0:T(2,128)(2,1)} %copy.238), calls=%async_computation.6 | async-start | bytes 1048576 | tf_op jit(solution)/shard_map/all_to_all | solution.py:117
  134.6 4.2 fusion.55
  138.8 4.1 copy.217
  142.9 3.8 reshape_reshape.19
  147.9 1.3 copy.219
  149.2 4.2 all-to-all-start.2
  154.8 1.3 copy.241
  156.1 5.3 %all-to-all-done.2 = bf16[8,4,32,2,128]{4,3,2,1,0:T(2,128)(2,1)} async-done(((bf16[8,4,32,2,128]{4,3,2,1,0:T(2,128)(2,1)}), bf16[8,4,32,2,128]{4,3,2,1,0:T(2,128)(2,1)}, u32[]{:S(2)}, u32[]{:S(2)}) %all-to-all-start.2) | async-done | bytes 524320 | tf_op jit(solution)/shard_map/all_to_all | solution.py:117
  161.5 9.8 %all-to-all-start.7 = ((bf16[2,16,32,2,128]{4,3,1,0,2:T(2,128)(2,1)}), bf16[2,16,32,2,128]{4,3,1,0,2:T(2,128)(2,1)}, u32[]{:S(2)}, u32[]{:S(2)}) async-start(bf16[2,16,32,2,128]{4,3,1,0,2:T(2,128)(2,1)} %copy.241), calls=%async_computation.7 | async-start | bytes 1048576 | tf_op jit(solution)/shard_map/all_to_all | solution.py:116
  171.3 2.0 fusion.37
  173.3 2.9 fusion.131
  177.3 1.3 copy.222
  178.7 3.6 all-to-all-done.7
  182.3 5.6 %all-to-all-start.3 = ((bf16[2,16,32,2,128]{4,3,1,0,2:T(2,128)(2,1)}), bf16[2,16,32,2,128]{4,3,1,0,2:T(2,128)(2,1)}, u32[]{:S(2)}, u32[]{:S(2)}) async-start(bf16[2,16,32,2,128]{4,3,1,0,2:T(2,128)(2,1)} %copy.222), calls=%async_computation.3 | async-start | bytes 1048576 | tf_op jit(solution)/shard_map/all_to_all | solution.py:116
  188.1 1.8 copy_convert_fusion
  191.8 2.4 fusion.71
  194.3 11.7 %fusion.36 = (f32[512]{0:T(512)S(1)}, f32[512]{0:T(512)S(1)}, f32[512]{0:T(512)S(1)}, f32[512]{0:T(512)S(1)}, f32[512]{0:T(512)}, /*index=5*/f32[512]{0:T(512)},...) fusion(bf16[34,65,512]{2,1,0:T(8,128)(2,1)S(1)} %copy-done.3, ...), kind=kOutput, calls=%fused_computation.61 | convolution fusion | flops 319876608 | bytes 21907456 | tf_op jit(solution)/shard_map/dot_general | solution.py:258
  206.0 1.4 copy-done.7
  207.4 3.5 collective-permute-start.4
  211.0 2.1 collective-permute-start.5
  213.1 1.4 convolution_bitcast_fusion.3
  214.6 1.6 copy.223
  217.4 3.2 collective-permute-start.6
  220.6 1.3 collective-permute-start.7
  222.0 2.0 fusion.132
  224.1 2.4 collective-permute-done.7
  226.4 3.2 maximum_maximum_fusion.1
  229.8 9.4 %fusion.22 = bf16[32,64,512]{2,1,0:T(8,128)(2,1)S(1)} fusion(f32[32,64,512]{2,1,0:T(8,128)S(1)} %copy-done.18, bf16[32,64,512]{2,1,0:T(8,128)(2,1)} %copy-done.7, bf16[34,65,512]{2,1,0:T(8,128)(2,1)S(1)} %get-tuple-element.42, bf16[1,64,512]{2,1,0:T(8,128)(2,1)S(1)} %collective-permute-done.5, bf16[34,65,512]{2,1,0:T(8,128)(2,1)S(1)} %get-tuple-element.41, ...), kind=kLoop, calls=%fused_computation.47 | loop fusion | flops 49283072 | bytes 21121024 | tf_op jit(solution)/shard_map/convert_element_type | solution.py:283
  239.2 1.3 copy-done.13
  240.6 1.7 convolution_bitcast_fusion.4
  242.3 2.4 fusion.64
  244.8 70.7 %all-reduce = (f32[128]{0:T(128)S(1)}, f32[9,512]{1,0:T(8,128)S(1)}, f32[128]{0:T(128)S(1)}, f32[4,225]{1,0:T(4,128)S(1)}) all-reduce(f32[128]{0:T(128)S(1)} %get-tuple-element.27, f32[9,512]{1,0:T(8,128)S(1)} %stack.55, f32[128]{0:T(128)S(1)} %copy-done.48, ...), channel_id=1, replica_groups=mesh['rows'=4,'cols'=32] {'rows','cols'}, use_global_device_ids=true, to_apply=%region_8.9 | all-reduce | flops 5764 | bytes 46112 | tf_op jit(solution)/shard_map/psum | solution.py:310
  317.3 1.4 fusion.63
  318.7 142.6 %all-reduce.4.cloned.1.call-done = (f32[128,512]{1,0:T(8,128)}, f32[512,128]{1,0:T(8,128)}, f32[128,384]{1,0:T(8,128)}, f32[128,128]{1,0:T(8,128)}) async-done(((f32[128,512]{1,0:T(8,128)}, f32[512,128]{1,0:T(8,128)}, f32[128,384]{1,0:T(8,128)}, f32[128,128]{1,0:T(8,128)}), (f32[128,512]{1,0:T(8,128)}, f32[512,128]{1,0:T(8,128)}, f32[128,384]{1,0:T(8,128)}, ...) | async-done | bytes 786448 | tf_op jit(solution)/shard_map/psum | solution.py:310
  461.2 1.7 broadcast_multiply_fusion
  462.9 1.7 broadcast_multiply_fusion.1
  464.6 1.6 broadcast_multiply_fusion.2
  466.2 1.5 broadcast_multiply_fusion.3
  (166 shorter events, 27.3 us)
Async XLA Ops:
  7.2 82.1 %copy-start = (f32[4,225]{1,0:T(4,128)S(1)}, f32[4,225]{1,0:T(4,128)}, u32[]{:S(2)}) copy-start(f32[4,225]{1,0:T(4,128)} %param.19) | copy-start | bytes 10804
  8.6 4.7 copy-start.27
  8.6 11.2 %copy-start.17 = (bf16[32,64,128]{2,1,0:T(8,128)(2,1)S(1)}, bf16[32,64,128]{2,1,0:T(8,128)(2,1)}, u32[]{:S(2)}) copy-start(bf16[32,64,128]{2,1,0:T(8,128)(2,1)} %param.11) | copy-start | bytes 1572868
  8.6 11.2 %copy-start.22 = (f32[128,128]{1,0:T(8,128)S(1)}, f32[128,128]{1,0:T(8,128)}, u32[]{:S(2)}) copy-start(f32[128,128]{1,0:T(8,128)} %param.18) | copy-start | bytes 196612
  13.3 17.1 %copy-start.4 = (bf16[32,64,512]{2,1,0:T(8,128)(2,1)}, bf16[32,64,512]{2,1,0:T(8,128)(2,1)S(1)}, u32[]{:S(2)}) copy-start(bf16[32,64,512]{2,1,0:T(8,128)(2,1)S(1)} %get-tuple-element.62) | copy-start | bytes 6291460
  13.3 16.8 %copy-start.43 = (f32[9,512]{1,0:T(8,128)S(1)}, f32[9,512]{1,0:T(8,128)}, u32[]{:S(2)}) copy-start(f32[9,512]{1,0:T(8,128)} %param.14) | copy-start | bytes 55300
  13.3 11.8 %collective-permute-start = (bf16[1,64,512]{2,1,0:T(8,128)(2,1)S(1)}, bf16[1,64,512]{2,1,0:T(8,128)(2,1)S(1)}, u32[]{:S(2)}, u32[]{:S(2)}) collective-permute-start(bf16[1,64,512]{2,1,0:T(8,128)(2,1)S(1)} %get-tuple-element.51), channel_id=1, source_target_pairs={{0,32},{32,64},{64,96},{1,33},{33,65},{65,97},{2,34},{34,66},{66,9... | collective-permute-start | bytes 196616 | tf_op jit(solution)/shard_map/ppermute | solution.py:20
  17.9 7.3 %collective-permute-start.1 = (bf16[1,64,512]{2,1,0:T(8,128)(2,1)S(1)}, bf16[1,64,512]{2,1,0:T(8,128)(2,1)S(1)}, u32[]{:S(2)}, u32[]{:S(2)}) collective-permute-start(bf16[1,64,512]{2,1,0:T(8,128)(2,1)S(1)} %get-tuple-element.52), channel_id=1, source_target_pairs={{32,0},{64,32},{96,64},{33,1},{65,33},{97,65},{34,2},{66,34},{98,6... | collective-permute-start | bytes 196616 | tf_op jit(solution)/shard_map/ppermute | solution.py:23
  20.9 28.0 %all-to-all-start.4 = ((bf16[2,16,64,128]{3,2,0,1:T(8,128)(2,1)}), bf16[2,16,64,128]{3,2,0,1:T(8,128)(2,1)}, u32[]{:S(2)}, u32[]{:S(2)}) async-start(bf16[2,16,64,128]{3,2,0,1:T(8,128)(2,1)} %copy.224), calls=%async_computation.4 | async-start | bytes 1048576 | tf_op jit(solution)/shard_map/all_to_all | solution.py:90
  25.2 5.2 %collective-permute-start.2 = (bf16[34,1,512]{2,1,0:T(2,128)(2,1)S(1)}, bf16[34,1,512]{2,1,0:T(2,128)(2,1)S(1)}, u32[]{:S(2)}, u32[]{:S(2)}) collective-permute-start(bf16[34,1,512]{2,1,0:T(2,128)(2,1)S(1)} %get-tuple-element.47), channel_id=1, source_target_pairs={{0,1},{1,2},{2,3},{3,4},{4,5},{5,6},{6,7},{7,8},{8,9},{9,10},{10,1... | collective-permute-start | bytes 104456 | tf_op jit(solution)/shard_map/ppermute | solution.py:20
  28.8 5.8 %collective-permute-start.3 = (bf16[34,1,512]{2,1,0:T(2,128)(2,1)S(1)}, bf16[34,1,512]{2,1,0:T(2,128)(2,1)S(1)}, u32[]{:S(2)}, u32[]{:S(2)}) collective-permute-start(bf16[34,1,512]{2,1,0:T(2,128)(2,1)S(1)} %get-tuple-element.48), channel_id=1, source_target_pairs={{1,0},{2,1},{3,2},{4,3},{5,4},{6,5},{7,6},{8,7},{9,8},{10,9},{11,1... | collective-permute-start | bytes 104456 | tf_op jit(solution)/shard_map/ppermute | solution.py:23
  30.1 15.4 %copy-start.29 = (f32[1,512]{1,0:T(1,128)}, f32[1,512]{1,0:T(1,128)S(1)}, u32[]{:S(2)}) copy-start(f32[1,512]{1,0:T(1,128)S(1)} %get-tuple-element.56) | copy-start | bytes 6148
  30.1 15.4 %copy-start.31 = (f32[1,512]{1,0:T(1,128)}, f32[1,512]{1,0:T(1,128)S(1)}, u32[]{:S(2)}) copy-start(f32[1,512]{1,0:T(1,128)S(1)} %get-tuple-element.57) | copy-start | bytes 6148
  30.1 15.3 %copy-start.33 = (f32[1,512]{1,0:T(1,128)}, f32[1,512]{1,0:T(1,128)S(1)}, u32[]{:S(2)}) copy-start(f32[1,512]{1,0:T(1,128)S(1)} %get-tuple-element.58) | copy-start | bytes 6148
  30.2 15.3 %copy-start.35 = (f32[1,512]{1,0:T(1,128)}, f32[1,512]{1,0:T(1,128)S(1)}, u32[]{:S(2)}) copy-start(f32[1,512]{1,0:T(1,128)S(1)} %get-tuple-element.59) | copy-start | bytes 6148
  30.2 15.3 %copy-start.37 = (f32[1,512]{1,0:T(1,128)}, f32[1,512]{1,0:T(1,128)S(1)}, u32[]{:S(2)}) copy-start(f32[1,512]{1,0:T(1,128)S(1)} %get-tuple-element.60) | copy-start | bytes 6148
  30.2 15.3 %copy-start.39 = (f32[1,512]{1,0:T(1,128)}, f32[1,512]{1,0:T(1,128)S(1)}, u32[]{:S(2)}) copy-start(f32[1,512]{1,0:T(1,128)S(1)} %get-tuple-element.61) | copy-start | bytes 6148
  37.8 7.7 %copy-start.2 = (bf16[34,65,512]{2,1,0:T(8,128)(2,1)}, bf16[34,65,512]{2,1,0:T(8,128)(2,1)S(1)}, u32[]{:S(2)}) copy-start(bf16[34,65,512]{2,1,0:T(8,128)(2,1)S(1)} %get-tuple-element.46) | copy-start | bytes 6789124
  37.8 9.1 %copy-start.14 = (bf16[32,64,128]{2,1,0:T(8,128)(2,1)S(1)}, bf16[32,64,128]{2,1,0:T(8,128)(2,1)}, u32[]{:S(2)}) copy-start(bf16[32,64,128]{2,1,0:T(8,128)(2,1)} %param.10) | copy-start | bytes 1572868
  37.9 9.1 %copy-start.24 = (f32[512,128]{1,0:T(8,128)S(1)}, f32[512,128]{1,0:T(8,128)}, u32[]{:S(2)}) copy-start(f32[512,128]{1,0:T(8,128)} %param.15) | copy-start | bytes 786436
  37.9 9.9 %copy-start.44 = (f32[128]{0:T(128)S(1)}, f32[128]{0:T(128)}, u32[]{:S(2)}) copy-start(f32[128]{0:T(128)} %param.16) | copy-start | bytes 1540
  48.1 41.0 %copy-start.26 = (f32[128,384]{1,0:T(8,128)S(1)}, f32[128,384]{1,0:T(8,128)}, u32[]{:S(2)}) copy-start(f32[128,384]{1,0:T(8,128)} %param.17) | copy-start | bytes 589828
  48.9 12.2 %all-to-all-start = ((bf16[2,16,64,128]{3,2,0,1:T(8,128)(2,1)}), bf16[2,16,64,128]{3,2,0,1:T(8,128)(2,1)}, u32[]{:S(2)}, u32[]{:S(2)}) async-start(bf16[2,16,64,128]{3,2,0,1:T(8,128)(2,1)} %copy.207), calls=%async_computation | async-start | bytes 1048576 | tf_op jit(solution)/shard_map/all_to_all | solution.py:90
  61.1 23.1 %all-to-all-start.5 = ((bf16[8,4,64,128]{3,1,0,2:T(4,128)(2,1)}), bf16[8,4,64,128]{3,1,0,2:T(4,128)(2,1)}, u32[]{:S(2)}, u32[]{:S(2)}) async-start(bf16[8,4,64,128]{3,1,0,2:T(4,128)(2,1)} %copy.227), calls=%async_computation.5 | async-start | bytes 1048576 | tf_op jit(solution)/shard_map/all_to_all | solution.py:89
  84.2 18.0 %all-to-all-start.1 = ((bf16[8,4,64,128]{3,1,0,2:T(4,128)(2,1)}), bf16[8,4,64,128]{3,1,0,2:T(4,128)(2,1)}, u32[]{:S(2)}, u32[]{:S(2)}) async-start(bf16[8,4,64,128]{3,1,0,2:T(4,128)(2,1)} %copy.210), calls=%async_computation.1 | async-start | bytes 1048576 | tf_op jit(solution)/shard_map/all_to_all | solution.py:89
  105.0 5.3 %copy-start.10 = (bf16[32,64,3,4,32]{1,4,3,2,0:T(8,128)(2,1)}, bf16[32,64,3,4,32]{1,4,3,2,0:T(8,128)(2,1)S(1)}, u32[]{:S(2)}) copy-start(bf16[32,64,3,4,32]{1,4,3,2,0:T(8,128)(2,1)S(1)} %get-tuple-element.66) | copy-start | bytes 4718596
  107.6 4.6 copy-start.9
  127.0 22.3 %all-to-all-start.6 = ((bf16[8,4,32,2,128]{4,3,2,1,0:T(2,128)(2,1)}), bf16[8,4,32,2,128]{4,3,2,1,0:T(2,128)(2,1)}, u32[]{:S(2)}, u32[]{:S(2)}) async-start(bf16[8,4,32,2,128]{4,3,2,1,0:T(2,128)(2,1)} %copy.238), calls=%async_computation.6 | async-start | bytes 1048576 | tf_op jit(solution)/shard_map/all_to_all | solution.py:117
  146.7 24.5 %copy-start.42 = (s32[4096]{0:T(1024)S(1)}, s32[4096]{0:T(1024)}, u32[]{:S(2)}) copy-start(s32[4096]{0:T(1024)} %copy-done.41) | copy-start | bytes 49156
  149.2 12.2 %all-to-all-start.2 = ((bf16[8,4,32,2,128]{4,3,2,1,0:T(2,128)(2,1)}), bf16[8,4,32,2,128]{4,3,2,1,0:T(2,128)(2,1)}, u32[]{:S(2)}, u32[]{:S(2)}) async-start(bf16[8,4,32,2,128]{4,3,2,1,0:T(2,128)(2,1)} %copy.219), calls=%async_computation.2 | async-start | bytes 1048576 | tf_op jit(solution)/shard_map/all_to_all | solution.py:117
  161.5 20.8 %all-to-all-start.7 = ((bf16[2,16,32,2,128]{4,3,1,0,2:T(2,128)(2,1)}), bf16[2,16,32,2,128]{4,3,1,0,2:T(2,128)(2,1)}, u32[]{:S(2)}, u32[]{:S(2)}) async-start(bf16[2,16,32,2,128]{4,3,1,0,2:T(2,128)(2,1)} %copy.241), calls=%async_computation.7 | async-start | bytes 1048576 | tf_op jit(solution)/shard_map/all_to_all | solution.py:116
  176.1 14.4 %copy-start.45 = (f32[128]{0:T(128)S(1)}, f32[128]{0:T(128)}, u32[]{:S(2)}) copy-start(f32[128]{0:T(128)} %param.16) | copy-start | bytes 1540
  182.3 32.2 %all-to-all-start.3 = ((bf16[2,16,32,2,128]{4,3,1,0,2:T(2,128)(2,1)}), bf16[2,16,32,2,128]{4,3,1,0,2:T(2,128)(2,1)}, u32[]{:S(2)}, u32[]{:S(2)}) async-start(bf16[2,16,32,2,128]{4,3,1,0,2:T(2,128)(2,1)} %copy.222), calls=%async_computation.3 | async-start | bytes 1048576 | tf_op jit(solution)/shard_map/all_to_all | solution.py:116
  188.0 6.2 %copy-start.25 = (f32[512,128]{1,0:T(8,128)S(1)}, f32[512,128]{1,0:T(8,128)}, u32[]{:S(2)}) copy-start(f32[512,128]{1,0:T(8,128)} %param.15) | copy-start | bytes 786436
  188.0 273.2 %all-reduce.4.cloned.1.call-start = ((), (), s32[]{:S(2)}) async-start(), calls=%async_computation.8 | async-start | bytes 1572864 | tf_op jit(solution)/shard_map/psum | solution.py:310
  188.0 6.2 %copy-start.3 = (bf16[34,65,512]{2,1,0:T(8,128)(2,1)S(1)}, bf16[34,65,512]{2,1,0:T(8,128)(2,1)}, u32[]{:S(2)}) copy-start(bf16[34,65,512]{2,1,0:T(8,128)(2,1)} %copy-done.2) | copy-start | bytes 6789124
  188.1 6.2 %copy-start.6 = (bf16[32,64,512]{2,1,0:T(8,128)(2,1)S(1)}, bf16[32,64,512]{2,1,0:T(8,128)(2,1)}, u32[]{:S(2)}) copy-start(bf16[32,64,512]{2,1,0:T(8,128)(2,1)} %copy-done.4) | copy-start | bytes 6291460
  194.2 18.9 %copy-start.19 = (bf16[32,64,128]{2,1,0:T(8,128)(2,1)}, bf16[32,64,128]{2,1,0:T(8,128)(2,1)S(1)}, u32[]{:S(2)}) copy-start(bf16[32,64,128]{2,1,0:T(8,128)(2,1)S(1)} %fusion.71) | copy-start | bytes 1572868
  194.2 18.9 %copy-start.12 = (bf16[32,64,512]{2,1,0:T(8,128)(2,1)S(1)}, bf16[32,64,512]{2,1,0:T(8,128)(2,1)}, u32[]{:S(2)}) copy-start(bf16[32,64,512]{2,1,0:T(8,128)(2,1)} %copy-done.11) | copy-start | bytes 6291460
  206.0 10.2 %copy-start.23 = (f32[128,128]{1,0:T(8,128)S(1)}, f32[128,128]{1,0:T(8,128)}, u32[]{:S(2)}) copy-start(f32[128,128]{1,0:T(8,128)} %param.18) | copy-start | bytes 196612
  207.3 9.9 %copy-start.8 = (bf16[32,64,512]{2,1,0:T(8,128)(2,1)S(1)}, bf16[32,64,512]{2,1,0:T(8,128)(2,1)}, u32[]{:S(2)}) copy-start(bf16[32,64,512]{2,1,0:T(8,128)(2,1)} %copy-done.7) | copy-start | bytes 6291460
  207.4 9.9 %collective-permute-start.4 = (bf16[1,64,512]{2,1,0:T(8,128)(2,1)S(1)}, bf16[1,64,512]{2,1,0:T(8,128)(2,1)S(1)}, u32[]{:S(2)}, u32[]{:S(2)}) collective-permute-start(bf16[1,64,512]{2,1,0:T(8,128)(2,1)S(1)} %get-tuple-element.49), channel_id=1, source_target_pairs={{0,32},{32,64},{64,96},{1,33},{33,65},{65,97},{2,34},{34,66},{66,9... | collective-permute-start | bytes 196616 | tf_op jit(solution)/shard_map/ppermute | solution.py:20
  210.9 13.1 %copy-start.49 = (f32[512]{0:T(512)S(1)}, f32[512]{0:T(512)}, u32[]{:S(2)}) copy-start(f32[512]{0:T(512)} %get-tuple-element.20) | copy-start | bytes 6148
  210.9 13.1 %copy-start.50 = (f32[512]{0:T(512)S(1)}, f32[512]{0:T(512)}, u32[]{:S(2)}) copy-start(f32[512]{0:T(512)} %get-tuple-element.21) | copy-start | bytes 6148
  210.9 13.1 %copy-start.51 = (f32[512]{0:T(512)S(1)}, f32[512]{0:T(512)}, u32[]{:S(2)}) copy-start(f32[512]{0:T(512)} %get-tuple-element.22) | copy-start | bytes 6148
  210.9 13.1 %copy-start.52 = (f32[512]{0:T(512)S(1)}, f32[512]{0:T(512)}, u32[]{:S(2)}) copy-start(f32[512]{0:T(512)} %get-tuple-element.23) | copy-start | bytes 6148
  211.0 13.1 %copy-start.53 = (f32[512]{0:T(512)S(1)}, f32[512]{0:T(512)}, u32[]{:S(2)}) copy-start(f32[512]{0:T(512)} %get-tuple-element.24) | copy-start | bytes 6148
  211.0 6.3 %collective-permute-start.5 = (bf16[1,64,512]{2,1,0:T(8,128)(2,1)S(1)}, bf16[1,64,512]{2,1,0:T(8,128)(2,1)S(1)}, u32[]{:S(2)}, u32[]{:S(2)}) collective-permute-start(bf16[1,64,512]{2,1,0:T(8,128)(2,1)S(1)} %get-tuple-element.50), channel_id=1, source_target_pairs={{32,0},{64,32},{96,64},{33,1},{65,33},{97,65},{34,2},{66,34},{98,6... | collective-permute-start | bytes 196616 | tf_op jit(solution)/shard_map/ppermute | solution.py:23
  217.4 6.7 %collective-permute-start.6 = (bf16[34,1,512]{2,1,0:T(2,128)(2,1)S(1)}, bf16[34,1,512]{2,1,0:T(2,128)(2,1)S(1)}, u32[]{:S(2)}, u32[]{:S(2)}) collective-permute-start(bf16[34,1,512]{2,1,0:T(2,128)(2,1)S(1)} %get-tuple-element.43), channel_id=1, source_target_pairs={{0,1},{1,2},{2,3},{3,4},{4,5},{5,6},{6,7},{7,8},{8,9},{9,10},{10,1... | collective-permute-start | bytes 104456 | tf_op jit(solution)/shard_map/ppermute | solution.py:20
  220.6 5.8 %collective-permute-start.7 = (bf16[34,1,512]{2,1,0:T(2,128)(2,1)S(1)}, bf16[34,1,512]{2,1,0:T(2,128)(2,1)S(1)}, u32[]{:S(2)}, u32[]{:S(2)}) collective-permute-start(bf16[34,1,512]{2,1,0:T(2,128)(2,1)S(1)} %get-tuple-element.44), channel_id=1, source_target_pairs={{1,0},{2,1},{3,2},{4,3},{5,4},{6,5},{7,6},{8,7},{9,8},{10,9},{11,1... | collective-permute-start | bytes 104456 | tf_op jit(solution)/shard_map/ppermute | solution.py:23
  221.9 7.8 %copy-start.30 = (f32[1,512]{1,0:T(1,128)S(1)}, f32[1,512]{1,0:T(1,128)}, u32[]{:S(2)}) copy-start(f32[1,512]{1,0:T(1,128)} %copy-done.29) | copy-start | bytes 6148
  221.9 7.8 %copy-start.32 = (f32[1,512]{1,0:T(1,128)S(1)}, f32[1,512]{1,0:T(1,128)}, u32[]{:S(2)}) copy-start(f32[1,512]{1,0:T(1,128)} %copy-done.31) | copy-start | bytes 6148
  221.9 7.8 %copy-start.34 = (f32[1,512]{1,0:T(1,128)S(1)}, f32[1,512]{1,0:T(1,128)}, u32[]{:S(2)}) copy-start(f32[1,512]{1,0:T(1,128)} %copy-done.33) | copy-start | bytes 6148
  221.9 7.8 %copy-start.36 = (f32[1,512]{1,0:T(1,128)S(1)}, f32[1,512]{1,0:T(1,128)}, u32[]{:S(2)}) copy-start(f32[1,512]{1,0:T(1,128)} %copy-done.35) | copy-start | bytes 6148
  222.0 7.8 %copy-start.38 = (f32[1,512]{1,0:T(1,128)S(1)}, f32[1,512]{1,0:T(1,128)}, u32[]{:S(2)}) copy-start(f32[1,512]{1,0:T(1,128)} %copy-done.37) | copy-start | bytes 6148
  222.0 7.8 %copy-start.40 = (f32[1,512]{1,0:T(1,128)S(1)}, f32[1,512]{1,0:T(1,128)}, u32[]{:S(2)}) copy-start(f32[1,512]{1,0:T(1,128)} %copy-done.39) | copy-start | bytes 6148
  224.1 5.7 %copy-start.18 = (f32[32,64,512]{2,1,0:T(8,128)S(1)}, f32[32,64,512]{2,1,0:T(8,128)}, u32[]{:S(2)}) copy-start(f32[32,64,512]{2,1,0:T(8,128)} %get-tuple-element.63) | copy-start | bytes 12582916
  229.8 10.8 %copy-start.15 = (bf16[32,64,128]{2,1,0:T(8,128)(2,1)S(1)}, bf16[32,64,128]{2,1,0:T(8,128)(2,1)}, u32[]{:S(2)}) copy-start(bf16[32,64,128]{2,1,0:T(8,128)(2,1)} %param.10) | copy-start | bytes 1572868
  229.8 10.8 %copy-start.28 = (f32[32,64]{1,0:T(8,128)S(1)}, f32[32,64]{1,0:T(8,128)}, u32[]{:S(2)}) copy-start(f32[32,64]{1,0:T(8,128)} %copy-done.27) | copy-start | bytes 24580
  229.8 10.8 %copy-start.47 = (f32[128]{0:T(128)S(1)}, f32[128]{0:T(128)}, u32[]{:S(2)}) copy-start(f32[128]{0:T(128)} %param.12) | copy-start | bytes 1540
  229.8 12.5 %copy-start.54 = (f32[128,512]{1,0:T(8,128)S(1)}, f32[128,512]{1,0:T(8,128)}, u32[]{:S(2)}) copy-start(f32[128,512]{1,0:T(8,128)} %param.13) | copy-start | bytes 786436
  240.6 4.2 copy-start.48
  240.6 76.6 %copy-start.20 = (bf16[32,64,128]{2,1,0:T(8,128)(2,1)S(1)}, bf16[32,64,128]{2,1,0:T(8,128)(2,1)}, u32[]{:S(2)}) copy-start(bf16[32,64,128]{2,1,0:T(8,128)(2,1)} %copy-done.19) | copy-start | bytes 1572868
  242.3 225.3 %copy-start.1 = (f32[4,225]{1,0:T(4,128)S(1)}, f32[4,225]{1,0:T(4,128)}, u32[]{:S(2)}) copy-start(f32[4,225]{1,0:T(4,128)} %param.19) | copy-start | bytes 10804
  (8 other events, 16.6 us)
Sparse Core Ops, SparseCore 0:
  316.9 144.3 all-reduce.3
where the time goes:
time: 483 us; the launch traced here: 475 us
  waiting for transfers between devices  172 us (36%)
  starting transfers between devices  74.7 us (15%)
  blocking collectives  70.7 us (15%)
  local copies, waits for them, and re-layouts  51.8 us (11%)
  matrix products  45.5 us (9%)
  other arithmetic  44.6 us (9%)
  between operations  15.3 us (3%)
    psum x1, waiting for transfers between devices, per_device(): lax.psum((grad_gain_one, grad_expand, grad_kernel, grad_project, grad_gai...  143 us
    psum x1, blocking collectives, per_device(): lax.psum((grad_gain_one, grad_expand, grad_kernel, grad_project, grad_gai...  70.7 us
    all_to_all x2, starting transfers between devices, window_layout(): lax.all_to_all(lax.all_to_all(tokens.reshape(per_dev, block_rows, cols_ti...  17.3 us
    all_to_all x2, starting transfers between devices, token_layout(): lax.all_to_all(lax.all_to_all(arranged, 'rows', split_axis=0, concat_axis...  15.4 us
    ppermute x4, starting transfers between devices, extended(): lax.ppermute(lax.slice_in_dim(block, block.shape[dim] - width, None, axis...  14.8 us
    all_to_all x2, starting transfers between devices, token_layout(): lax.all_to_all(arranged, 'rows', split_axis=0, concat_axis=1, tiled=True)  11.8 us
    dot_general x1, matrix products, per_device(): jnp.dot(grad_middle.reshape(-1, channels), project_half.T, preferred_elem...  11.7 us
  transfers between devices with their start and end apart: 17, of which 8 were waited for; matrix products, arithmetic and copies ran while one was open for 17% of the time, Pallas kernels for 0%

commit v1 on v0

v1 whole, which is shorter than its diff:
```python
import math

import jax
import jax.numpy as jnp
import numpy as np
from jax import lax
from jax.experimental import pallas as pl
from jax.experimental.pallas import tpu as pltpu
from jax.sharding import Mesh
from jax.sharding import PartitionSpec as P

GRID = 8
C = 128
E = 512
HEADS = 4
RD = 32
CD = 64
LANES = 128
GROUPS = E // LANES
epsilon = 1e-06
gelu_coef = math.sqrt(2.0 / math.pi)
bf16 = jnp.bfloat16
f32 = jnp.float32
VMEM_LIMIT = 50 * 1024 * 1024

PLANE = ("rows", "group")
COLS = ("group", "plane")
ALL = ("rows", "group", "plane")

ROW_EXPAND = 0
ROW_PROJECT = 512
ROW_QKV = 1024
ROW_OUT = 1408
ROW_KERNEL = 1536
ROW_BIAS = 1600
ROWS_USED = 1616
PACK_ROWS = 2048

NT = (((1,), (1,)), ((), ()))
TN = (((0,), (0,)), ((), ()))


def dot(a, b, dims=(((1,), (0,)), ((), ()))):
    return lax.dot_general(a, b, dims, preferred_element_type=f32)


def gelu_value(t):
    t2 = t * t
    u = jnp.tanh(t * (t2 * (0.044715 * gelu_coef) + gelu_coef))
    return t * (0.5 * u + 0.5)


def gelu_pair(t):
    t2 = t * t
    u = jnp.tanh(t * (t2 * (0.044715 * gelu_coef) + gelu_coef))
    h = 0.5 * u + 0.5
    value = t * h
    slope = h + value * (1.0 - h) * (t2 * (2.0 * 0.134145 * gelu_coef) + 2.0 * gelu_coef)
    return value, slope


def normalise(v):
    inverse = lax.rsqrt(jnp.mean(v * v, axis=-1, keepdims=True) + epsilon)
    return inverse, v * inverse


def lane_group(g):
    return slice(g * LANES, (g + 1) * LANES)


def to_columns_kernel(x_ref, o_ref, rows):
    rows[...] = x_ref[...].reshape(RD * CD, C).astype(f32)
    for col in range(CD):
        part = rows[pl.ds(col, RD, stride=CD), :]
        o_ref[col // 2, (col % 2) * RD : (col % 2 + 1) * RD, :] = part.astype(bf16)


def to_columns(x):
    return pl.pallas_call(
        to_columns_kernel,
        out_shape=jax.ShapeDtypeStruct((CD // 2, 2 * RD, C), bf16),
        scratch_shapes=[pltpu.VMEM((RD * CD, C), f32)],
        compiler_params=pltpu.CompilerParams(vmem_limit_bytes=VMEM_LIMIT),
        cost_estimate=pl.CostEstimate(flops=0, bytes_accessed=4 * RD * CD * C, transcendentals=0),
        name="to_columns",
    )(x)


def from_columns_kernel(x_ref, o_ref, cols):
    cols[...] = x_ref[...].reshape(RD * CD, C).astype(f32)
    for row in range(RD):
        o_ref[row, :, :] = cols[pl.ds(row, CD, stride=RD), :].astype(bf16)


def from_columns(x):
    return pl.pallas_call(
        from_columns_kernel,
        out_shape=jax.ShapeDtypeStruct((RD, CD, C), bf16),
        scratch_shapes=[pltpu.VMEM((RD * CD, C), f32)],
        compiler_params=pltpu.CompilerParams(vmem_limit_bytes=VMEM_LIMIT),
        cost_estimate=pl.CostEstimate(flops=0, bytes_accessed=4 * RD * CD * C, transcendentals=0),
        name="from_columns",
    )(x)


def expand_kernel(x_ref, gain_ref, w_ref, e_ref, s_ref, n_ref):
    def step(i, carry):
        at = pl.ds(pl.multiple_of(i * 256, 256), 256)
        normed = (normalise(x_ref[at, :].astype(f32))[1] * gain_ref[...]).astype(bf16)
        n_ref[at, :] = normed
        for g in range(GROUPS):
            value, slope = gelu_pair(dot(normed, w_ref[:, lane_group(g)]))
            e_ref[at, lane_group(g)] = value.astype(bf16)
            s_ref[at, lane_group(g)] = slope.astype(bf16)
        return carry

    lax.fori_loop(0, x_ref.shape[0] // 256, step, 0)


def expand(x, gain, w):
    tokens = x.shape[0]
    block = 512
    wide = pl.BlockSpec((block, E), lambda i: (i, 0))
    slim = pl.BlockSpec((block, C), lambda i: (i, 0))
    return pl.pallas_call(
        expand_kernel,
        grid=(tokens // block,),
        in_specs=[
            slim,
            pl.BlockSpec((1, C), lambda i: (0, 0)),
            pl.BlockSpec((C, E), lambda i: (0, 0)),
        ],
        out_specs=[wide, wide, slim],
        out_shape=[
            jax.ShapeDtypeStruct((tokens, E), bf16),
            jax.ShapeDtypeStruct((tokens, E), bf16),
            jax.ShapeDtypeStruct((tokens, C), bf16),
        ],
        compiler_params=pltpu.CompilerParams(vmem_limit_bytes=VMEM_LIMIT),
        cost_estimate=pl.CostEstimate(
            flops=2 * tokens * C * E + 20 * tokens * E,
            bytes_accessed=tokens * (4 * E + 4 * C),
            transcendentals=tokens * E,
        ),
        name="expand",
    )(x, gain, w)


def conv_row(src, taps, g, row):
    total = None
    for a in range(3):
        for b in range(3):
            term = taps[3 * a + b] * src[g, row + a, 15 + b : 15 + b + CD, :]
            total = term if total is None else total + term
    return total


def depth_kernel(
    e_ref,
    x_ref,
    halo_ref,
    strip_ref,
    gain_ref,
    w1_ref,
    dw_ref,
    w2_ref,
    send_ref,
    d_ref,
    s_ref,
    ss_ref,
    ext,
    side,
    mid,
):
    gain = gain_ref[...]
    halo = normalise(halo_ref[...].reshape(4 * CD, C).astype(f32))[1]
    halo = (halo * gain).astype(bf16)
    strip = normalise(strip_ref[...].reshape(6 * 48, C).astype(f32))[1]
    strip = (strip * gain).astype(bf16)
    for g in range(GROUPS):
        weight = w1_ref[:, lane_group(g)]
        value = gelu_value(dot(halo, weight)).astype(bf16).astype(f32).reshape(4, CD, C)
        for k, row in enumerate((0, 1, RD + 2, RD + 3)):
            ext[g, row, 16 : 16 + CD, :] = value[k]
        value = gelu_value(dot(strip, weight)).astype(bf16).astype(f32).reshape(6, 48, C)
        side[g, :, 0:48, :] = value
        side[g, :, 48:56, :] = jnp.zeros((6, 8, C), f32)
        for row in range(RD + 4):
            ext[g, row, 15:16, :] = value[1, row : row + 1]
            ext[g, row, 16 + CD : 17 + CD, :] = value[4, row : row + 1]

    def fill(row, carry):
        for g in range(GROUPS):
            ext[g, row + 2, 16 : 16 + CD, :] = e_ref[row, :, lane_group(g)].astype(f32)
        return carry

    lax.fori_loop(0, RD, fill, 0)

    def taps_of(g):
        return [dw_ref[t : t + 1, lane_group(g)] for t in range(9)]

    def block(i, carry):
        for k in range(4):
            row = i * 4 + k
            at = pl.ds(pl.multiple_of(row * CD, CD), CD)
            ring = pl.ds(pl.multiple_of(row * CD + CD, CD), CD)
            for g in range(GROUPS):
                value, slope = gelu_pair(conv_row(ext, taps_of(g), g, row + 1))
                d_ref[at, lane_group(g)] = value.astype(bf16)
                s_ref[ring, lane_group(g)] = slope.astype(bf16)
        four = pl.ds(pl.multiple_of(i * 4 * CD, 4 * CD), 4 * CD)
        mid[four, :] = x_ref[four, :].astype(f32) + dot(d_ref[four, :], w2_ref[...])
        return carry

    lax.fori_loop(0, RD // 4, block, 0)
    for g in range(GROUPS):
        taps = taps_of(g)
        for row in (0, RD + 1):
            slope = gelu_pair(conv_row(ext, taps, g, row))[1]
            s_ref[row * CD : (row + 1) * CD, lane_group(g)] = slope.astype(bf16)
        for end in range(2):
            total = None
            for a in range(3):
                for b in range(3):
                    term = taps[3 * a + b] * side[g, 3 * end + b, a : a + 48, :]
                    total = term if total is None else total + term
            ss_ref[end, :, lane_group(g)] = gelu_pair(total)[1].astype(bf16)
    for col in range(CD):
        part = mid[pl.ds(col, RD, stride=CD), :]
        send_ref[col // 2, (col % 2) * RD : (col % 2 + 1) * RD, :] = part.astype(bf16)


def depth(expanded, x, halo, strip, gain, w1, taps, w2):
    tokens = RD * CD
    return pl.pallas_call(
        depth_kernel,
        out_shape=[
            jax.ShapeDtypeStruct((CD // 2, 2 * RD, C), bf16),
            jax.ShapeDtypeStruct((tokens, E), bf16),
            jax.ShapeDtypeStruct((tokens + 2 * CD, E), bf16),
            jax.ShapeDtypeStruct((2, 48, E), bf16),
        ],
        scratch_shapes=[
            pltpu.VMEM((GROUPS, RD + 4, 96, LANES), f32),
            pltpu.VMEM((GROUPS, 6, 56, LANES), f32),
            pltpu.VMEM((tokens, C), f32),
        ],
        compiler_params=pltpu.CompilerParams(vmem_limit_bytes=VMEM_LIMIT),
        cost_estimate=pl.CostEstimate(
            flops=2 * tokens * C * E + 40 * tokens * E,
            bytes_accessed=tokens * (6 * E + 4 * C),
            transcendentals=tokens * E,
        ),
        name="depth",
    )(expanded.reshape(RD, CD, E), x, halo, strip, gain, w1, taps, w2)


def side_by_side(x):
    return jnp.concatenate([x[:64], x[64:]], axis=1)


def stacked(x):
    return jnp.concatenate([x[:, :C], x[:, C:]], axis=0)


def diagonal(x):
    return jnp.concatenate([x[:64, :C], x[64:, C:]], axis=0)


def attend_kernel(
    m_ref,
    c_ref,
    gain_ref,
    wq_ref,
    wo_ref,
    bias_ref,
    bo_ref,
    gm_ref,
    gq_ref,
    go_ref,
    ds_ref,
    mid,
    cot,
    out,
    grad,
    norms,
    atts,
    cots,
    mixes,
):
    mid[...] = m_ref[...].reshape(RD * CD, C).astype(f32)
    cot[...] = c_ref[...].reshape(RD * CD, C).astype(f32)
    grad[...] = jnp.zeros(grad.shape, f32)
    ds_ref[...] = jnp.zeros(ds_ref.shape, f32)
    gain = gain_ref[...]
    scale = 32**-0.5
    row_head = lax.broadcasted_iota(jnp.int32, (256, 256), 0) // 64
    lane_head = (lax.broadcasted_iota(jnp.int32, (256, 256), 1) % C) // 32
    own_head = row_head == lane_head
    fold_head = (lax.broadcasted_iota(jnp.int32, (64, 256), 1) % C) // 32

    def per_head(x):
        x = side_by_side(x)
        x = jnp.concatenate([x, x, x, x], axis=0)
        return jnp.where(own_head, x, jnp.zeros_like(x))

    def per_window(x):
        none = jnp.zeros((64, C), x.dtype)
        top = jnp.concatenate([x[:64], none], axis=1)
        low = jnp.concatenate([none, x[64:]], axis=1)
        return jnp.concatenate([top, low], axis=0)

    def fold(x):
        total = x[0:64]
        for h in range(1, HEADS):
            total = jnp.where(fold_head == h, x[h * 64 : (h + 1) * 64], total)
        return stacked(total)

    def windows(src, r0, width, first):
        parts = []
        for c in range(2):
            for il in range(2):
                at = pl.ds(c * (width // 2) + il * 16 + first + r0, 32, stride=width)
                parts.append(src[at, :])
        return jnp.concatenate(parts, axis=0)

    def put(dst, r0, width, first, x):
        for c in range(2):
            for il in range(2):
                at = pl.ds(c * (width // 2) + il * 16 + first + r0, 32, stride=width)
                k = 2 * c + il
                dst[at, :] = x[k * 32 : (k + 1) * 32]

    def pair(r0, carry):
        at = pl.ds(pl.multiple_of(r0 * 128, 128), 128)
        m = windows(mid, r0, 64, 0)
        ct = windows(cot, r0, 64, 0)
        ctb = ct.astype(bf16)
        inverse, unit = normalise(m)
        normed = (unit * gain).astype(bf16)
        mixture = dot(normed, wq_ref[...])
        q = (mixture[:, :C] * scale).astype(bf16)
        k = mixture[:, C : 2 * C].astype(bf16)
        v = mixture[:, 2 * C :].astype(bf16)
        ga = dot(ctb, wo_ref[...], NT).astype(bf16)
        k4 = per_head(k)
        v4 = per_head(v)
        qd = per_window(q)
        gd = per_window(ga)
        scores = (dot(k4, qd, NT) + bias_ref[...]).reshape(HEADS, 64, 128)
        weights = jnp.exp(scores - jnp.max(scores, axis=1, keepdims=True))
        prob = weights * (1.0 / jnp.sum(weights, axis=1, keepdims=True))
        rounded = prob.reshape(256, 128).astype(bf16)
        att = diagonal(dot(rounded, v4, TN)).astype(bf16)
        gp = dot(v4, gd, NT).reshape(HEADS, 64, 128)
        gs = prob * (gp - jnp.sum(prob * gp, axis=1, keepdims=True))
        gs = gs.reshape(256, 128)
        ds_ref[...] += gs
        gr = gs.astype(bf16)
        gv = fold(dot(rounded, gd))
        gk = fold(dot(gr, qd))
        gq = diagonal(dot(gr, k4, TN)) * scale
        gx = jnp.concatenate([gq, gk, gv], axis=1).astype(bf16)
        gn = dot(gx, wq_ref[...], NT).astype(bf16).astype(f32)
        scaled = gn * gain
        gm = ct + inverse * (scaled - unit * jnp.mean(scaled * unit, axis=-1, keepdims=True))
        put(grad, r0, 80, 1, gm)
        put(out, r0, 64, 0, m + dot(att, wo_ref[...]))
        norms[at, :] = normed
        atts[at, :] = att
        cots[at, :] = ctb
        mixes[at, :] = gx
        return carry

    lax.fori_loop(0, 16, pair, 0)
    for k in range(3):
        gq_ref[k * C : (k + 1) * C, :] = dot(norms[...], mixes[:, k * C : (k + 1) * C], TN)
    go_ref[...] = dot(atts[...], cots[...], TN)
    for c in range(2):
        low = grad[pl.ds(c * 40 + 32, 24, stride=80), :]
        high = grad[pl.ds(c * 40 + 1 + 8 * 80, 24, stride=80), :]
        grad[pl.ds(c * 40 + 8 * 80, 24, stride=80), :] = low
        grad[pl.ds(c * 40 + 33, 24, stride=80), :] = high
    bo_ref[...] = out[...].astype(bf16).reshape(bo_ref.shape)
    gm_ref[...] = grad[...].astype(bf16).reshape(gm_ref.shape)


def attend(mid, cot, gain, wq, wo, bias):
    tokens = RD * CD
    return pl.pallas_call(
        attend_kernel,
        out_shape=[
            jax.ShapeDtypeStruct((32, 64, C), bf16),
            jax.ShapeDtypeStruct((32, 80, C), bf16),
            jax.ShapeDtypeStruct((3 * C, C), f32),
            jax.ShapeDtypeStruct((C, C), f32),
            jax.ShapeDtypeStruct((256, 128), f32),
        ],
        scratch_shapes=[
            pltpu.VMEM((tokens, C), f32),
            pltpu.VMEM((tokens, C), f32),
            pltpu.VMEM((tokens, C), f32),
            pltpu.VMEM((32 * 80, C), f32),
            pltpu.VMEM((tokens, C), bf16),
            pltpu.VMEM((tokens, C), bf16),
            pltpu.VMEM((tokens, C), bf16),
            pltpu.VMEM((tokens, 3 * C), bf16),
        ],
        compiler_params=pltpu.CompilerParams(vmem_limit_bytes=VMEM_LIMIT),
        cost_estimate=pl.CostEstimate(
            flops=40 * tokens * C * C, bytes_accessed=tokens * 8 * C, transcendentals=tokens * 256
        ),
        name="attend",
    )(mid, cot, gain, wq, wo, bias)


def project_grad_kernel(g_ref, w2_ref, d_ref, s_ref, b_ref, gp_ref, gm_ref, cols):
    cols[...] = g_ref[...].reshape(CD * 40, C).astype(f32)
    gp_ref[...] = jnp.zeros(gp_ref.shape, f32)

    def rows(first, count):
        parts = [cols[pl.ds(first + k, CD, stride=40), :] for k in range(count)]
        return jnp.concatenate(parts, axis=0).astype(bf16)

    def before(g, at):
        for k in range(GROUPS):
            wide = dot(g, w2_ref[lane_group(k), :], NT)
            wide = wide * s_ref[at, lane_group(k)].astype(f32)
            b_ref[at, lane_group(k)] = wide.astype(bf16)

    def block(i, carry):
        four = pl.ds(pl.multiple_of(i * 4 * CD, 4 * CD), 4 * CD)
        ring = pl.ds(pl.multiple_of(i * 4 * CD + CD, CD), 4 * CD)
        g = rows(i * 4 + 1, 4)
        gm_ref[four, :] = g
        before(g, ring)
        for k in range(GROUPS):
            gp_ref[lane_group(k), :] += dot(g, d_ref[four, lane_group(k)], TN)
        return carry

    lax.fori_loop(0, RD // 4, block, 0)
    for row in (0, RD + 1):
        before(rows(row, 1), pl.ds(row * CD, CD))


def project_grad(gm, w2, depthed, slope):
    tokens = RD * CD
    return pl.pallas_call(
        project_grad_kernel,
        out_shape=[
            jax.ShapeDtypeStruct((tokens + 2 * CD, E), bf16),
            jax.ShapeDtypeStruct((E, C), f32),
            jax.ShapeDtypeStruct((tokens, C), bf16),
        ],
        scratch_shapes=[pltpu.VMEM((CD * 40, C), f32)],
        compiler_params=pltpu.CompilerParams(vmem_limit_bytes=VMEM_LIMIT),
        cost_estimate=pl.CostEstimate(
            flops=4 * tokens * C * E, bytes_accessed=tokens * (6 * E + 4 * C), transcendentals=0
        ),
        name="project_grad",
    )(gm, w2, depthed, slope)


def depth_grad_kernel(
    b_ref,
    strip_ref,
    ss_ref,
    w2_ref,
    dw_ref,
    e_ref,
    s_ref,
    n_ref,
    gp_ref,
    gq_ref,
    go_ref,
    gb_ref,
    x_ref,
    pack_ref,
    ext,
    sums,
    total,
):
    strip = strip_ref[...].reshape(2 * 48, C)
    for g in range(GROUPS):
        wide = dot(strip, w2_ref[lane_group(g), :], NT).reshape(2, 48, LANES)
        wide = (wide * ss_ref[:, :, lane_group(g)].astype(f32)).astype(bf16).astype(f32)
        for row in range(RD + 2):
            ext[g, row, 15:16, :] = wide[0, row : row + 1]
            ext[g, row, 16 + CD : 17 + CD, :] = wide[1, row : row + 1]

    def fill(row, carry):
        for g in range(GROUPS):
            ext[g, row, 16 : 16 + CD, :] = b_ref[row, :, lane_group(g)].astype(f32)
        return carry

    lax.fori_loop(0, RD + 2, fill, 0)
    sums[...] = jnp.zeros(sums.shape, f32)
    total[...] = jnp.zeros(total.shape, f32)

    def block(i, carry):
        for k in range(4):
            row = i * 4 + k
            at = pl.ds(pl.multiple_of(row * CD, CD), CD)
            for g in range(GROUPS):
                own = e_ref[at, lane_group(g)].astype(f32)
                running = None
                for t in range(9):
                    window = ext[g, row + t // 3, 15 + t % 3 : 15 + t % 3 + CD, :]
                    term = dw_ref[8 - t : 9 - t, lane_group(g)] * window
                    running = term if running is None else running + term
                    sums[g, 8 - t] += jnp.sum((own * window).reshape(CD // 8, 8, LANES), axis=0)
                wide = running * s_ref[at, lane_group(g)].astype(f32)
                x_ref[at, lane_group(g)] = wide.astype(bf16)
        four = pl.ds(pl.multiple_of(i * 4 * CD, 4 * CD), 4 * CD)
        normed = n_ref[four, :]
        for g in range(GROUPS):
            total[lane_group(g), :] += dot(normed, x_ref[four, lane_group(g)], TN)
        return carry

    lax.fori_loop(0, RD // 4, block, 0)
    pack_ref[ROW_EXPAND : ROW_EXPAND + E, :] = total[...].astype(bf16)
    pack_ref[ROW_PROJECT : ROW_PROJECT + E, :] = gp_ref[...].astype(bf16)
    pack_ref[ROW_QKV : ROW_QKV + 3 * C, :] = gq_ref[...].astype(bf16)
    pack_ref[ROW_OUT : ROW_OUT + C, :] = go_ref[...].astype(bf16)
    for g in range(GROUPS):
        kernel_sums = jnp.sum(sums[g], axis=1)
        kernel_sums = jnp.concatenate([kernel_sums, jnp.zeros((7, LANES), f32)], axis=0)
        pack_ref[ROW_KERNEL + 16 * g : ROW_KERNEL + 16 * g + 16, :] = kernel_sums.astype(bf16)
    pack_ref[ROW_BIAS : ROW_BIAS + 16, :] = gb_ref[...].astype(bf16)
    pack_ref[ROWS_USED:PACK_ROWS, :] = jnp.zeros((PACK_ROWS - ROWS_USED, C), bf16)


def depth_grad(before, strip, ss, w2, taps, expanded, slope, normed, gp, gq, go, gb):
    tokens = RD * CD
    return pl.pallas_call(
        depth_grad_kernel,
        out_shape=[
            jax.ShapeDtypeStruct((tokens, E), bf16),
            jax.ShapeDtypeStruct((PACK_ROWS, C), bf16),
        ],
        scratch_shapes=[
            pltpu.VMEM((GROUPS, RD + 2, 96, LANES), f32),
            pltpu.VMEM((GROUPS, 9, 8, LANES), f32),
            pltpu.VMEM((E, C), f32),
        ],
        compiler_params=pltpu.CompilerParams(vmem_limit_bytes=VMEM_LIMIT),
        cost_estimate=pl.CostEstimate(
            flops=2 * tokens * C * E + 60 * tokens * E,
            bytes_accessed=tokens * (8 * E + 4 * C),
            transcendentals=0,
        ),
        name="depth_grad",
    )(
        before.reshape(RD + 2, CD, E), strip, ss, w2, taps, expanded, slope, normed, gp, gq, go, gb
    )


def image_grad_kernel(g_ref, w_ref, gain_ref, x_ref, m_ref, o_ref):
    def step(i, carry):
        at = pl.ds(pl.multiple_of(i * 256, 256), 256)
        scaled = dot(g_ref[at, :], w_ref[...], NT) * gain_ref[...]
        inverse, unit = normalise(x_ref[at, :].astype(f32))
        mean = jnp.mean(scaled * unit, axis=-1, keepdims=True)
        o_ref[at, :] = (m_ref[at, :].astype(f32) + inverse * (scaled - unit * mean)).astype(bf16)
        return carry

    lax.fori_loop(0, x_ref.shape[0] // 256, step, 0)


def image_grad(g, w, gain, x, gm):
    tokens = x.shape[0]
    block = 1024
    slim = pl.BlockSpec((block, C), lambda i: (i, 0))
    return pl.pallas_call(
        image_grad_kernel,
        grid=(tokens // block,),
        in_specs=[
            pl.BlockSpec((block, E), lambda i: (i, 0)),
            pl.BlockSpec((C, E), lambda i: (0, 0)),
            pl.BlockSpec((1, C), lambda i: (0, 0)),
            slim,
            slim,
        ],
        out_specs=slim,
        out_shape=jax.ShapeDtypeStruct((tokens, C), bf16),
        compiler_params=pltpu.CompilerParams(vmem_limit_bytes=VMEM_LIMIT),
        cost_estimate=pl.CostEstimate(
            flops=2 * tokens * C * E, bytes_accessed=tokens * (2 * E + 6 * C), transcendentals=0
        ),
        name="image_grad",
    )(g, w, gain, x, gm)


def sum_parts_kernel(factor, x_ref, o_ref):
    total = x_ref[0].astype(f32)
    for k in range(1, x_ref.shape[0]):
        total = total + x_ref[k].astype(f32)
    total = (total * factor).astype(bf16)
    for k in range(x_ref.shape[0]):
        o_ref[k] = total


def sum_parts(x, factor):
    return pl.pallas_call(
        lambda x_ref, o_ref: sum_parts_kernel(factor, x_ref, o_ref),
        out_shape=jax.ShapeDtypeStruct(x.shape, bf16),
        compiler_params=pltpu.CompilerParams(vmem_limit_bytes=VMEM_LIMIT),
        cost_estimate=pl.CostEstimate(
            flops=2 * x.size, bytes_accessed=4 * x.size, transcendentals=0
        ),
        name="sum_parts",
    )(x)


def column_sums(x):
    line = jnp.sum(x, axis=1, keepdims=True)
    return jnp.broadcast_to(line, (C, C)).T[0:1]


def unpack_kernel(
    p_ref, w1_ref, wq_ref, gain1_ref, gain2_ref, g1_ref, ex_ref, k_ref, pr_ref, g2_ref, qk_ref,
    o_ref, b_ref
):
    first = jnp.zeros((C, C), f32)
    second = jnp.zeros((C, C), f32)
    for g in range(GROUPS):
        part = p_ref[ROW_EXPAND + g * C : ROW_EXPAND + (g + 1) * C, :].astype(f32)
        ex_ref[:, lane_group(g)] = part
        first = first + part * w1_ref[:, lane_group(g)].astype(f32)
        part = p_ref[ROW_PROJECT + g * C : ROW_PROJECT + (g + 1) * C, :].astype(f32)
        pr_ref[g * C : (g + 1) * C, :] = part.T
        part = p_ref[ROW_KERNEL + g * 16 : ROW_KERNEL + (g + 1) * 16, :].astype(f32)
        k_ref[:, lane_group(g)] = part[0:9]
    for k in range(3):
        part = p_ref[ROW_QKV + k * C : ROW_QKV + (k + 1) * C, :].astype(f32)
        qk_ref[:, lane_group(k)] = part
        second = second + part * wq_ref[:, lane_group(k)].astype(f32)
    g1_ref[...] = column_sums(first) / gain1_ref[...]
    g2_ref[...] = column_sums(second) / gain2_ref[...]
    o_ref[...] = p_ref[ROW_OUT : ROW_OUT + C, :].astype(f32)
    part = p_ref[ROW_BIAS : ROW_BIAS + 16, :].astype(f32)
    b_ref[...] = jnp.concatenate([part[0:4], part[4:8]], axis=1)[:, :225]


def unpack(pack, w1, wq, gain1, gain2):
    return pl.pallas_call(
        unpack_kernel,
        out_shape=[
            jax.ShapeDtypeStruct((1, C), f32),
            jax.ShapeDtypeStruct((C, E), f32),
            jax.ShapeDtypeStruct((9, E), f32),
            jax.ShapeDtypeStruct((E, C), f32),
            jax.ShapeDtypeStruct((1, C), f32),
            jax.ShapeDtypeStruct((C, 3 * C), f32),
            jax.ShapeDtypeStruct((C, C), f32),
            jax.ShapeDtypeStruct((HEADS, 225), f32),
        ],
        compiler_params=pltpu.CompilerParams(vmem_limit_bytes=VMEM_LIMIT),
        cost_estimate=pl.CostEstimate(
            flops=4 * pack.size, bytes_accessed=6 * pack.size, transcendentals=0
        ),
        name="unpack",
    )(pack, w1, wq, gain1, gain2)


def pair_onehot():
    place = np.arange(64)
    row = 2 * ((place % 32) // 8) + place // 32
    col = place % 8
    first, second = place[None, :], place[:, None]
    index = 15 * (row[first] - row[second] + 7) + col[first] - col[second] + 7
    index = jnp.asarray(np.concatenate([index, index], axis=1), jnp.int32)
    return (index[:, :, None] == jnp.arange(225, dtype=jnp.int32)).astype(f32)


def per_device(
    image,
    cotangent,
    norm1_gain,
    w_expand,
    dw_kernel,
    w_project,
    norm2_gain,
    w_qkv,
    w_out,
    bias_table,
):
    factor = 1.0 / math.sqrt(RD * CD * 128)
    w1 = w_expand.astype(bf16)
    w2 = w_project.astype(bf16)
    wq = w_qkv.astype(bf16)
    wo = w_out.astype(bf16)
    gain1 = norm1_gain.reshape(1, C)
    gain2 = norm2_gain.reshape(1, C)
    onehot = pair_onehot()
    bias = jnp.einsum("hq,jlq->hjl", bias_table, onehot, precision=lax.Precision.HIGHEST)
    bias = bias.reshape(HEADS * 64, 128)

    row_up = [(i, i + 1) for i in range(3)]
    row_down = [(i + 1, i) for i in range(3)]
    col_up = [(i, i + 1) for i in range(31)]
    col_down = [(i + 1, i) for i in range(31)]

    above = lax.ppermute(image[RD - 2 :], "rows", row_up)
    below = lax.ppermute(image[:2], "rows", row_down)
    cot_windows = lax.all_to_all(to_columns(cotangent), PLANE, 0, 0, tiled=True)
    tokens = image.reshape(RD * CD, C)
    expanded, slope1, normed1 = expand(tokens, gain1, w1)

    halo = jnp.concatenate([above, below], axis=0)
    left = jnp.concatenate([above[:, :2], image[:, :2], below[:, :2]], axis=0)
    right = jnp.concatenate([above[:, -2:], image[:, -2:], below[:, -2:]], axis=0)
    left = left.transpose(1, 0, 2)
    right = right.transpose(1, 0, 2)
    before_left = lax.ppermute(right, COLS, col_up)
    after_right = lax.ppermute(left, COLS, col_down)
    strip = jnp.concatenate([before_left, left[:1], right[1:], after_right], axis=0)
    strip = jnp.pad(strip, ((0, 0), (0, 12), (0, 0)))
    send, depthed, slope2, slope2_strip = depth(
        expanded, tokens, halo, strip, gain1, w1, dw_kernel, w2
    )

    mid_windows = lax.all_to_all(send, PLANE, 0, 0, tiled=True)
    out_windows, grad_windows, grad_qkv, grad_out, score_sums = attend(
        mid_windows, cot_windows, gain2, wq, wo, bias
    )
    grad_cols = lax.all_to_all(grad_windows, PLANE, 0, 0, tiled=True)
    grad_left = lax.ppermute(grad_cols[31, 40:], COLS, col_up)
    grad_right = lax.ppermute(grad_cols[0, :40], COLS, col_down)
    before, grad_project, grad_middle = project_grad(grad_cols, w2, depthed, slope2)
    grad_strip = jnp.pad(jnp.stack([grad_left, grad_right]), ((0, 0), (0, 8), (0, 0)))

    grad_bias = jnp.einsum(
        "hjl,jlq->hq",
        score_sums.reshape(HEADS, 64, 128),
        onehot,
        precision=lax.Precision.HIGHEST,
    )
    grad_bias = jnp.pad(grad_bias, ((0, 0), (0, 31)))
    grad_bias = jnp.concatenate([grad_bias[:, :128], grad_bias[:, 128:]], axis=0)
    grad_bias = jnp.pad(grad_bias, ((0, 8), (0, 0)))
    block_cols = lax.all_to_all(out_windows, PLANE, 0, 0, tiled=True)

    grad_wide, pack = depth_grad(
        before, grad_strip, slope2_strip, w2, dw_kernel, expanded, slope1, normed1,
        grad_project, grad_qkv, grad_out, grad_bias,
    )
    parts = lax.all_to_all(pack.reshape(128, 16, C), ALL, 0, 0, tiled=True)
    grad_image = image_grad(grad_wide, w1, gain1, tokens, grad_middle)
    block_out = from_columns(block_cols)
    whole = lax.all_to_all(sum_parts(parts, factor), ALL, 0, 0, tiled=True)
    g1, ge, gk, gp, g2, gq, go, gb = unpack(whole.reshape(PACK_ROWS, C), w1, wq, gain1, gain2)
    return (
        block_out,
        grad_image.reshape(RD, CD, C),
        g1.reshape(C),
        ge,
        gk,
        gp,
        g2.reshape(C),
        gq,
        go,
        gb,
    )


def solution(mesh):
    mesh = Mesh(mesh.devices.reshape(4, 8, 4), ALL)
    tiles = P("rows", COLS, None)
    return jax.shard_map(
        per_device,
        mesh=mesh,
        in_specs=(tiles, tiles) + (P(),) * 8,
        out_specs=(tiles, tiles) + (P(),) * 8,
        check_vma=False,
    )
```

time: 483 us -> 197 us (0.41); the launches traced: 475 us -> 196 us
  waiting for transfers between devices: 172 us -> 33.1 us
  Pallas kernels: 0 us -> 61.5 us
  blocking collectives: 70.7 us -> 25 us
  other arithmetic: 44.6 us -> 1.11 us
  matrix products: 45.5 us -> 7.68 us
  local copies, waits for them, and re-layouts: 51.8 us -> 15.6 us
  starting transfers between devices: 74.7 us -> 51 us
  between operations: 15.3 us -> 1.15 us
    psum x1 -> x0, waiting for transfers between devices: 143 us -> none  [per_device(): lax.psum((grad_gain_one, grad_expand, grad_kernel, grad_project, grad_gai...]
    psum x1 -> x0, blocking collectives: 70.7 us -> none  [per_device(): lax.psum((grad_gain_one, grad_expand, grad_kernel, grad_project, grad_gai...]
    pallas_call x0 -> x10, Pallas kernels: none -> 61.5 us  [the longest x1 21.3 us: attend(): pl.pallas_call(attend_kernel, out_shape=[jax.ShapeDtypeStruct((32, 64, C)...]
    dot_general x20 -> x2, matrix products: 45.5 us -> 7.68 us  [the longest x1 4.41 us: per_device(): jnp.einsum('hjl,jlq->hq', score_sums.reshape(HEADS, 64, 128), onehot, pre...]
    all_to_all x0 -> x1, blocking collectives: none -> 25 us  [per_device(): parts = lax.all_to_all(pack.reshape(128, 16, C), ALL, 0, 0, tiled=True)]
    convert_element_type x7 -> x4, other arithmetic: 23.8 us -> 0.98 us  [the longest x1 0.94 us: per_device(): wq = w_qkv.astype(bf16)]
    all_to_all x8 -> x5, starting transfers between devices: 53.2 us -> 36.5 us  [the longest x1 17.3 us: per_device(): mid_windows = lax.all_to_all(send, PLANE, 0, 0, tiled=True)]
    convert_element_type x4 -> x0, local copies, waits for them, and re-layouts: 14 us -> none  [the longest x2 9.28 us: attend_backward(): grad_mixture = grad_mixture.astype(jnp.bfloat16).reshape(-1, 3 * channels)]
  transfers between devices with their start and end apart: 17 -> 11, of which waited for: 8 -> 5; matrix products, arithmetic and copies ran while one was open for 17% -> 5% of each run, Pallas kernels for 0% -> 14%
where the time goes in v1:
time: 197 us; the launch traced here: 196 us
  Pallas kernels  61.5 us (31%)
  starting transfers between devices  51 us (26%)
  waiting for transfers between devices  33.1 us (17%)
  blocking collectives  25 us (13%)
  local copies, waits for them, and re-layouts  15.6 us (8%)
  matrix products  7.68 us (4%)
    all_to_all x1, blocking collectives, per_device(): parts = lax.all_to_all(pack.reshape(128, 16, C), ALL, 0, 0, tiled=True)  25 us
    pallas_call x1, Pallas kernels, attend(): pl.pallas_call(attend_kernel, out_shape=[jax.ShapeDtypeStruct((32, 64, C)...  21.3 us
    all_to_all x1, starting transfers between devices, per_device(): mid_windows = lax.all_to_all(send, PLANE, 0, 0, tiled=True)  17.3 us
    unnamed x70, local copies, waits for them, and re-layouts  14 us
    pallas_call x1, Pallas kernels, depth(): pl.pallas_call(depth_kernel, out_shape=[jax.ShapeDtypeStruct((CD // 2, 2...  11.3 us
    pallas_call x1, Pallas kernels, depth_grad(): pl.pallas_call(depth_grad_kernel, out_shape=[jax.ShapeDtypeStruct((tokens...  11 us
    all_to_all x1, waiting for transfers between devices, per_device(): block_cols = lax.all_to_all(out_windows, PLANE, 0, 0, tiled=True)  9.77 us
    all_to_all x1, waiting for transfers between devices, per_device(): grad_cols = lax.all_to_all(grad_windows, PLANE, 0, 0, tiled=True)  8.59 us
  transfers between devices with their start and end apart: 11, of which 5 were waited for; matrix products, arithmetic and copies ran while one was open for 5% of the time, Pallas kernels for 14%

profile of v1, /device:TPU:1, one launch (start us, length us, event | category | flops | bytes accessed | tf_op | source)
XLA Modules:
  0.0 196.1 jit_solution(6179183238695591937)
XLA Ops:
  0.6 0.0 copy-start
  0.7 0.8 fusion.19
  1.5 3.3 %collective-permute-start.1 = (bf16[2,64,128]{2,0,1:T(2,128)(2,1)S(1)}, bf16[2,64,128]{2,0,1:T(2,128)(2,1)S(1)}, u32[]{:S(2)}, u32[]{:S(2)}) collective-permute-start(bf16[2,64,128]{2,0,1:T(2,128)(2,1)S(1)} %copy.29), channel_id=1, source_target_pairs={{32,0},{64,32},{96,64},{33,1},{65,33},{97,65},{34,2},{66,34},{98,6... | collective-permute-start | bytes 98312 | tf_op jit(solution)/shard_map/ppermute | solution.py:705
  4.9 3.1 %collective-permute-start = (bf16[2,64,128]{2,0,1:T(2,128)(2,1)S(1)}, bf16[2,64,128]{2,0,1:T(2,128)(2,1)S(1)}, u32[]{:S(2)}, u32[]{:S(2)}) collective-permute-start(bf16[2,64,128]{2,0,1:T(2,128)(2,1)S(1)} %copy.28), channel_id=1, source_target_pairs={{0,32},{32,64},{64,96},{1,33},{33,65},{65,97},{2,34},{34,66},{66,9... | collective-permute-start | bytes 98312 | tf_op jit(solution)/shard_map/ppermute | solution.py:704
  8.0 0.0 copy-start.8
  8.0 1.0 copy-done.8
  9.1 1.4 to_columns.1
  10.5 7.3 %all-to-all-start.1 = ((bf16[32,64,128]{2,1,0:T(8,128)(2,1)}), bf16[32,64,128]{2,1,0:T(8,128)(2,1)S(1)}, u32[]{:S(2)}, u32[]{:S(2)}) async-start(bf16[32,64,128]{2,1,0:T(8,128)(2,1)} %to_columns.1), calls=%async_computation.1 | async-start | bytes 1048576 | tf_op jit(solution)/shard_map/all_to_all | solution.py:706
  17.8 0.0 copy-done.2
  18.0 4.8 %expand.1 = (bf16[2048,512]{1,0:T(8,128)(2,1)S(1)}, bf16[2048,512]{1,0:T(8,128)(2,1)}, bf16[2048,128]{1,0:T(8,128)(2,1)S(1)}) custom-call(bf16[2048,128]{1,0:T(8,128)(2,1)S(1)} %bitcast.30, f32[1,128]{1,0:T(1,128)S(1)} %bitcast.36, bf16[128,512]{1,0:T(8,128)(2,1)S(1)} %convert_element_type.21.w_ref.w1_ref), custom_call_target="tpu_custom_call" | custom-call | flops 289406976 | bytes 5242880 | tf_op jit(solution)/shard_map/expand/pallas_call | solution.py:125
  22.8 1.4 copy-done.1
  24.2 0.0 collective-permute-done.1
  24.2 0.0 collective-permute-done
  24.3 1.3 collective-permute-start.3
  25.6 4.2 %collective-permute-start.2 = (bf16[2,36,128]{2,1,0:T(8,128)(2,1)S(1)}, bf16[2,36,128]{2,1,0:T(8,128)(2,1)S(1)}, u32[]{:S(2)}, u32[]{:S(2)}) collective-permute-start(bf16[2,36,128]{2,1,0:T(8,128)(2,1)S(1)} %maximum_bitcast_fusion), channel_id=1, source_target_pairs={{0,1},{1,2},{2,3},{3,4},{4,5},{5,6},{6,7},{7,8},{8,9},{9,10},{10,1... | collective-permute-start | bytes 55304 | tf_op jit(solution)/shard_map/ppermute | solution.py:715
  29.8 0.1 pad_maximum_fusion
  29.9 0.0 copy-start.32
  29.9 0.0 collective-permute-done.3
  29.9 0.7 collective-permute-done.2
  30.7 11.3 %depth.1 = (bf16[32,64,128]{2,1,0:T(8,128)(2,1)S(1)}, bf16[2048,512]{1,0:T(8,128)(2,1)S(1)}, bf16[2176,512]{1,0:T(8,128)(2,1)}, bf16[2,48,512]{2,1,0:T(8,128)(2,1)S(1)}) custom-call(bf16[32,64,512]{2,1,0:T(8,128)(2,1)} %bitcast.29, bf16[2048,128]{1,0:T(8,128)(2,1)S(1)} %bitcast.31, bf16[4,64,128]{2,1,0:T(8,128)(2,1)S(1)} %copy.25.halo_ref, ...), custom_call_target="tpu_custom_call" | custom-call | flops 310378496 | bytes 7340032 | tf_op jit(solution)/shard_map/depth/pallas_call | solution.py:235
  42.0 0.8 copy-done.10
  42.8 0.6 copy-done.22
  43.4 0.0 all-to-all-done.1.c_ref
  43.4 17.3 %all-to-all-start = ((bf16[32,64,128]{2,1,0:T(8,128)(2,1)}), bf16[32,64,128]{2,1,0:T(8,128)(2,1)}, u32[]{:S(2)}, u32[]{:S(2)}) async-start(bf16[32,64,128]{2,1,0:T(8,128)(2,1)} %copy-done.10), calls=%async_computation | async-start | bytes 1048576 | tf_op jit(solution)/shard_map/all_to_all | solution.py:723
  60.8 0.9 convert_element_type.23.wq_ref
  61.8 3.3 %fusion.4 = f32[4,64,128]{2,0,1:T(4,128)S(1)} fusion(s32[64,128]{1,0:T(8,128)} %constant.7.clone, f32[4,225]{1,0:T(4,128)S(1)} %copy-done), kind=kOutput, calls=%fused_computation.5 | convolution fusion | flops 90316800 | bytes 167440 | tf_op jit(solution)/shard_map/hq,jlq->hjl/dot_general | solution.py:696
  65.0 0.7 copy.26
  65.7 6.9 %all-to-all-done.m_ref = bf16[32,64,128]{2,1,0:T(8,128)(2,1)} async-done(((bf16[32,64,128]{2,1,0:T(8,128)(2,1)}), bf16[32,64,128]{2,1,0:T(8,128)(2,1)}, u32[]{:S(2)}, u32[]{:S(2)}) %all-to-all-start) | async-done | bytes 524320 | tf_op jit(solution)/shard_map/all_to_all | solution.py:723
  72.6 0.9 copy-done.21
  73.5 21.3 %attend.1 = (bf16[32,64,128]{2,1,0:T(8,128)(2,1)S(1)}, bf16[32,80,128]{2,1,0:T(8,128)(2,1)S(1)}, f32[384,128]{1,0:T(8,128)S(1)}, f32[128,128]{1,0:T(8,128)S(1)}, f32[256,128]{1,0:T(8,128)S(1)}) custom-call(bf16[32,64,128]{2,1,0:T(8,128)(2,1)} %all-to-all-done.m_ref, bf16[32,64,128]{2,1,0:T(8,128)(2,1)S(1)} %all-to-all-done.1.c_ref, f32[1,128]{1,0:T(1,128)S(1)} %bitcast.40, ...), custom_call_target="tpu_custom_call" | custom-call | flops 1342177280 | bytes 2097152 | tf_op jit(solution)/shard_map/attend/pallas_call | solution.py:390
  94.8 0.8 copy-done.7
  95.7 0.8 copy-done.9
  96.5 0.7 copy-done.17
  97.1 0.6 copy-done.24
  97.8 0.7 copy-done.29
  98.4 3.9 %all-to-all-start.3 = ((bf16[32,80,128]{2,1,0:T(8,128)(2,1)}), bf16[32,80,128]{2,1,0:T(8,128)(2,1)S(1)}, u32[]{:S(2)}, u32[]{:S(2)}) async-start(bf16[32,80,128]{2,1,0:T(8,128)(2,1)} %copy-done.7), calls=%async_computation.3 | async-start | bytes 1310720 | tf_op jit(solution)/shard_map/all_to_all | solution.py:727
  102.3 4.4 %fusion.5 = f32[4,225]{1,0:T(4,128)S(1)} fusion(s32[64,128]{1,0:T(8,128)} %constant.7.clone, f32[4,64,128]{2,1,0:T(8,128)} %bitcast.42), kind=kOutput, calls=%fused_computation.6 | convolution fusion | flops 90316800 | bytes 167440 | tf_op jit(solution)/shard_map/hjl,jlq->hq/dot_general | solution.py:733
  106.8 8.6 %all-to-all-done.3.g_ref = bf16[32,80,128]{2,1,0:T(8,128)(2,1)S(1)} async-done(((bf16[32,80,128]{2,1,0:T(8,128)(2,1)}), bf16[32,80,128]{2,1,0:T(8,128)(2,1)S(1)}, u32[]{:S(2)}, u32[]{:S(2)}) %all-to-all-start.3) | async-done | bytes 655392 | tf_op jit(solution)/shard_map/all_to_all | solution.py:727
  115.4 1.3 collective-permute-start.4
  116.6 1.3 collective-permute-start.5
  117.9 0.0 copy-start.18
  118.0 0.0 copy-start.20
  118.0 0.0 copy-start.23
  118.0 0.0 copy-start.25
  118.0 5.9 %project_grad.1 = (bf16[2176,512]{1,0:T(8,128)(2,1)}, f32[512,128]{1,0:T(8,128)S(1)}, bf16[2048,128]{1,0:T(8,128)(2,1)S(1)}) custom-call(bf16[32,80,128]{2,1,0:T(8,128)(2,1)S(1)} %all-to-all-done.3.g_ref, bf16[512,128]{1,0:T(8,128)(2,1)S(1)} %convert_element_type.22.w2_ref, bf16[2048,512]{1,0:T(8,128)(2,1)S(1)} %get-tuple-element.39.d_ref, ...), custom_call_target="tpu_custom_call" | custom-call | flops 536870912 | bytes 7340032 | tf_op jit(solution)/shard_map/project_grad/pallas_call | solution.py:448
  123.9 0.8 copy-done.11
  124.7 0.0 collective-permute-done.4
  124.7 0.0 collective-permute-done.5
  124.8 11.0 %depth_grad.1 = (bf16[2048,512]{1,0:T(8,128)(2,1)S(1)}, bf16[2048,128]{1,0:T(8,128)(2,1)S(1)}) custom-call(bf16[34,64,512]{2,1,0:T(8,128)(2,1)} %bitcast.43, bf16[2,48,128]{2,1,0:T(8,128)(2,1)S(1)} %fusion.16.strip_ref, bf16[2,48,512]{2,1,0:T(8,128)(2,1)S(1)} %copy-done.23, bf16[512,128]{1,0:T(8,128)(2,1)S(1)} %convert_element_type.22.w2_ref, ...), custom_call_target="tpu_custom_call" | custom-call | flops 331350016 | bytes 9437184 | tf_op jit(solution)/shard_map/depth_grad/pallas_call | solution.py:535
  135.8 25.0 %all_to_all.30.x_ref = bf16[128,16,128]{2,1,0:T(8,128)(2,1)} all-to-all(bf16[128,16,128]{2,1,0:T(8,128)(2,1)S(1)} %bitcast.34), channel_id=1, replica_groups=mesh['rows'=4,'group'=8,'plane'=4] {'rows','group','plane'}, dimensions={0} | all-to-all | bytes 1048576 | tf_op jit(solution)/shard_map/all_to_all | solution.py:748
  160.8 4.5 %all-to-all-start.2 = ((bf16[32,64,128]{2,1,0:T(8,128)(2,1)}), bf16[32,64,128]{2,1,0:T(8,128)(2,1)S(1)}, u32[]{:S(2)}, u32[]{:S(2)}) async-start(bf16[32,64,128]{2,1,0:T(8,128)(2,1)} %copy-done.9), calls=%async_computation.2 | async-start | bytes 1048576 | tf_op jit(solution)/shard_map/all_to_all | solution.py:742
  165.3 1.0 copy-done.6
  166.3 0.2 sum_parts.1
  166.5 0.8 copy-done.3
  167.3 9.8 %all-to-all-done.2.x_ref = bf16[32,64,128]{2,1,0:T(8,128)(2,1)S(1)} async-done(((bf16[32,64,128]{2,1,0:T(8,128)(2,1)}), bf16[32,64,128]{2,1,0:T(8,128)(2,1)S(1)}, u32[]{:S(2)}, u32[]{:S(2)}) %all-to-all-start.2) | async-done | bytes 524320 | tf_op jit(solution)/shard_map/all_to_all | solution.py:742
  177.1 0.8 copy-done.4
  177.9 3.5 %all-to-all-start.5 = ((bf16[128,16,128]{2,1,0:T(8,128)(2,1)}), bf16[128,16,128]{2,1,0:T(8,128)(2,1)S(1)}, u32[]{:S(2)}, u32[]{:S(2)}) async-start(bf16[128,16,128]{2,1,0:T(8,128)(2,1)} %copy-done.3), calls=%async_computation.5 | async-start | bytes 1048576 | tf_op jit(solution)/shard_map/all_to_all | solution.py:751
  181.4 0.0 copy-start.5
  181.4 1.0 copy-done.5
  182.5 1.4 from_columns.1
  183.9 1.1 copy-done.12
  185.0 3.2 %image_grad.1 = bf16[2048,128]{1,0:T(8,128)(2,1)} custom-call(bf16[2048,512]{1,0:T(8,128)(2,1)S(1)} %get-tuple-element.49.g_ref, bf16[128,512]{1,0:T(8,128)(2,1)S(1)} %convert_element_type.21.w_ref.w1_ref, f32[1,128]{1,0:T(1,128)S(1)} %bitcast.38, bf16[2048,128]{1,0:T(8,128)(2,1)S(1)} %bitcast.32, bf16[2048,128]{1,0:T(8,128)(2,1)S(1)} %copy-done.12), custom_call_target="tpu_custom_call" | custom-call | flops 268435456 | bytes 3670016 | tf_op jit(solution)/shard_map/image_grad/pallas_call | solution.py:574
  188.2 7.0 %all-to-all-done.5 = bf16[128,16,128]{2,1,0:T(8,128)(2,1)S(1)} async-done(((bf16[128,16,128]{2,1,0:T(8,128)(2,1)}), bf16[128,16,128]{2,1,0:T(8,128)(2,1)S(1)}, u32[]{:S(2)}, u32[]{:S(2)}) %all-to-all-start.5) | async-done | bytes 524320 | tf_op jit(solution)/shard_map/all_to_all | solution.py:751
  195.2 0.9 unpack.1
  (61 shorter events, 0.3 us)
Async XLA Ops:
  0.6 61.1 %copy-start = (f32[4,225]{1,0:T(4,128)S(1)}, f32[4,225]{1,0:T(4,128)}, u32[]{:S(2)}) copy-start(f32[4,225]{1,0:T(4,128)} %param.20) | copy-start | bytes 10804
  0.7 17.2 %copy-start.2 = (bf16[32,64,128]{2,1,0:T(8,128)(2,1)S(1)}, bf16[32,64,128]{2,1,0:T(8,128)(2,1)}, u32[]{:S(2)}) copy-start(bf16[32,64,128]{2,1,0:T(8,128)(2,1)} %param.11) | copy-start | bytes 1572868
  1.5 22.7 %collective-permute-start.1 = (bf16[2,64,128]{2,0,1:T(2,128)(2,1)S(1)}, bf16[2,64,128]{2,0,1:T(2,128)(2,1)S(1)}, u32[]{:S(2)}, u32[]{:S(2)}) collective-permute-start(bf16[2,64,128]{2,0,1:T(2,128)(2,1)S(1)} %copy.29), channel_id=1, source_target_pairs={{32,0},{64,32},{96,64},{33,1},{65,33},{97,65},{34,2},{66,34},{98,6... | collective-permute-start | bytes 98312 | tf_op jit(solution)/shard_map/ppermute | solution.py:705
  4.9 19.3 %collective-permute-start = (bf16[2,64,128]{2,0,1:T(2,128)(2,1)S(1)}, bf16[2,64,128]{2,0,1:T(2,128)(2,1)S(1)}, u32[]{:S(2)}, u32[]{:S(2)}) collective-permute-start(bf16[2,64,128]{2,0,1:T(2,128)(2,1)S(1)} %copy.28), channel_id=1, source_target_pairs={{0,32},{32,64},{64,96},{1,33},{33,65},{65,97},{2,34},{34,66},{66,9... | collective-permute-start | bytes 98312 | tf_op jit(solution)/shard_map/ppermute | solution.py:704
  8.0 1.0 copy-start.8
  9.1 8.8 %copy-start.30 = (f32[128,512]{1,0:T(8,128)S(1)}, f32[128,512]{1,0:T(8,128)}, u32[]{:S(2)}) copy-start(f32[128,512]{1,0:T(8,128)} %param.14) | copy-start | bytes 786436
  9.1 8.9 %copy-start.31 = (f32[512,128]{1,0:T(8,128)S(1)}, f32[512,128]{1,0:T(8,128)}, u32[]{:S(2)}) copy-start(f32[512,128]{1,0:T(8,128)} %param.16) | copy-start | bytes 786436
  9.1 8.9 %copy-start.26 = (f32[128]{0:T(128)S(1)}, f32[128]{0:T(128)}, u32[]{:S(2)}) copy-start(f32[128]{0:T(128)} %param.13) | copy-start | bytes 1540
  10.5 20.2 %copy-start.19 = (f32[9,512]{1,0:T(8,128)S(1)}, f32[9,512]{1,0:T(8,128)}, u32[]{:S(2)}) copy-start(f32[9,512]{1,0:T(8,128)} %dw_ref.3) | copy-start | bytes 55300
  10.5 32.9 %all-to-all-start.1 = ((bf16[32,64,128]{2,1,0:T(8,128)(2,1)}), bf16[32,64,128]{2,1,0:T(8,128)(2,1)S(1)}, u32[]{:S(2)}, u32[]{:S(2)}) async-start(bf16[32,64,128]{2,1,0:T(8,128)(2,1)} %to_columns.1), calls=%async_computation.1 | async-start | bytes 1048576 | tf_op jit(solution)/shard_map/all_to_all | solution.py:706
  22.8 1.4 copy-start.1
  24.2 6.5 %copy-start.13 = (bf16[2048,128]{1,0:T(8,128)(2,1)}, bf16[2048,128]{1,0:T(8,128)(2,1)S(1)}, u32[]{:S(2)}) copy-start(bf16[2048,128]{1,0:T(8,128)(2,1)S(1)} %get-tuple-element.44.n_ref) | copy-start | bytes 1572868
  24.3 5.6 %collective-permute-start.3 = (bf16[2,36,128]{2,1,0:T(8,128)(2,1)S(1)}, bf16[2,36,128]{2,1,0:T(8,128)(2,1)S(1)}, u32[]{:S(2)}, u32[]{:S(2)}) collective-permute-start(bf16[2,36,128]{2,1,0:T(8,128)(2,1)S(1)} %maximum_bitcast_fusion.1), channel_id=1, source_target_pairs={{1,0},{2,1},{3,2},{4,3},{5,4},{6,5},{7,6},{8,7},{9,8},{10,9},{11,1... | collective-permute-start | bytes 55304 | tf_op jit(solution)/shard_map/ppermute | solution.py:716
  25.6 5.1 %collective-permute-start.2 = (bf16[2,36,128]{2,1,0:T(8,128)(2,1)S(1)}, bf16[2,36,128]{2,1,0:T(8,128)(2,1)S(1)}, u32[]{:S(2)}, u32[]{:S(2)}) collective-permute-start(bf16[2,36,128]{2,1,0:T(8,128)(2,1)S(1)} %maximum_bitcast_fusion), channel_id=1, source_target_pairs={{0,1},{1,2},{2,3},{3,4},{4,5},{5,6},{6,7},{7,8},{8,9},{9,10},{10,1... | collective-permute-start | bytes 55304 | tf_op jit(solution)/shard_map/ppermute | solution.py:715
  29.9 30.9 %copy-start.32 = (f32[128,128]{1,0:T(8,128)S(1)}, f32[128,128]{1,0:T(8,128)}, u32[]{:S(2)}) copy-start(f32[128,128]{1,0:T(8,128)} %param.19) | copy-start | bytes 196612
  42.0 0.8 copy-start.10
  42.8 0.6 copy-start.22
  43.4 29.2 %copy-start.27 = (f32[128]{0:T(128)S(1)}, f32[128]{0:T(128)}, u32[]{:S(2)}) copy-start(f32[128]{0:T(128)} %param.17) | copy-start | bytes 1540
  43.4 29.2 %all-to-all-start = ((bf16[32,64,128]{2,1,0:T(8,128)(2,1)}), bf16[32,64,128]{2,1,0:T(8,128)(2,1)}, u32[]{:S(2)}, u32[]{:S(2)}) async-start(bf16[32,64,128]{2,1,0:T(8,128)(2,1)} %copy-done.10), calls=%async_computation | async-start | bytes 1048576 | tf_op jit(solution)/shard_map/all_to_all | solution.py:723
  61.8 33.1 %copy-start.15 = (bf16[128,384]{1,0:T(8,128)(2,1)}, bf16[128,384]{1,0:T(8,128)(2,1)S(1)}, u32[]{:S(2)}) copy-start(bf16[128,384]{1,0:T(8,128)(2,1)S(1)} %convert_element_type.23.wq_ref) | copy-start | bytes 294916
  72.6 0.9 copy-start.21
  94.8 0.9 copy-start.7
  95.7 0.8 copy-start.9
  96.5 0.7 copy-start.17
  97.1 0.6 copy-start.24
  97.8 0.7 copy-start.29
  98.4 16.9 %all-to-all-start.3 = ((bf16[32,80,128]{2,1,0:T(8,128)(2,1)}), bf16[32,80,128]{2,1,0:T(8,128)(2,1)S(1)}, u32[]{:S(2)}, u32[]{:S(2)}) async-start(bf16[32,80,128]{2,1,0:T(8,128)(2,1)} %copy-done.7), calls=%async_computation.3 | async-start | bytes 1310720 | tf_op jit(solution)/shard_map/all_to_all | solution.py:727
  115.4 9.4 %collective-permute-start.4 = (bf16[40,128]{1,0:T(8,128)(2,1)S(1)}, bf16[40,128]{1,0:T(8,128)(2,1)S(1)}, u32[]{:S(2)}, u32[]{:S(2)}) collective-permute-start(bf16[40,128]{1,0:T(8,128)(2,1)S(1)} %get-tuple-element.60), channel_id=1, source_target_pairs={{0,1},{1,2},{2,3},{3,4},{4,5},{5,6},{6,7},{7,8},{8,9},{9,10},{10,1... | collective-permute-start | bytes 30728 | tf_op jit(solution)/shard_map/ppermute | solution.py:728
  116.6 8.1 %collective-permute-start.5 = (bf16[40,128]{1,0:T(8,128)(2,1)S(1)}, bf16[40,128]{1,0:T(8,128)(2,1)S(1)}, u32[]{:S(2)}, u32[]{:S(2)}) collective-permute-start(bf16[40,128]{1,0:T(8,128)(2,1)S(1)} %get-tuple-element.61), channel_id=1, source_target_pairs={{1,0},{2,1},{3,2},{4,3},{5,4},{6,5},{7,6},{8,7},{9,8},{10,9},{11,1... | collective-permute-start | bytes 30728 | tf_op jit(solution)/shard_map/ppermute | solution.py:729
  117.9 6.8 %copy-start.14 = (bf16[2048,128]{1,0:T(8,128)(2,1)S(1)}, bf16[2048,128]{1,0:T(8,128)(2,1)}, u32[]{:S(2)}) copy-start(bf16[2048,128]{1,0:T(8,128)(2,1)} %copy-done.13) | copy-start | bytes 1572868
  117.9 6.8 %copy-start.18 = (f32[384,128]{1,0:T(8,128)S(1)}, f32[384,128]{1,0:T(8,128)}, u32[]{:S(2)}) copy-start(f32[384,128]{1,0:T(8,128)} %copy-done.17) | copy-start | bytes 589828
  118.0 6.8 %copy-start.20 = (f32[9,512]{1,0:T(8,128)S(1)}, f32[9,512]{1,0:T(8,128)}, u32[]{:S(2)}) copy-start(f32[9,512]{1,0:T(8,128)} %dw_ref.3) | copy-start | bytes 55300
  118.0 6.8 %copy-start.23 = (bf16[2,48,512]{2,1,0:T(8,128)(2,1)S(1)}, bf16[2,48,512]{2,1,0:T(8,128)(2,1)}, u32[]{:S(2)}) copy-start(bf16[2,48,512]{2,1,0:T(8,128)(2,1)} %copy-done.22) | copy-start | bytes 294916
  118.0 6.8 %copy-start.25 = (f32[128,128]{1,0:T(8,128)S(1)}, f32[128,128]{1,0:T(8,128)}, u32[]{:S(2)}) copy-start(f32[128,128]{1,0:T(8,128)} %copy-done.24) | copy-start | bytes 196612
  123.9 0.8 copy-start.11
  160.8 16.3 %all-to-all-start.2 = ((bf16[32,64,128]{2,1,0:T(8,128)(2,1)}), bf16[32,64,128]{2,1,0:T(8,128)(2,1)S(1)}, u32[]{:S(2)}, u32[]{:S(2)}) async-start(bf16[32,64,128]{2,1,0:T(8,128)(2,1)} %copy-done.9), calls=%async_computation.2 | async-start | bytes 1048576 | tf_op jit(solution)/shard_map/all_to_all | solution.py:742
  165.3 1.0 copy-start.6
  166.5 0.8 copy-start.3
  177.1 0.8 copy-start.4
  177.9 17.3 %all-to-all-start.5 = ((bf16[128,16,128]{2,1,0:T(8,128)(2,1)}), bf16[128,16,128]{2,1,0:T(8,128)(2,1)S(1)}, u32[]{:S(2)}, u32[]{:S(2)}) async-start(bf16[128,16,128]{2,1,0:T(8,128)(2,1)} %copy-done.3), calls=%async_computation.5 | async-start | bytes 1048576 | tf_op jit(solution)/shard_map/all_to_all | solution.py:751
  181.4 1.0 copy-start.5
  182.5 12.7 %copy-start.16 = (bf16[128,384]{1,0:T(8,128)(2,1)S(1)}, bf16[128,384]{1,0:T(8,128)(2,1)}, u32[]{:S(2)}) copy-start(bf16[128,384]{1,0:T(8,128)(2,1)} %copy-done.15) | copy-start | bytes 294916
  183.9 11.3 %copy-start.28 = (f32[128]{0:T(128)S(1)}, f32[128]{0:T(128)}, u32[]{:S(2)}) copy-start(f32[128]{0:T(128)} %param.17) | copy-start | bytes 1540
  183.9 1.1 copy-start.12

commit v2 on v1

--- a/solution.py
+++ b/solution.py
@@ -21,7 +21,7 @@
 gelu_coef = math.sqrt(2.0 / math.pi)
 bf16 = jnp.bfloat16
 f32 = jnp.float32
-VMEM_LIMIT = 50 * 1024 * 1024
+VMEM_LIMIT = 24 * 1024 * 1024
 
 PLANE = ("rows", "group")
 COLS = ("group", "plane")
@@ -36,6 +36,10 @@
 ROWS_USED = 1616
 PACK_ROWS = 2048
 
+PAIRS = 4
+
+HBM = pl.BlockSpec(memory_space=pltpu.HBM)
+ANY = pl.BlockSpec()
 NT = (((1,), (1,)), ((), ()))
 TN = (((0,), (0,)), ((), ()))
 
@@ -64,6 +68,32 @@
     return inverse, v * inverse
 
 
+def rows_of(i, count):
+    return pl.ds(pl.multiple_of(i * count, count), count)
+
+
+def copies(pairs, sems):
+    return [pltpu.make_async_copy(a, b, sems.at[k]) for k, (a, b) in enumerate(pairs)]
+
+
+class Blocks:
+    def __init__(self, src, dst, sems, count):
+        self.src, self.dst, self.sems, self.count = src, dst, sems, count
+        self.steps = src.shape[0] // count
+
+    def copy(self, i):
+        at = rows_of(i, self.count) if not isinstance(i, int) else pl.ds(i * self.count, self.count)
+        return pltpu.make_async_copy(self.src.at[at], self.dst.at[at], self.sems.at[i])
+
+    def start_all(self):
+        for i in range(self.steps):
+            self.copy(i).start()
+
+    def wait_all(self):
+        for i in range(self.steps):
+            self.copy(i).wait()
+
+
 def lane_group(g):
     return slice(g * LANES, (g + 1) * LANES)
 
@@ -87,7 +117,7 @@
 
 
 def from_columns_kernel(x_ref, o_ref, cols):
-    cols[...] = x_ref[...].reshape(RD * CD, C).astype(f32)
+    cols[...] = x_ref[:, 80:144, :].reshape(RD * CD, C).astype(f32)
     for row in range(RD):
         o_ref[row, :, :] = cols[pl.ds(row, CD, stride=RD), :].astype(bf16)
 
@@ -104,12 +134,14 @@
 
 
 def expand_kernel(x_ref, gain_ref, w_ref, e_ref, s_ref, n_ref):
+    w = w_ref[...].astype(bf16)
+
     def step(i, carry):
         at = pl.ds(pl.multiple_of(i * 256, 256), 256)
         normed = (normalise(x_ref[at, :].astype(f32))[1] * gain_ref[...]).astype(bf16)
         n_ref[at, :] = normed
         for g in range(GROUPS):
-            value, slope = gelu_pair(dot(normed, w_ref[:, lane_group(g)]))
+            value, slope = gelu_pair(dot(normed, w[:, lane_group(g)]))
             e_ref[at, lane_group(g)] = value.astype(bf16)
             s_ref[at, lane_group(g)] = slope.astype(bf16)
         return carry
@@ -119,18 +151,8 @@
 
 def expand(x, gain, w):
     tokens = x.shape[0]
-    block = 512
-    wide = pl.BlockSpec((block, E), lambda i: (i, 0))
-    slim = pl.BlockSpec((block, C), lambda i: (i, 0))
     return pl.pallas_call(
         expand_kernel,
-        grid=(tokens // block,),
-        in_specs=[
-            slim,
-            pl.BlockSpec((1, C), lambda i: (0, 0)),
-            pl.BlockSpec((C, E), lambda i: (0, 0)),
-        ],
-        out_specs=[wide, wide, slim],
         out_shape=[
             jax.ShapeDtypeStruct((tokens, E), bf16),
             jax.ShapeDtypeStruct((tokens, E), bf16),
@@ -158,12 +180,13 @@
 def depth_kernel(
     e_ref,
     x_ref,
+    c_ref,
     halo_ref,
     strip_ref,
     gain_ref,
     w1_ref,
     dw_ref,
-    w2_ref,
+    w2f_ref,
     send_ref,
     d_ref,
     s_ref,
@@ -171,14 +194,17 @@
     ext,
     side,
     mid,
+    w2_ref,
 ):
+    w2_ref[...] = w2f_ref[...].astype(bf16)
+    send_ref[:, 64:128, :] = c_ref[...]
     gain = gain_ref[...]
     halo = normalise(halo_ref[...].reshape(4 * CD, C).astype(f32))[1]
     halo = (halo * gain).astype(bf16)
     strip = normalise(strip_ref[...].reshape(6 * 48, C).astype(f32))[1]
     strip = (strip * gain).astype(bf16)
     for g in range(GROUPS):
-        weight = w1_ref[:, lane_group(g)]
+        weight = w1_ref[:, lane_group(g)].astype(bf16)
         value = gelu_value(dot(halo, weight)).astype(bf16).astype(f32).reshape(4, CD, C)
         for k, row in enumerate((0, 1, RD + 2, RD + 3)):
             ext[g, row, 16 : 16 + CD, :] = value[k]
@@ -189,17 +215,22 @@
             ext[g, row, 15:16, :] = value[1, row : row + 1]
             ext[g, row, 16 + CD : 17 + CD, :] = value[4, row : row + 1]
 
-    def fill(row, carry):
-        for g in range(GROUPS):
-            ext[g, row + 2, 16 : 16 + CD, :] = e_ref[row, :, lane_group(g)].astype(f32)
-        return carry
-
-    lax.fori_loop(0, RD, fill, 0)
+    def fill(i):
+        for k in range(4):
+            row = i * 4 + k
+            for g in range(GROUPS):
+                ext[g, row + 2, 16 : 16 + CD, :] = e_ref[row, :, lane_group(g)].astype(f32)
 
     def taps_of(g):
         return [dw_ref[t : t + 1, lane_group(g)] for t in range(9)]
 
+    fill(0)
+
     def block(i, carry):
+        @pl.when(i < RD // 4 - 1)
+        def _():
+            fill(i + 1)
+
         for k in range(4):
             row = i * 4 + k
             at = pl.ds(pl.multiple_of(row * CD, CD), CD)
@@ -213,6 +244,9 @@
         return carry
 
     lax.fori_loop(0, RD // 4, block, 0)
+    for col in range(CD):
+        part = mid[pl.ds(col, RD, stride=CD), :]
+        send_ref[col // 2, (col % 2) * RD : (col % 2 + 1) * RD, :] = part.astype(bf16)
     for g in range(GROUPS):
         taps = taps_of(g)
         for row in (0, RD + 1):
@@ -225,17 +259,14 @@
                     term = taps[3 * a + b] * side[g, 3 * end + b, a : a + 48, :]
                     total = term if total is None else total + term
             ss_ref[end, :, lane_group(g)] = gelu_pair(total)[1].astype(bf16)
-    for col in range(CD):
-        part = mid[pl.ds(col, RD, stride=CD), :]
-        send_ref[col // 2, (col % 2) * RD : (col % 2 + 1) * RD, :] = part.astype(bf16)
-
-
-def depth(expanded, x, halo, strip, gain, w1, taps, w2):
+
+
+def depth(expanded, x, cot, halo, strip, gain, w1, taps, w2):
     tokens = RD * CD
     return pl.pallas_call(
         depth_kernel,
         out_shape=[
-            jax.ShapeDtypeStruct((CD // 2, 2 * RD, C), bf16),
+            jax.ShapeDtypeStruct((CD // 2, 4 * RD, C), bf16),
             jax.ShapeDtypeStruct((tokens, E), bf16),
             jax.ShapeDtypeStruct((tokens + 2 * CD, E), bf16),
             jax.ShapeDtypeStruct((2, 48, E), bf16),
@@ -244,6 +275,7 @@
             pltpu.VMEM((GROUPS, RD + 4, 96, LANES), f32),
             pltpu.VMEM((GROUPS, 6, 56, LANES), f32),
             pltpu.VMEM((tokens, C), f32),
+            pltpu.VMEM((E, C), bf16),
         ],
         compiler_params=pltpu.CompilerParams(vmem_limit_bytes=VMEM_LIMIT),
         cost_estimate=pl.CostEstimate(
@@ -252,7 +284,7 @@
             transcendentals=tokens * E,
         ),
         name="depth",
-    )(expanded.reshape(RD, CD, E), x, halo, strip, gain, w1, taps, w2)
+    )(expanded.reshape(RD, CD, E), x, cot, halo, strip, gain, w1, taps, w2)
 
 
 def side_by_side(x):
@@ -268,17 +300,15 @@
 
 
 def attend_kernel(
-    m_ref,
-    c_ref,
+    x_ref,
     gain_ref,
-    wq_ref,
-    wo_ref,
+    wqf_ref,
+    wof_ref,
     bias_ref,
-    bo_ref,
-    gm_ref,
+    back_ref,
     gq_ref,
     go_ref,
-    ds_ref,
+    gb_ref,
     mid,
     cot,
     out,
@@ -287,11 +317,16 @@
     atts,
     cots,
     mixes,
+    ds_ref,
+    wq_ref,
+    wo_ref,
 ):
-    mid[...] = m_ref[...].reshape(RD * CD, C).astype(f32)
-    cot[...] = c_ref[...].reshape(RD * CD, C).astype(f32)
     grad[...] = jnp.zeros(grad.shape, f32)
     ds_ref[...] = jnp.zeros(ds_ref.shape, f32)
+    wq_ref[...] = wqf_ref[...].astype(bf16)
+    wo_ref[...] = wof_ref[...].astype(bf16)
+    mid[...] = x_ref[:, 0:64, :].reshape(RD * CD, C).astype(f32)
+    cot[...] = x_ref[:, 64:128, :].reshape(RD * CD, C).astype(f32)
     gain = gain_ref[...]
     scale = 32**-0.5
     row_head = lax.broadcasted_iota(jnp.int32, (256, 256), 0) // 64
@@ -331,70 +366,104 @@
                 k = 2 * c + il
                 dst[at, :] = x[k * 32 : (k + 1) * 32]
 
-    def pair(r0, carry):
-        at = pl.ds(pl.multiple_of(r0 * 128, 128), 128)
-        m = windows(mid, r0, 64, 0)
-        ct = windows(cot, r0, 64, 0)
-        ctb = ct.astype(bf16)
-        inverse, unit = normalise(m)
-        normed = (unit * gain).astype(bf16)
-        mixture = dot(normed, wq_ref[...])
-        q = (mixture[:, :C] * scale).astype(bf16)
-        k = mixture[:, C : 2 * C].astype(bf16)
-        v = mixture[:, 2 * C :].astype(bf16)
-        ga = dot(ctb, wo_ref[...], NT).astype(bf16)
-        k4 = per_head(k)
-        v4 = per_head(v)
-        qd = per_window(q)
-        gd = per_window(ga)
-        scores = (dot(k4, qd, NT) + bias_ref[...]).reshape(HEADS, 64, 128)
-        weights = jnp.exp(scores - jnp.max(scores, axis=1, keepdims=True))
-        prob = weights * (1.0 / jnp.sum(weights, axis=1, keepdims=True))
-        rounded = prob.reshape(256, 128).astype(bf16)
-        att = diagonal(dot(rounded, v4, TN)).astype(bf16)
-        gp = dot(v4, gd, NT).reshape(HEADS, 64, 128)
-        gs = prob * (gp - jnp.sum(prob * gp, axis=1, keepdims=True))
-        gs = gs.reshape(256, 128)
-        ds_ref[...] += gs
-        gr = gs.astype(bf16)
-        gv = fold(dot(rounded, gd))
-        gk = fold(dot(gr, qd))
-        gq = diagonal(dot(gr, k4, TN)) * scale
-        gx = jnp.concatenate([gq, gk, gv], axis=1).astype(bf16)
-        gn = dot(gx, wq_ref[...], NT).astype(bf16).astype(f32)
-        scaled = gn * gain
-        gm = ct + inverse * (scaled - unit * jnp.mean(scaled * unit, axis=-1, keepdims=True))
-        put(grad, r0, 80, 1, gm)
-        put(out, r0, 64, 0, m + dot(att, wo_ref[...]))
-        norms[at, :] = normed
-        atts[at, :] = att
-        cots[at, :] = ctb
-        mixes[at, :] = gx
+    def pairs(i, carry):
+        each = range(PAIRS)
+        r0s = [i * PAIRS + p for p in each]
+        ms = [windows(mid, r0, 64, 0) for r0 in r0s]
+        cts = [windows(cot, r0, 64, 0) for r0 in r0s]
+        ctbs = [ct.astype(bf16) for ct in cts]
+        scales = [normalise(m) for m in ms]
+        normed = [(unit * gain).astype(bf16) for _, unit in scales]
+        mixture = [dot(n, wq_ref[...]) for n in normed]
+        ga = [dot(ct, wo_ref[...], NT).astype(bf16) for ct in ctbs]
+        qd = [per_window((x[:, :C] * scale).astype(bf16)) for x in mixture]
+        k4 = [per_head(x[:, C : 2 * C].astype(bf16)) for x in mixture]
+        v4 = [per_head(x[:, 2 * C :].astype(bf16)) for x in mixture]
+        gd = [per_window(x) for x in ga]
+        scores = [dot(k4[p], qd[p], NT) for p in each]
+        gp = [dot(v4[p], gd[p], NT).reshape(HEADS, 64, 128) for p in each]
+        scores = [(x + bias_ref[...]).reshape(HEADS, 64, 128) for x in scores]
+        weights = [jnp.exp(x - jnp.max(x, axis=1, keepdims=True)) for x in scores]
+        prob = [x * (1.0 / jnp.sum(x, axis=1, keepdims=True)) for x in weights]
+        rounded = [x.reshape(256, 128).astype(bf16) for x in prob]
+        att = [diagonal(dot(rounded[p], v4[p], TN)).astype(bf16) for p in each]
+        gv = [fold(dot(rounded[p], gd[p])) for p in each]
+        gs = [
+            prob[p] * (gp[p] - jnp.sum(prob[p] * gp[p], axis=1, keepdims=True)) for p in each
+        ]
+        gs = [x.reshape(256, 128) for x in gs]
+        total = gs[0]
+        for x in gs[1:]:
+            total = total + x
+        ds_ref[...] += total
+        gr = [x.astype(bf16) for x in gs]
+        gk = [fold(dot(gr[p], qd[p])) for p in each]
+        gq = [diagonal(dot(gr[p], k4[p], TN)) * scale for p in each]
+        gx = [jnp.concatenate([gq[p], gk[p], gv[p]], axis=1).astype(bf16) for p in each]
+        gn = [dot(x, wq_ref[...], NT).astype(bf16).astype(f32) for x in gx]
+        mixed = [dot(x, wo_ref[...]) for x in att]
+        for p in each:
+            at = pl.ds(pl.multiple_of(r0s[p] * 128, 128), 128)
+            inverse, unit = scales[p]
+            scaled = gn[p] * gain
+            mean = jnp.mean(scaled * unit, axis=-1, keepdims=True)
+            put(grad, r0s[p], 80, 1, cts[p] + inverse * (scaled - unit * mean))
+            put(out, r0s[p], 64, 0, ms[p] + mixed[p])
+            norms[at, :] = normed[p]
+            atts[at, :] = att[p]
+            cots[at, :] = ctbs[p]
+            mixes[at, :] = gx[p]
         return carry
 
-    lax.fori_loop(0, 16, pair, 0)
-    for k in range(3):
-        gq_ref[k * C : (k + 1) * C, :] = dot(norms[...], mixes[:, k * C : (k + 1) * C], TN)
-    go_ref[...] = dot(atts[...], cots[...], TN)
+    lax.fori_loop(0, 16 // PAIRS, pairs, 0)
     for c in range(2):
         low = grad[pl.ds(c * 40 + 32, 24, stride=80), :]
         high = grad[pl.ds(c * 40 + 1 + 8 * 80, 24, stride=80), :]
         grad[pl.ds(c * 40 + 8 * 80, 24, stride=80), :] = low
         grad[pl.ds(c * 40 + 33, 24, stride=80), :] = high
-    bo_ref[...] = out[...].astype(bf16).reshape(bo_ref.shape)
-    gm_ref[...] = grad[...].astype(bf16).reshape(gm_ref.shape)
-
-
-def attend(mid, cot, gain, wq, wo, bias):
+    back_ref[:, 0:80, :] = grad[...].astype(bf16).reshape(32, 80, C)
+    back_ref[:, 80:144, :] = out[...].astype(bf16).reshape(32, 64, C)
+    gb_ref[...] = table_sums(ds_ref)
+    for k in range(3):
+        gq_ref[k * C : (k + 1) * C, :] = dot(norms[...], mixes[:, k * C : (k + 1) * C], TN)
+    go_ref[...] = dot(atts[...], cots[...], TN)
+
+
+def table_sums(ds_ref):
+    at = lax.broadcasted_iota(jnp.int32, (128, 128), 0) % 64
+    lane = lax.broadcasted_iota(jnp.int32, (128, 128), 1)
+    same_row = 2 * (at % 32 // 8) + at // 32 == lane // 16
+    total = jnp.zeros((32, 128), f32)
+    for col in range(8):
+        place = same_row & (at % 8 - col + 7 == lane % 16)
+        place = jnp.where(place, 1.0, 0.0).astype(bf16)
+        part = ds_ref[pl.ds(col, 32, stride=8), :]
+        high = part.astype(bf16)
+        rest = part - high.astype(f32)
+        total = total + dot(high, place) + dot(rest.astype(bf16), place)
+    rows = []
+    for h in range(HEADS):
+        row_sum = None
+        for k in range(8):
+            shift = 16 * (7 - (2 * (k % 4) + k // 4))
+            part = total[8 * h + k : 8 * h + k + 1]
+            none = jnp.zeros((1, 128), f32)
+            part = jnp.concatenate([part, none], axis=1)
+            part = pltpu.roll(part, shift, 1) if shift else part
+            row_sum = part if row_sum is None else row_sum + part
+        rows.append(row_sum)
+    return jnp.concatenate(rows + [jnp.zeros((4, 256), f32)], axis=0)
+
+
+def attend(x, gain, wq, wo, bias):
     tokens = RD * CD
     return pl.pallas_call(
         attend_kernel,
         out_shape=[
-            jax.ShapeDtypeStruct((32, 64, C), bf16),
-            jax.ShapeDtypeStruct((32, 80, C), bf16),
+            jax.ShapeDtypeStruct((32, 144, C), bf16),
             jax.ShapeDtypeStruct((3 * C, C), f32),
             jax.ShapeDtypeStruct((C, C), f32),
-            jax.ShapeDtypeStruct((256, 128), f32),
+            jax.ShapeDtypeStruct((8, 256), f32),
         ],
         scratch_shapes=[
             pltpu.VMEM((tokens, C), f32),
@@ -405,18 +474,22 @@
             pltpu.VMEM((tokens, C), bf16),
             pltpu.VMEM((tokens, C), bf16),
             pltpu.VMEM((tokens, 3 * C), bf16),
+            pltpu.VMEM((256, 128), f32),
+            pltpu.VMEM((C, 3 * C), bf16),
+            pltpu.VMEM((C, C), bf16),
         ],
         compiler_params=pltpu.CompilerParams(vmem_limit_bytes=VMEM_LIMIT),
         cost_estimate=pl.CostEstimate(
             flops=40 * tokens * C * C, bytes_accessed=tokens * 8 * C, transcendentals=tokens * 256
         ),
         name="attend",
-    )(mid, cot, gain, wq, wo, bias)
+    )(x, gain, wq, wo, bias)
 
 
 def project_grad_kernel(g_ref, w2_ref, d_ref, s_ref, b_ref, gp_ref, gm_ref, cols):
-    cols[...] = g_ref[...].reshape(CD * 40, C).astype(f32)
     gp_ref[...] = jnp.zeros(gp_ref.shape, f32)
+    w2 = w2_ref[...].astype(bf16)
+    cols[...] = g_ref[:, 0:80, :].reshape(CD * 40, C).astype(f32)
 
     def rows(first, count):
         parts = [cols[pl.ds(first + k, CD, stride=40), :] for k in range(count)]
@@ -424,12 +497,18 @@
 
     def before(g, at):
         for k in range(GROUPS):
-            wide = dot(g, w2_ref[lane_group(k), :], NT)
+            wide = dot(g, w2[lane_group(k)], NT)
             wide = wide * s_ref[at, lane_group(k)].astype(f32)
             b_ref[at, lane_group(k)] = wide.astype(bf16)
 
+    def edge(row):
+        before(rows(row, 1), pl.ds(row * CD, CD))
+
+    edge(0)
+    edge(RD + 1)
+
     def block(i, carry):
-        four = pl.ds(pl.multiple_of(i * 4 * CD, 4 * CD), 4 * CD)
+        four = rows_of(i, 4 * CD)
         ring = pl.ds(pl.multiple_of(i * 4 * CD + CD, CD), 4 * CD)
         g = rows(i * 4 + 1, 4)
         gm_ref[four, :] = g
@@ -439,16 +518,15 @@
         return carry
 
     lax.fori_loop(0, RD // 4, block, 0)
-    for row in (0, RD + 1):
-        before(rows(row, 1), pl.ds(row * CD, CD))
 
 
 def project_grad(gm, w2, depthed, slope):
     tokens = RD * CD
+    ring = tokens + 2 * CD
     return pl.pallas_call(
         project_grad_kernel,
         out_shape=[
-            jax.ShapeDtypeStruct((tokens + 2 * CD, E), bf16),
+            jax.ShapeDtypeStruct((ring, E), bf16),
             jax.ShapeDtypeStruct((E, C), f32),
             jax.ShapeDtypeStruct((tokens, C), bf16),
         ],
@@ -480,24 +558,27 @@
     sums,
     total,
 ):
+    w2 = w2_ref[...].astype(bf16)
     strip = strip_ref[...].reshape(2 * 48, C)
     for g in range(GROUPS):
-        wide = dot(strip, w2_ref[lane_group(g), :], NT).reshape(2, 48, LANES)
+        wide = dot(strip, w2[lane_group(g)], NT).reshape(2, 48, LANES)
         wide = (wide * ss_ref[:, :, lane_group(g)].astype(f32)).astype(bf16).astype(f32)
         for row in range(RD + 2):
             ext[g, row, 15:16, :] = wide[0, row : row + 1]
             ext[g, row, 16 + CD : 17 + CD, :] = wide[1, row : row + 1]
 
-    def fill(row, carry):
-        for g in range(GROUPS):
-            ext[g, row, 16 : 16 + CD, :] = b_ref[row, :, lane_group(g)].astype(f32)
-        return carry
-
-    lax.fori_loop(0, RD + 2, fill, 0)
+    def fill(first, count):
+        for k in range(count):
+            for g in range(GROUPS):
+                part = b_ref[first + k, :, lane_group(g)]
+                ext[g, first + k, 16 : 16 + CD, :] = part.astype(f32)
+
+    fill(0, 2)
     sums[...] = jnp.zeros(sums.shape, f32)
     total[...] = jnp.zeros(total.shape, f32)
 
     def block(i, carry):
+        fill(i * 4 + 2, 4)
         for k in range(4):
             row = i * 4 + k
             at = pl.ds(pl.multiple_of(row * CD, CD), CD)
@@ -526,7 +607,8 @@
         kernel_sums = jnp.sum(sums[g], axis=1)
         kernel_sums = jnp.concatenate([kernel_sums, jnp.zeros((7, LANES), f32)], axis=0)
         pack_ref[ROW_KERNEL + 16 * g : ROW_KERNEL + 16 * g + 16, :] = kernel_sums.astype(bf16)
-    pack_ref[ROW_BIAS : ROW_BIAS + 16, :] = gb_ref[...].astype(bf16)
+    table = jnp.concatenate([gb_ref[:, :LANES], gb_ref[:, LANES:]], axis=0)
+    pack_ref[ROW_BIAS : ROW_BIAS + 16, :] = table.astype(bf16)
     pack_ref[ROWS_USED:PACK_ROWS, :] = jnp.zeros((PACK_ROWS - ROWS_USED, C), bf16)
 
 
@@ -556,9 +638,11 @@
 
 
 def image_grad_kernel(g_ref, w_ref, gain_ref, x_ref, m_ref, o_ref):
+    w = w_ref[...].astype(bf16)
+
     def step(i, carry):
         at = pl.ds(pl.multiple_of(i * 256, 256), 256)
-        scaled = dot(g_ref[at, :], w_ref[...], NT) * gain_ref[...]
+        scaled = dot(g_ref[at, :], w, NT) * gain_ref[...]
         inverse, unit = normalise(x_ref[at, :].astype(f32))
         mean = jnp.mean(scaled * unit, axis=-1, keepdims=True)
         o_ref[at, :] = (m_ref[at, :].astype(f32) + inverse * (scaled - unit * mean)).astype(bf16)
@@ -569,19 +653,8 @@
 
 def image_grad(g, w, gain, x, gm):
     tokens = x.shape[0]
-    block = 1024
-    slim = pl.BlockSpec((block, C), lambda i: (i, 0))
     return pl.pallas_call(
         image_grad_kernel,
-        grid=(tokens // block,),
-        in_specs=[
-            pl.BlockSpec((block, E), lambda i: (i, 0)),
-            pl.BlockSpec((C, E), lambda i: (0, 0)),
-            pl.BlockSpec((1, C), lambda i: (0, 0)),
-            slim,
-            slim,
-        ],
-        out_specs=slim,
         out_shape=jax.ShapeDtypeStruct((tokens, C), bf16),
         compiler_params=pltpu.CompilerParams(vmem_limit_bytes=VMEM_LIMIT),
         cost_estimate=pl.CostEstimate(
@@ -591,19 +664,37 @@
     )(g, w, gain, x, gm)
 
 
-def sum_parts_kernel(factor, x_ref, o_ref):
-    total = x_ref[0].astype(f32)
-    for k in range(1, x_ref.shape[0]):
-        total = total + x_ref[k].astype(f32)
+def sum_parts_kernel(factor, x_hbm, o_hbm, x_ref, o_ref, xs, outs):
+    x_in = Blocks(x_hbm, x_ref, xs, 32)
+    x_in.start_all()
+    total = jnp.zeros(x_ref.shape[1:], f32)
+    for i in range(4):
+        x_in.copy(i).wait()
+        for k in range(32):
+            total = total + x_ref[32 * i + k].astype(f32)
     total = (total * factor).astype(bf16)
-    for k in range(x_ref.shape[0]):
+    for k in range(16):
         o_ref[k] = total
+    spread = [(o_ref, o_hbm.at[pl.ds(16 * k, 16)]) for k in range(8)]
+    spread = copies(spread, outs)
+    for copy in spread:
+        copy.start()
+    for copy in spread:
+        copy.wait()
 
 
 def sum_parts(x, factor):
     return pl.pallas_call(
-        lambda x_ref, o_ref: sum_parts_kernel(factor, x_ref, o_ref),
+        lambda *refs: sum_parts_kernel(factor, *refs),
         out_shape=jax.ShapeDtypeStruct(x.shape, bf16),
+        in_specs=[HBM],
+        out_specs=HBM,
+        scratch_shapes=[
+            pltpu.VMEM(x.shape, bf16),
+            pltpu.VMEM((16,) + x.shape[1:], bf16),
+            pltpu.SemaphoreType.DMA((4,)),
+            pltpu.SemaphoreType.DMA((8,)),
+        ],
         compiler_params=pltpu.CompilerParams(vmem_limit_bytes=VMEM_LIMIT),
         cost_estimate=pl.CostEstimate(
             flops=2 * x.size, bytes_accessed=4 * x.size, transcendentals=0
@@ -626,7 +717,7 @@
     for g in range(GROUPS):
         part = p_ref[ROW_EXPAND + g * C : ROW_EXPAND + (g + 1) * C, :].astype(f32)
         ex_ref[:, lane_group(g)] = part
-        first = first + part * w1_ref[:, lane_group(g)].astype(f32)
+        first = first + part * w1_ref[:, lane_group(g)].astype(bf16).astype(f32)
         part = p_ref[ROW_PROJECT + g * C : ROW_PROJECT + (g + 1) * C, :].astype(f32)
         pr_ref[g * C : (g + 1) * C, :] = part.T
         part = p_ref[ROW_KERNEL + g * 16 : ROW_KERNEL + (g + 1) * 16, :].astype(f32)
@@ -634,12 +725,13 @@
     for k in range(3):
         part = p_ref[ROW_QKV + k * C : ROW_QKV + (k + 1) * C, :].astype(f32)
         qk_ref[:, lane_group(k)] = part
-        second = second + part * wq_ref[:, lane_group(k)].astype(f32)
+        second = second + part * wq_ref[:, lane_group(k)].astype(bf16).astype(f32)
     g1_ref[...] = column_sums(first) / gain1_ref[...]
     g2_ref[...] = column_sums(second) / gain2_ref[...]
     o_ref[...] = p_ref[ROW_OUT : ROW_OUT + C, :].astype(f32)
     part = p_ref[ROW_BIAS : ROW_BIAS + 16, :].astype(f32)
-    b_ref[...] = jnp.concatenate([part[0:4], part[4:8]], axis=1)[:, :225]
+    table = jnp.concatenate([part[0:4], part[8:12]], axis=1)
+    b_ref[...] = jnp.concatenate([table[:, 16 * k : 16 * k + 15] for k in range(15)], axis=1)
 
 
 def unpack(pack, w1, wq, gain1, gain2):
@@ -671,6 +763,16 @@
     index = 15 * (row[first] - row[second] + 7) + col[first] - col[second] + 7
     index = jnp.asarray(np.concatenate([index, index], axis=1), jnp.int32)
     return (index[:, :, None] == jnp.arange(225, dtype=jnp.int32)).astype(f32)
+
+
+def swap_ends(low, high, axis):
+    count = lax.axis_size(axis)
+    odd = lax.axis_index(axis) % 2 == 1
+    pairs = [(i, i ^ 1) for i in range(count)]
+    others = [(i, ((i - 1) ^ 1) + 1) for i in range(1, count - 1)]
+    first = lax.ppermute(jnp.where(odd, low, high), axis, pairs)
+    second = lax.ppermute(jnp.where(odd, high, low), axis, others)
+    return jnp.where(odd, first, second), jnp.where(odd, second, first)
 
 
 def per_device(
@@ -686,68 +788,44 @@
     bias_table,
 ):
     factor = 1.0 / math.sqrt(RD * CD * 128)
-    w1 = w_expand.astype(bf16)
-    w2 = w_project.astype(bf16)
-    wq = w_qkv.astype(bf16)
-    wo = w_out.astype(bf16)
+    w1, w2, wq, wo = w_expand, w_project, w_qkv, w_out
     gain1 = norm1_gain.reshape(1, C)
     gain2 = norm2_gain.reshape(1, C)
     onehot = pair_onehot()
     bias = jnp.einsum("hq,jlq->hjl", bias_table, onehot, precision=lax.Precision.HIGHEST)
     bias = bias.reshape(HEADS * 64, 128)
 
-    row_up = [(i, i + 1) for i in range(3)]
-    row_down = [(i + 1, i) for i in range(3)]
-    col_up = [(i, i + 1) for i in range(31)]
-    col_down = [(i + 1, i) for i in range(31)]
-
-    above = lax.ppermute(image[RD - 2 :], "rows", row_up)
-    below = lax.ppermute(image[:2], "rows", row_down)
-    cot_windows = lax.all_to_all(to_columns(cotangent), PLANE, 0, 0, tiled=True)
     tokens = image.reshape(RD * CD, C)
-    expanded, slope1, normed1 = expand(tokens, gain1, w1)
-
-    halo = jnp.concatenate([above, below], axis=0)
+    above, below = swap_ends(tokens[: 2 * CD], tokens[(RD - 2) * CD :], "rows")
+    above = above.reshape(2, CD, C)
+    below = below.reshape(2, CD, C)
     left = jnp.concatenate([above[:, :2], image[:, :2], below[:, :2]], axis=0)
     right = jnp.concatenate([above[:, -2:], image[:, -2:], below[:, -2:]], axis=0)
     left = left.transpose(1, 0, 2)
     right = right.transpose(1, 0, 2)
-    before_left = lax.ppermute(right, COLS, col_up)
-    after_right = lax.ppermute(left, COLS, col_down)
+    before_left, after_right = swap_ends(left, right, COLS)
+    expanded, slope1, normed1 = expand(tokens, gain1, w1)
+    halo = jnp.concatenate([above, below], axis=0)
     strip = jnp.concatenate([before_left, left[:1], right[1:], after_right], axis=0)
     strip = jnp.pad(strip, ((0, 0), (0, 12), (0, 0)))
     send, depthed, slope2, slope2_strip = depth(
-        expanded, tokens, halo, strip, gain1, w1, dw_kernel, w2
+        expanded, tokens, to_columns(cotangent), halo, strip, gain1, w1, dw_kernel, w2
     )
-
-    mid_windows = lax.all_to_all(send, PLANE, 0, 0, tiled=True)
-    out_windows, grad_windows, grad_qkv, grad_out, score_sums = attend(
-        mid_windows, cot_windows, gain2, wq, wo, bias
-    )
-    grad_cols = lax.all_to_all(grad_windows, PLANE, 0, 0, tiled=True)
-    grad_left = lax.ppermute(grad_cols[31, 40:], COLS, col_up)
-    grad_right = lax.ppermute(grad_cols[0, :40], COLS, col_down)
-    before, grad_project, grad_middle = project_grad(grad_cols, w2, depthed, slope2)
+    send, bias = lax.optimization_barrier((send, bias))
+    windows = lax.all_to_all(send, PLANE, 0, 0, tiled=True)
+    back, grad_qkv, grad_out, grad_bias = attend(windows, gain2, wq, wo, bias)
+    back = lax.all_to_all(back, PLANE, 0, 0, tiled=True)
+    grad_left, grad_right = swap_ends(back[0, :40], back[31, 40:80], COLS)
+    before, grad_project, grad_middle = project_grad(back, w2, depthed, slope2)
     grad_strip = jnp.pad(jnp.stack([grad_left, grad_right]), ((0, 0), (0, 8), (0, 0)))
-
-    grad_bias = jnp.einsum(
-        "hjl,jlq->hq",
-        score_sums.reshape(HEADS, 64, 128),
-        onehot,
-        precision=lax.Precision.HIGHEST,
-    )
-    grad_bias = jnp.pad(grad_bias, ((0, 0), (0, 31)))
-    grad_bias = jnp.concatenate([grad_bias[:, :128], grad_bias[:, 128:]], axis=0)
-    grad_bias = jnp.pad(grad_bias, ((0, 8), (0, 0)))
-    block_cols = lax.all_to_all(out_windows, PLANE, 0, 0, tiled=True)
-
     grad_wide, pack = depth_grad(
         before, grad_strip, slope2_strip, w2, dw_kernel, expanded, slope1, normed1,
         grad_project, grad_qkv, grad_out, grad_bias,
     )
     parts = lax.all_to_all(pack.reshape(128, 16, C), ALL, 0, 0, tiled=True)
     grad_image = image_grad(grad_wide, w1, gain1, tokens, grad_middle)
-    block_out = from_columns(block_cols)
+    parts, grad_image = lax.optimization_barrier((parts, grad_image))
+    block_out = from_columns(back)
     whole = lax.all_to_all(sum_parts(parts, factor), ALL, 0, 0, tiled=True)
     g1, ge, gk, gp, g2, gq, go, gb = unpack(whole.reshape(PACK_ROWS, C), w1, wq, gain1, gain2)
     return (

time: 197 us -> 154 us (0.78)
  blocking collectives: 25 us -> 55.1 us
  starting transfers between devices: 51 us -> 24.8 us
  Pallas kernels: 61.5 us -> 41.1 us
  waiting for transfers between devices: 33.1 us -> 21.9 us
  local copies, waits for them, and re-layouts: 15.6 us -> 4.78 us
  matrix products: 7.68 us -> 3.25 us
    all_to_all x1 -> x2, blocking collectives: 25 us -> 55.1 us  [the longest x1 32.7 us: per_device(): windows = lax.all_to_all(send, PLANE, 0, 0, tiled=True)]
    all_to_all x4 -> x1, starting transfers between devices: 33 us -> 12.6 us  [per_device(): parts = lax.all_to_all(pack.reshape(128, 16, C), ALL, 0, 0, tiled=True)]
    pallas_call x6, Pallas kernels: 46.7 us -> 30 us  [the longest x1 9.8 us: attend(): pl.pallas_call(attend_kernel, out_shape=[jax.ShapeDtypeStruct((32, 144, C...]
    all_to_all x4 -> x1, waiting for transfers between devices: 25.3 us -> 8.87 us  [per_device(): parts = lax.all_to_all(pack.reshape(128, 16, C), ALL, 0, 0, tiled=True)]
    unnamed x70 -> x32, local copies, waits for them, and re-layouts: 14 us -> 3.81 us
    ppermute x6, starting transfers between devices: 14.5 us -> 7.88 us  [the longest x3 5.99 us: swap_ends(): second = lax.ppermute(jnp.where(odd, high, low), axis, others)]
    all_to_all x1, waiting for transfers between devices: 7.04 us -> 12.5 us  [per_device(): whole = lax.all_to_all(sum_parts(parts, factor), ALL, 0, 0, tiled=True)]
    dot_general x1 -> x0, matrix products: 4.41 us -> none  [per_device(): jnp.einsum('hjl,jlq->hq', score_sums.reshape(HEADS, 64, 128), onehot, pre...]
  transfers between devices with their start and end apart: 11 -> 8, of which waited for: 5 -> 3; matrix products, arithmetic and copies ran while one was open for 5% -> 3% of each run, Pallas kernels for 14% -> 8%
where the time goes in v2:
time: 154 us; the launch traced here: 153 us
  blocking collectives  55.1 us (36%)
  Pallas kernels  41.1 us (27%)
  starting transfers between devices  24.8 us (16%)
  waiting for transfers between devices  21.9 us (14%)
  local copies, waits for them, and re-layouts  4.78 us (3%)
  matrix products  3.25 us (2%)
    all_to_all x1, blocking collectives, per_device(): windows = lax.all_to_all(send, PLANE, 0, 0, tiled=True)  32.7 us
    all_to_all x1, blocking collectives, per_device(): back = lax.all_to_all(back, PLANE, 0, 0, tiled=True)  22.4 us
    all_to_all x1, starting transfers between devices, per_device(): parts = lax.all_to_all(pack.reshape(128, 16, C), ALL, 0, 0, tiled=True)  12.6 us
    all_to_all x1, waiting for transfers between devices, per_device(): whole = lax.all_to_all(sum_parts(parts, factor), ALL, 0, 0, tiled=True)  12.5 us
    pallas_call x1, Pallas kernels, attend(): pl.pallas_call(attend_kernel, out_shape=[jax.ShapeDtypeStruct((32, 144, C...  9.8 us
    all_to_all x1, waiting for transfers between devices, per_device(): parts = lax.all_to_all(pack.reshape(128, 16, C), ALL, 0, 0, tiled=True)  8.87 us
    pallas_call x1, Pallas kernels, depth(): pl.pallas_call(depth_kernel, out_shape=[jax.ShapeDtypeStruct((CD // 2, 4...  8.32 us
    pallas_call x1, Pallas kernels, depth_grad(): pl.pallas_call(depth_grad_kernel, out_shape=[jax.ShapeDtypeStruct((tokens...  8.04 us
  transfers between devices with their start and end apart: 8, of which 3 were waited for; matrix products, arithmetic and copies ran while one was open for 3% of the time, Pallas kernels for 8%

profile of v2, /device:TPU:1, one launch (start us, length us, event | category | flops | bytes accessed | tf_op | source)
XLA Modules:
  0.0 153.1 jit_solution(9910485713624413971)
XLA Ops:
  0.6 0.0 copy-start
  0.7 0.0 copy-start.1
  0.7 0.0 copy-start.6
  0.7 0.0 copy-start.3
  0.7 0.0 copy-start.10
  0.7 0.9 broadcast_select_fusion.1
  1.6 4.5 %collective-permute-start.1 = (bf16[128,128]{1,0:T(8,128)(2,1)S(1)}, bf16[128,128]{1,0:T(8,128)(2,1)S(1)}, u32[]{:S(2)}, u32[]{:S(2)}) collective-permute-start(bf16[128,128]{1,0:T(8,128)(2,1)S(1)} %bitcast.60), channel_id=1, source_target_pairs={{32,64},{64,32},{33,65},{65,33},{34,66},{66,34},{35,67},{67,35},{3... | collective-permute-start | bytes 98312 | tf_op jit(solution)/shard_map/ppermute | solution.py:774
  6.1 0.1 collective-permute-start
  6.2 0.0 copy-done
  6.2 3.2 %fusion.2 = f32[4,64,128]{2,0,1:T(4,128)S(1)} fusion(s32[64,128]{1,0:T(8,128)} %constant.40.clone, f32[4,225]{1,0:T(4,128)S(1)} %copy-done), kind=kOutput, calls=%fused_computation.3 | convolution fusion | flops 90316800 | bytes 167440 | tf_op jit(solution)/shard_map/hq,jlq->hjl/dot_general | solution.py:795
  9.5 0.0 copy-start.2
  9.5 0.0 copy-start.9
  9.5 0.9 fusion.14
  10.5 0.0 copy-done.6
  10.5 0.6 to_columns.1.c_ref
  11.1 0.0 copy-done.1
  11.1 0.0 copy-done.3
  11.1 0.0 copy-done.10
  11.1 4.0 %expand.1 = (bf16[2048,512]{1,0:T(8,128)(2,1)S(1)}, bf16[2048,512]{1,0:T(8,128)(2,1)S(1)}, bf16[2048,128]{1,0:T(8,128)(2,1)S(1)}) custom-call(bf16[2048,128]{1,0:T(8,128)(2,1)S(1)} %bitcast.41, f32[1,128]{1,0:T(1,128)S(1)} %bitcast.48, f32[128,512]{1,0:T(8,128)S(1)} %copy-done.3), custom_call_target="tpu_custom_call" | custom-call | flops 289406976 | bytes 5242880 | tf_op jit(solution)/shard_map/expand/pallas_call | solution.py:154
  15.2 0.0 collective-permute-done.1
  15.2 0.0 collective-permute-done
  15.4 1.7 %collective-permute-start.2 = (bf16[2,36,128]{2,1,0:T(8,128)(2,1)S(1)}, bf16[2,36,128]{2,1,0:T(8,128)(2,1)S(1)}, u32[]{:S(2)}, u32[]{:S(2)}) collective-permute-start(bf16[2,36,128]{2,1,0:T(8,128)(2,1)S(1)} %get-tuple-element.76), channel_id=1, source_target_pairs={{0,1},{1,0},{2,3},{3,2},{4,5},{5,4},{6,7},{7,6},{8,9},{9,8},{10,11... | collective-permute-start | bytes 55304 | tf_op jit(solution)/shard_map/ppermute | solution.py:773
  17.1 0.7 collective-permute-start.3
  17.8 0.5 collective-permute-done.2
  18.3 0.0 collective-permute-done.3
  18.3 0.0 copy-done.2
  18.3 0.0 copy-done.9
  18.3 0.0 copy-start.8
  18.3 0.0 copy-start.11
  18.3 0.0 copy-start.12
  18.4 8.3 %depth.1 = (bf16[32,128,128]{2,1,0:T(8,128)(2,1)S(1)}, bf16[2048,512]{1,0:T(8,128)(2,1)S(1)}, bf16[2176,512]{1,0:T(8,128)(2,1)S(1)}, bf16[2,48,512]{2,1,0:T(8,128)(2,1)S(1)}) custom-call(bf16[32,64,512]{2,1,0:T(8,128)(2,1)S(1)} %bitcast.40, bf16[2048,128]{1,0:T(8,128)(2,1)S(1)} %bitcast.42, bf16[32,64,128]{2,1,0:T(8,128)(2,1)S(1)} %to_columns.1.c_ref, ...), custom_call_target="tpu_custom_call" | custom-call | flops 310378496 | bytes 7340032 | tf_op jit(solution)/shard_map/depth/pallas_call | solution.py:266
  26.7 32.7 %all_to_all.20.x_ref = bf16[32,128,128]{2,1,0:T(8,128)(2,1)S(1)} all-to-all(bf16[32,128,128]{2,1,0:T(8,128)(2,1)S(1)} %get-tuple-element.40), channel_id=1, replica_groups=mesh['rows'=4,'group'=8,'plane'=4] {'rows','group'}, dimensions={0} | all-to-all | bytes 2097152 | tf_op jit(solution)/shard_map/all_to_all | solution.py:815
  59.4 0.0 copy-done.8
  59.4 0.0 copy-done.11
  59.4 0.0 copy-done.12
  59.4 9.8 %attend.1 = (bf16[32,144,128]{2,1,0:T(8,128)(2,1)S(1)}, f32[384,128]{1,0:T(8,128)S(1)}, f32[128,128]{1,0:T(8,128)S(1)}, f32[8,256]{1,0:T(8,128)S(1)}) custom-call(bf16[32,128,128]{2,1,0:T(8,128)(2,1)S(1)} %all_to_all.20.x_ref, f32[1,128]{1,0:T(1,128)S(1)} %bitcast.52, f32[128,384]{1,0:T(8,128)S(1)} %copy-done.8, f32[128,128]{1,0:T(8,128)S(1)} %copy-done.12, ...), custom_call_target="tpu_custom_call" | custom-call | flops 1342177280 | bytes 2097152 | tf_op jit(solution)/shard_map/attend/pallas_call | solution.py:460
  69.2 22.4 %all_to_all.21.x_ref.g_ref = bf16[32,144,128]{2,1,0:T(8,128)(2,1)S(1)} all-to-all(bf16[32,144,128]{2,1,0:T(8,128)(2,1)S(1)} %get-tuple-element.42), channel_id=1, replica_groups=mesh['rows'=4,'group'=8,'plane'=4] {'rows','group'}, dimensions={0} | all-to-all | bytes 2359296 | tf_op jit(solution)/shard_map/all_to_all | solution.py:817
  91.6 0.1 collective-permute-start.4
  91.7 0.8 collective-permute-start.5
  92.6 2.8 %project_grad.1 = (bf16[2176,512]{1,0:T(8,128)(2,1)S(1)}, f32[512,128]{1,0:T(8,128)S(1)}, bf16[2048,128]{1,0:T(8,128)(2,1)S(1)}) custom-call(bf16[32,144,128]{2,1,0:T(8,128)(2,1)S(1)} %all_to_all.21.x_ref.g_ref, f32[512,128]{1,0:T(8,128)S(1)} %copy-done.2, bf16[2048,512]{1,0:T(8,128)(2,1)S(1)} %get-tuple-element.43.d_ref, ...), custom_call_target="tpu_custom_call" | custom-call | flops 536870912 | bytes 7340032 | tf_op jit(solution)/shard_map/project_grad/pallas_call | solution.py:526
  95.3 0.0 collective-permute-done.4
  95.3 0.0 collective-permute-done.5
  95.4 8.0 %depth_grad.1 = (bf16[2048,512]{1,0:T(8,128)(2,1)S(1)}, bf16[2048,128]{1,0:T(8,128)(2,1)S(1)}) custom-call(bf16[34,64,512]{2,1,0:T(8,128)(2,1)S(1)} %bitcast.44, bf16[2,48,128]{2,1,0:T(8,128)(2,1)S(1)} %fusion.12.strip_ref, bf16[2,48,512]{2,1,0:T(8,128)(2,1)S(1)} %get-tuple-element.46.ss_ref, f32[512,128]{1,0:T(8,128)S(1)} %copy-done.2, ...), custom_call_target="tpu_custom_call" | custom-call | flops 331350016 | bytes 9437184 | tf_op jit(solution)/shard_map/depth_grad/pallas_call | solution.py:617
  103.4 0.0 copy-start.4
  103.4 1.3 copy-done.4
  104.8 0.0 copy-start.7
  104.8 0.8 copy-done.7
  105.6 12.6 %all-to-all-start.2 = ((bf16[128,16,128]{2,1,0:T(8,128)(2,1)}), bf16[128,16,128]{2,1,0:T(8,128)(2,1)S(1)}, u32[]{:S(2)}, u32[]{:S(2)}) async-start(bf16[128,16,128]{2,1,0:T(8,128)(2,1)} %bitcast.46), calls=%async_computation.2 | async-start | bytes 1048576 | tf_op jit(solution)/shard_map/all_to_all | solution.py:825
  118.2 0.0 copy-start.5
  118.2 1.6 %copy-done.5 = bf16[2048,512]{1,0:T(8,128)(2,1)S(1)} copy-done((bf16[2048,512]{1,0:T(8,128)(2,1)S(1)}, bf16[2048,512]{1,0:T(8,128)(2,1)}, u32[]{:S(2)}) %copy-start.5) | copy-done | bytes 2097176
  119.8 3.4 %image_grad.1 = bf16[2048,128]{1,0:T(8,128)(2,1)} custom-call(bf16[2048,512]{1,0:T(8,128)(2,1)S(1)} %copy-done.5, f32[128,512]{1,0:T(8,128)S(1)} %copy-done.3, f32[1,128]{1,0:T(1,128)S(1)} %bitcast.50, bf16[2048,128]{1,0:T(8,128)(2,1)S(1)} %bitcast.43, bf16[2048,128]{1,0:T(8,128)(2,1)S(1)} %get-tuple-element.55.m_ref), custom_call_target="tpu_custom_call" | custom-call | flops 268435456 | bytes 3670016 | tf_op jit(solution)/shard_map/image_grad/pallas_call | solution.py:656
  123.2 8.9 %all-to-all-done.2.refs_0_ = bf16[128,16,128]{2,1,0:T(8,128)(2,1)S(1)} async-done(((bf16[128,16,128]{2,1,0:T(8,128)(2,1)}), bf16[128,16,128]{2,1,0:T(8,128)(2,1)S(1)}, u32[]{:S(2)}, u32[]{:S(2)}) %all-to-all-start.2) | async-done | bytes 524320 | tf_op jit(solution)/shard_map/all_to_all | solution.py:825
  132.0 1.7 %sum_parts.1 = bf16[128,16,128]{2,1,0:T(8,128)(2,1)} custom-call(bf16[128,16,128]{2,1,0:T(8,128)(2,1)S(1)} %all-to-all-done.2.refs_0_), custom_call_target="tpu_custom_call" | custom-call | flops 524288 | bytes 1048576 | tf_op jit(solution)/shard_map/sum_parts/pallas_call | solution.py:687
  133.7 4.3 %all-to-all-start.3 = ((bf16[128,16,128]{2,1,0:T(8,128)(2,1)}), bf16[128,16,128]{2,1,0:T(8,128)(2,1)S(1)}, u32[]{:S(2)}, u32[]{:S(2)}) async-start(bf16[128,16,128]{2,1,0:T(8,128)(2,1)} %sum_parts.1), calls=%async_computation.3 | async-start | bytes 1048576 | tf_op jit(solution)/shard_map/all_to_all | solution.py:829
  138.1 1.4 from_columns.1
  139.5 12.5 %all-to-all-done.3 = bf16[128,16,128]{2,1,0:T(8,128)(2,1)S(1)} async-done(((bf16[128,16,128]{2,1,0:T(8,128)(2,1)}), bf16[128,16,128]{2,1,0:T(8,128)(2,1)S(1)}, u32[]{:S(2)}, u32[]{:S(2)}) %all-to-all-start.3) | async-done | bytes 524320 | tf_op jit(solution)/shard_map/all_to_all | solution.py:829
  152.0 1.1 unpack.1
  (21 shorter events, 0.2 us)
Async XLA Ops:
  0.6 5.6 %copy-start = (f32[4,225]{1,0:T(4,128)S(1)}, f32[4,225]{1,0:T(4,128)}, u32[]{:S(2)}) copy-start(f32[4,225]{1,0:T(4,128)} %param.20) | copy-start | bytes 10804
  0.7 10.5 %copy-start.1 = (bf16[32,64,128]{2,1,0:T(8,128)(2,1)S(1)}, bf16[32,64,128]{2,1,0:T(8,128)(2,1)}, u32[]{:S(2)}) copy-start(bf16[32,64,128]{2,1,0:T(8,128)(2,1)} %param.11) | copy-start | bytes 1572868
  0.7 9.8 %copy-start.6 = (bf16[32,64,128]{2,1,0:T(8,128)(2,1)S(1)}, bf16[32,64,128]{2,1,0:T(8,128)(2,1)}, u32[]{:S(2)}) copy-start(bf16[32,64,128]{2,1,0:T(8,128)(2,1)} %x_ref.1) | copy-start | bytes 1572868
  0.7 10.4 %copy-start.3 = (f32[128,512]{1,0:T(8,128)S(1)}, f32[128,512]{1,0:T(8,128)}, u32[]{:S(2)}) copy-start(f32[128,512]{1,0:T(8,128)} %w1_ref.3) | copy-start | bytes 786436
  0.7 10.4 %copy-start.10 = (f32[128]{0:T(128)S(1)}, f32[128]{0:T(128)}, u32[]{:S(2)}) copy-start(f32[128]{0:T(128)} %param.13) | copy-start | bytes 1540
  1.6 13.6 %collective-permute-start.1 = (bf16[128,128]{1,0:T(8,128)(2,1)S(1)}, bf16[128,128]{1,0:T(8,128)(2,1)S(1)}, u32[]{:S(2)}, u32[]{:S(2)}) collective-permute-start(bf16[128,128]{1,0:T(8,128)(2,1)S(1)} %bitcast.60), channel_id=1, source_target_pairs={{32,64},{64,32},{33,65},{65,33},{34,66},{66,34},{35,67},{67,35},{3... | collective-permute-start | bytes 98312 | tf_op jit(solution)/shard_map/ppermute | solution.py:774
  6.1 9.1 %collective-permute-start = (bf16[128,128]{1,0:T(8,128)(2,1)S(1)}, bf16[128,128]{1,0:T(8,128)(2,1)S(1)}, u32[]{:S(2)}, u32[]{:S(2)}) collective-permute-start(bf16[128,128]{1,0:T(8,128)(2,1)S(1)} %bitcast.59), channel_id=1, source_target_pairs={{0,32},{32,0},{64,96},{96,64},{1,33},{33,1},{65,97},{97,65},{2,34}... | collective-permute-start | bytes 98312 | tf_op jit(solution)/shard_map/ppermute | solution.py:773
  9.5 8.9 %copy-start.2 = (f32[512,128]{1,0:T(8,128)S(1)}, f32[512,128]{1,0:T(8,128)}, u32[]{:S(2)}) copy-start(f32[512,128]{1,0:T(8,128)} %w2_ref.3) | copy-start | bytes 786436
  9.5 8.9 %copy-start.9 = (f32[9,512]{1,0:T(8,128)S(1)}, f32[9,512]{1,0:T(8,128)}, u32[]{:S(2)}) copy-start(f32[9,512]{1,0:T(8,128)} %dw_ref.3) | copy-start | bytes 55300
  15.4 2.9 %collective-permute-start.2 = (bf16[2,36,128]{2,1,0:T(8,128)(2,1)S(1)}, bf16[2,36,128]{2,1,0:T(8,128)(2,1)S(1)}, u32[]{:S(2)}, u32[]{:S(2)}) collective-permute-start(bf16[2,36,128]{2,1,0:T(8,128)(2,1)S(1)} %get-tuple-element.76), channel_id=1, source_target_pairs={{0,1},{1,0},{2,3},{3,2},{4,5},{5,4},{6,7},{7,6},{8,9},{9,8},{10,11... | collective-permute-start | bytes 55304 | tf_op jit(solution)/shard_map/ppermute | solution.py:773
  17.1 1.2 collective-permute-start.3
  18.3 41.0 %copy-start.8 = (f32[128,384]{1,0:T(8,128)S(1)}, f32[128,384]{1,0:T(8,128)}, u32[]{:S(2)}) copy-start(f32[128,384]{1,0:T(8,128)} %wq_ref.1) | copy-start | bytes 589828
  18.3 41.0 %copy-start.11 = (f32[128]{0:T(128)S(1)}, f32[128]{0:T(128)}, u32[]{:S(2)}) copy-start(f32[128]{0:T(128)} %param.17) | copy-start | bytes 1540
  18.3 41.0 %copy-start.12 = (f32[128,128]{1,0:T(8,128)S(1)}, f32[128,128]{1,0:T(8,128)}, u32[]{:S(2)}) copy-start(f32[128,128]{1,0:T(8,128)} %wof_ref.1) | copy-start | bytes 196612
  91.6 3.7 %collective-permute-start.4 = (bf16[40,128]{1,0:T(8,128)(2,1)S(1)}, bf16[40,128]{1,0:T(8,128)(2,1)S(1)}, u32[]{:S(2)}, u32[]{:S(2)}) collective-permute-start(bf16[40,128]{1,0:T(8,128)(2,1)S(1)} %get-tuple-element.66), channel_id=1, source_target_pairs={{0,1},{1,0},{2,3},{3,2},{4,5},{5,4},{6,7},{7,6},{8,9},{9,8},{10,11... | collective-permute-start | bytes 30728 | tf_op jit(solution)/shard_map/ppermute | solution.py:773
  91.7 3.6 %collective-permute-start.5 = (bf16[40,128]{1,0:T(8,128)(2,1)S(1)}, bf16[40,128]{1,0:T(8,128)(2,1)S(1)}, u32[]{:S(2)}, u32[]{:S(2)}) collective-permute-start(bf16[40,128]{1,0:T(8,128)(2,1)S(1)} %get-tuple-element.67), channel_id=1, source_target_pairs={{1,2},{2,1},{3,4},{4,3},{5,6},{6,5},{7,8},{8,7},{9,10},{10,9},{11,... | collective-permute-start | bytes 30728 | tf_op jit(solution)/shard_map/ppermute | solution.py:774
  103.4 1.4 copy-start.4
  104.8 0.8 copy-start.7
  105.6 26.5 %all-to-all-start.2 = ((bf16[128,16,128]{2,1,0:T(8,128)(2,1)}), bf16[128,16,128]{2,1,0:T(8,128)(2,1)S(1)}, u32[]{:S(2)}, u32[]{:S(2)}) async-start(bf16[128,16,128]{2,1,0:T(8,128)(2,1)} %bitcast.46), calls=%async_computation.2 | async-start | bytes 1048576 | tf_op jit(solution)/shard_map/all_to_all | solution.py:825
  118.2 1.6 %copy-start.5 = (bf16[2048,512]{1,0:T(8,128)(2,1)S(1)}, bf16[2048,512]{1,0:T(8,128)(2,1)}, u32[]{:S(2)}) copy-start(bf16[2048,512]{1,0:T(8,128)(2,1)} %copy-done.4) | copy-start | bytes 6291460
  133.7 18.3 %all-to-all-start.3 = ((bf16[128,16,128]{2,1,0:T(8,128)(2,1)}), bf16[128,16,128]{2,1,0:T(8,128)(2,1)S(1)}, u32[]{:S(2)}, u32[]{:S(2)}) async-start(bf16[128,16,128]{2,1,0:T(8,128)(2,1)} %sum_parts.1), calls=%async_computation.3 | async-start | bytes 1048576 | tf_op jit(solution)/shard_map/all_to_all | solution.py:829

commit v3 on v2

--- a/solution.py
+++ b/solution.py
@@ -2,7 +2,6 @@
 
 import jax
 import jax.numpy as jnp
-import numpy as np
 from jax import lax
 from jax.experimental import pallas as pl
 from jax.experimental.pallas import tpu as pltpu
@@ -36,7 +35,7 @@
 ROWS_USED = 1616
 PACK_ROWS = 2048
 
-PAIRS = 4
+PAIRS = 8
 
 HBM = pl.BlockSpec(memory_space=pltpu.HBM)
 ANY = pl.BlockSpec()
@@ -304,7 +303,7 @@
     gain_ref,
     wqf_ref,
     wof_ref,
-    bias_ref,
+    table_ref,
     back_ref,
     gq_ref,
     go_ref,
@@ -320,7 +319,9 @@
     ds_ref,
     wq_ref,
     wo_ref,
+    bias_ref,
 ):
+    spread_table(table_ref, bias_ref)
     grad[...] = jnp.zeros(grad.shape, f32)
     ds_ref[...] = jnp.zeros(ds_ref.shape, f32)
     wq_ref[...] = wqf_ref[...].astype(bf16)
@@ -429,23 +430,49 @@
     go_ref[...] = dot(atts[...], cots[...], TN)
 
 
-def table_sums(ds_ref):
+def place_of(col):
     at = lax.broadcasted_iota(jnp.int32, (128, 128), 0) % 64
     lane = lax.broadcasted_iota(jnp.int32, (128, 128), 1)
-    same_row = 2 * (at % 32 // 8) + at // 32 == lane // 16
+    fits = (2 * (at % 32 // 8) + at // 32 == lane // 16) & (at % 8 - col + 7 == lane % 16)
+    return jnp.where(fits, 1.0, 0.0).astype(bf16)
+
+
+def row_of(k):
+    return 2 * (k % 4) + k // 4
+
+
+def spread_table(table_ref, bias_ref):
+    none = jnp.zeros((HEADS, 1), f32)
+    parts = []
+    for k in range(15):
+        parts += [table_ref[:, 15 * k : 15 * k + 15], none]
+    table = jnp.concatenate(parts + [jnp.zeros((HEADS, 16), f32)], axis=1)
+    shifted = [table[:, 16 * (7 - row_of(k)) : 16 * (7 - row_of(k)) + 128] for k in range(8)]
+    rows = [shifted[k][h : h + 1] for h in range(HEADS) for k in range(8)]
+    rows = jnp.concatenate(rows, axis=0)
+    terms = []
+    for _ in range(3):
+        terms.append(rows.astype(bf16))
+        rows = rows - terms[-1].astype(f32)
+    terms = jnp.concatenate(terms, axis=0)
+    for col in range(8):
+        part = dot(terms, place_of(col), NT)
+        bias_ref[pl.ds(col, 32, stride=8), :] = part[0:32] + part[32:64] + part[64:96]
+
+
+def table_sums(ds_ref):
     total = jnp.zeros((32, 128), f32)
     for col in range(8):
-        place = same_row & (at % 8 - col + 7 == lane % 16)
-        place = jnp.where(place, 1.0, 0.0).astype(bf16)
         part = ds_ref[pl.ds(col, 32, stride=8), :]
         high = part.astype(bf16)
-        rest = part - high.astype(f32)
-        total = total + dot(high, place) + dot(rest.astype(bf16), place)
+        rest = (part - high.astype(f32)).astype(bf16)
+        both = dot(jnp.concatenate([high, rest], axis=0), place_of(col))
+        total = total + both[0:32] + both[32:64]
     rows = []
     for h in range(HEADS):
         row_sum = None
         for k in range(8):
-            shift = 16 * (7 - (2 * (k % 4) + k // 4))
+            shift = 16 * (7 - row_of(k))
             part = total[8 * h + k : 8 * h + k + 1]
             none = jnp.zeros((1, 128), f32)
             part = jnp.concatenate([part, none], axis=1)
@@ -455,7 +482,7 @@
     return jnp.concatenate(rows + [jnp.zeros((4, 256), f32)], axis=0)
 
 
-def attend(x, gain, wq, wo, bias):
+def attend(x, gain, wq, wo, table):
     tokens = RD * CD
     return pl.pallas_call(
         attend_kernel,
@@ -477,13 +504,14 @@
             pltpu.VMEM((256, 128), f32),
             pltpu.VMEM((C, 3 * C), bf16),
             pltpu.VMEM((C, C), bf16),
+            pltpu.VMEM((256, 128), f32),
         ],
         compiler_params=pltpu.CompilerParams(vmem_limit_bytes=VMEM_LIMIT),
         cost_estimate=pl.CostEstimate(
             flops=40 * tokens * C * C, bytes_accessed=tokens * 8 * C, transcendentals=tokens * 256
         ),
         name="attend",
-    )(x, gain, wq, wo, bias)
+    )(x, gain, wq, wo, table)
 
 
 def project_grad_kernel(g_ref, w2_ref, d_ref, s_ref, b_ref, gp_ref, gm_ref, cols):
@@ -755,24 +783,17 @@
     )(pack, w1, wq, gain1, gain2)
 
 
-def pair_onehot():
-    place = np.arange(64)
-    row = 2 * ((place % 32) // 8) + place // 32
-    col = place % 8
-    first, second = place[None, :], place[:, None]
-    index = 15 * (row[first] - row[second] + 7) + col[first] - col[second] + 7
-    index = jnp.asarray(np.concatenate([index, index], axis=1), jnp.int32)
-    return (index[:, :, None] == jnp.arange(225, dtype=jnp.int32)).astype(f32)
-
-
-def swap_ends(low, high, axis):
+def swap_ends(low, high, axis, beside=None):
     count = lax.axis_size(axis)
     odd = lax.axis_index(axis) % 2 == 1
     pairs = [(i, i ^ 1) for i in range(count)]
     others = [(i, ((i - 1) ^ 1) + 1) for i in range(1, count - 1)]
     first = lax.ppermute(jnp.where(odd, low, high), axis, pairs)
     second = lax.ppermute(jnp.where(odd, high, low), axis, others)
-    return jnp.where(odd, first, second), jnp.where(odd, second, first)
+    if beside is not None:
+        first, beside = lax.optimization_barrier((first, beside))
+    ends = jnp.where(odd, first, second), jnp.where(odd, second, first)
+    return ends if beside is None else (ends, beside)
 
 
 def per_device(
@@ -791,10 +812,6 @@
     w1, w2, wq, wo = w_expand, w_project, w_qkv, w_out
     gain1 = norm1_gain.reshape(1, C)
     gain2 = norm2_gain.reshape(1, C)
-    onehot = pair_onehot()
-    bias = jnp.einsum("hq,jlq->hjl", bias_table, onehot, precision=lax.Precision.HIGHEST)
-    bias = bias.reshape(HEADS * 64, 128)
-
     tokens = image.reshape(RD * CD, C)
     above, below = swap_ends(tokens[: 2 * CD], tokens[(RD - 2) * CD :], "rows")
     above = above.reshape(2, CD, C)
@@ -803,17 +820,16 @@
     right = jnp.concatenate([above[:, -2:], image[:, -2:], below[:, -2:]], axis=0)
     left = left.transpose(1, 0, 2)
     right = right.transpose(1, 0, 2)
-    before_left, after_right = swap_ends(left, right, COLS)
-    expanded, slope1, normed1 = expand(tokens, gain1, w1)
+    (before_left, after_right), late_gain = swap_ends(left, right, COLS, gain1)
+    expanded, slope1, normed1 = expand(tokens, late_gain, w1)
     halo = jnp.concatenate([above, below], axis=0)
     strip = jnp.concatenate([before_left, left[:1], right[1:], after_right], axis=0)
     strip = jnp.pad(strip, ((0, 0), (0, 12), (0, 0)))
     send, depthed, slope2, slope2_strip = depth(
         expanded, tokens, to_columns(cotangent), halo, strip, gain1, w1, dw_kernel, w2
     )
-    send, bias = lax.optimization_barrier((send, bias))
     windows = lax.all_to_all(send, PLANE, 0, 0, tiled=True)
-    back, grad_qkv, grad_out, grad_bias = attend(windows, gain2, wq, wo, bias)
+    back, grad_qkv, grad_out, grad_bias = attend(windows, gain2, wq, wo, bias_table)
     back = lax.all_to_all(back, PLANE, 0, 0, tiled=True)
     grad_left, grad_right = swap_ends(back[0, :40], back[31, 40:80], COLS)
     before, grad_project, grad_middle = project_grad(back, w2, depthed, slope2)
@@ -823,8 +839,8 @@
         grad_project, grad_qkv, grad_out, grad_bias,
     )
     parts = lax.all_to_all(pack.reshape(128, 16, C), ALL, 0, 0, tiled=True)
+    grad_wide, parts = lax.optimization_barrier((grad_wide, parts))
     grad_image = image_grad(grad_wide, w1, gain1, tokens, grad_middle)
-    parts, grad_image = lax.optimization_barrier((parts, grad_image))
     block_out = from_columns(back)
     whole = lax.all_to_all(sum_parts(parts, factor), ALL, 0, 0, tiled=True)
     g1, ge, gk, gp, g2, gq, go, gb = unpack(whole.reshape(PACK_ROWS, C), w1, wq, gain1, gain2)

time: 154 us -> 145 us (0.942)
  blocking collectives: 55.1 us -> 74.5 us
  waiting for transfers between devices: 21.9 us -> 8.04 us
  starting transfers between devices: 24.8 us -> 12.7 us
  matrix products: 3.25 us -> 0 us
  local copies, waits for them, and re-layouts: 4.78 us -> 7.62 us
    all_to_all x0 -> x1, blocking collectives: none -> 23.9 us  [per_device(): parts = lax.all_to_all(pack.reshape(128, 16, C), ALL, 0, 0, tiled=True)]
    all_to_all x1 -> x0, starting transfers between devices: 12.6 us -> none  [per_device(): parts = lax.all_to_all(pack.reshape(128, 16, C), ALL, 0, 0, tiled=True)]
    all_to_all x1 -> x0, waiting for transfers between devices: 8.87 us -> none  [per_device(): parts = lax.all_to_all(pack.reshape(128, 16, C), ALL, 0, 0, tiled=True)]
    all_to_all x1, waiting for transfers between devices: 12.5 us -> 7.56 us  [per_device(): whole = lax.all_to_all(sum_parts(parts, factor), ALL, 0, 0, tiled=True)]
    all_to_all x1, blocking collectives: 32.7 us -> 28.2 us  [per_device(): windows = lax.all_to_all(send, PLANE, 0, 0, tiled=True)]
    dot_general x1 -> x0, matrix products: 3.25 us -> none  [per_device(): jnp.einsum('hq,jlq->hjl', bias_table, onehot, precision=lax.Precision.HIG...]
    unnamed x32 -> x36, local copies, waits for them, and re-layouts: 3.81 us -> 6.69 us
  transfers between devices with their start and end apart: 8 -> 7, of which waited for: 3 -> 2; matrix products, arithmetic and copies ran while one was open for 3% -> 1% of each run, Pallas kernels for 8% -> 8%
where the time goes in v3:
time: 145 us
  blocking collectives  74.5 us (51%)
  Pallas kernels  39.8 us (27%)
  starting transfers between devices  12.7 us (9%)
  waiting for transfers between devices  8.04 us (6%)
  local copies, waits for them, and re-layouts  7.62 us (5%)
    all_to_all x1, blocking collectives, per_device(): windows = lax.all_to_all(send, PLANE, 0, 0, tiled=True)  28.2 us
    all_to_all x1, blocking collectives, per_device(): parts = lax.all_to_all(pack.reshape(128, 16, C), ALL, 0, 0, tiled=True)  23.9 us
    all_to_all x1, blocking collectives, per_device(): back = lax.all_to_all(back, PLANE, 0, 0, tiled=True)  22.4 us
    pallas_call x1, Pallas kernels, attend(): pl.pallas_call(attend_kernel, out_shape=[jax.ShapeDtypeStruct((32, 144, C...  8.68 us
    pallas_call x1, Pallas kernels, depth(): pl.pallas_call(depth_kernel, out_shape=[jax.ShapeDtypeStruct((CD // 2, 4...  8.25 us
    pallas_call x1, Pallas kernels, depth_grad(): pl.pallas_call(depth_grad_kernel, out_shape=[jax.ShapeDtypeStruct((tokens...  7.84 us
    all_to_all x1, waiting for transfers between devices, per_device(): whole = lax.all_to_all(sum_parts(parts, factor), ALL, 0, 0, tiled=True)  7.56 us
    unnamed x36, local copies, waits for them, and re-layouts  6.69 us
  transfers between devices with their start and end apart: 7, of which 2 were waited for; matrix products, arithmetic and copies ran while one was open for 1% of the time, Pallas kernels for 8%

profile of v3, /device:TPU:1, one launch (start us, length us, event | category | flops | bytes accessed | tf_op | source)
XLA Modules:
  0.0 144.7 jit_solution(9781873431795278072)
XLA Ops:
  0.6 0.0 copy-start.2
  0.7 0.0 copy-start.9
  0.7 0.8 broadcast_select_fusion.1
  1.5 4.5 %collective-permute-start.1 = (bf16[128,128]{1,0:T(8,128)(2,1)S(1)}, bf16[128,128]{1,0:T(8,128)(2,1)S(1)}, u32[]{:S(2)}, u32[]{:S(2)}) collective-permute-start(bf16[128,128]{1,0:T(8,128)(2,1)S(1)} %bitcast.53), channel_id=1, source_target_pairs={{32,64},{64,32},{33,65},{65,33},{34,66},{66,34},{35,67},{67,35},{3... | collective-permute-start | bytes 98312 | tf_op jit(solution)/shard_map/ppermute | solution.py:792
  6.0 0.1 collective-permute-start
  6.1 0.9 fusion.10
  7.0 0.0 copy-start.7
  7.1 1.0 copy-done.7
  8.1 0.6 to_columns.1.c_ref
  8.7 0.0 collective-permute-done.1
  8.7 0.0 collective-permute-done
  8.9 1.7 %collective-permute-start.2 = (bf16[2,36,128]{2,1,0:T(8,128)(2,1)S(1)}, bf16[2,36,128]{2,1,0:T(8,128)(2,1)S(1)}, u32[]{:S(2)}, u32[]{:S(2)}) collective-permute-start(bf16[2,36,128]{2,1,0:T(8,128)(2,1)S(1)} %get-tuple-element.77), channel_id=1, source_target_pairs={{0,1},{1,0},{2,3},{3,2},{4,5},{5,4},{6,7},{7,6},{8,9},{9,8},{10,11... | collective-permute-start | bytes 55304 | tf_op jit(solution)/shard_map/ppermute | solution.py:791
  10.7 0.7 collective-permute-start.3
  11.3 0.5 collective-permute-done.2
  11.8 0.0 copy-start
  11.8 1.0 copy-done
  12.9 0.0 copy-start.3
  12.9 0.9 copy-done.3
  13.8 0.0 copy-start.10
  13.8 0.7 copy-done.10
  14.5 4.0 %expand.1 = (bf16[2048,512]{1,0:T(8,128)(2,1)S(1)}, bf16[2048,512]{1,0:T(8,128)(2,1)S(1)}, bf16[2048,128]{1,0:T(8,128)(2,1)S(1)}) custom-call(bf16[2048,128]{1,0:T(8,128)(2,1)S(1)} %bitcast.35, f32[1,128]{1,0:T(1,128)S(1)} %bitcast.41, f32[128,512]{1,0:T(8,128)S(1)} %copy-done.3), custom_call_target="tpu_custom_call" | custom-call | flops 289406976 | bytes 5242880 | tf_op jit(solution)/shard_map/expand/pallas_call | solution.py:153
  18.5 0.0 collective-permute-done.3
  18.5 0.0 copy-done.2
  18.6 0.0 copy-done.9
  18.6 0.0 copy-start.8
  18.6 0.0 copy-start.12
  18.6 0.0 copy-start.13
  18.6 0.0 copy-start.14
  18.6 8.3 %depth.1 = (bf16[32,128,128]{2,1,0:T(8,128)(2,1)S(1)}, bf16[2048,512]{1,0:T(8,128)(2,1)S(1)}, bf16[2176,512]{1,0:T(8,128)(2,1)S(1)}, bf16[2,48,512]{2,1,0:T(8,128)(2,1)S(1)}) custom-call(bf16[32,64,512]{2,1,0:T(8,128)(2,1)S(1)} %bitcast.34, bf16[2048,128]{1,0:T(8,128)(2,1)S(1)} %bitcast.36, bf16[32,64,128]{2,1,0:T(8,128)(2,1)S(1)} %to_columns.1.c_ref, ...), custom_call_target="tpu_custom_call" | custom-call | flops 310378496 | bytes 7340032 | tf_op jit(solution)/shard_map/depth/pallas_call | solution.py:265
  26.9 28.2 %all_to_all.20.x_ref = bf16[32,128,128]{2,1,0:T(8,128)(2,1)S(1)} all-to-all(bf16[32,128,128]{2,1,0:T(8,128)(2,1)S(1)} %get-tuple-element.41), channel_id=1, replica_groups=mesh['rows'=4,'group'=8,'plane'=4] {'rows','group'}, dimensions={0} | all-to-all | bytes 2097152 | tf_op jit(solution)/shard_map/all_to_all | solution.py:831
  55.0 0.0 copy-done.8
  55.0 0.0 copy-done.12
  55.1 0.0 copy-done.13
  55.1 0.0 copy-done.14
  55.1 8.7 %attend.1 = (bf16[32,144,128]{2,1,0:T(8,128)(2,1)S(1)}, f32[384,128]{1,0:T(8,128)S(1)}, f32[128,128]{1,0:T(8,128)S(1)}, f32[8,256]{1,0:T(8,128)S(1)}) custom-call(bf16[32,128,128]{2,1,0:T(8,128)(2,1)S(1)} %all_to_all.20.x_ref, f32[1,128]{1,0:T(1,128)S(1)} %bitcast.45, f32[128,384]{1,0:T(8,128)S(1)} %copy-done.8, f32[128,128]{1,0:T(8,128)S(1)} %copy-done.13, ...), custom_call_target="tpu_custom_call" | custom-call | flops 1342177280 | bytes 2097152 | tf_op jit(solution)/shard_map/attend/pallas_call | solution.py:487
  63.8 22.4 %all_to_all.21.x_ref.g_ref = bf16[32,144,128]{2,1,0:T(8,128)(2,1)S(1)} all-to-all(bf16[32,144,128]{2,1,0:T(8,128)(2,1)S(1)} %get-tuple-element.42), channel_id=1, replica_groups=mesh['rows'=4,'group'=8,'plane'=4] {'rows','group'}, dimensions={0} | all-to-all | bytes 2359296 | tf_op jit(solution)/shard_map/all_to_all | solution.py:833
  86.2 0.6 collective-permute-start.4
  86.8 0.8 collective-permute-start.5
  87.6 2.8 %project_grad.1 = (bf16[2176,512]{1,0:T(8,128)(2,1)S(1)}, f32[512,128]{1,0:T(8,128)S(1)}, bf16[2048,128]{1,0:T(8,128)(2,1)S(1)}) custom-call(bf16[32,144,128]{2,1,0:T(8,128)(2,1)S(1)} %all_to_all.21.x_ref.g_ref, f32[512,128]{1,0:T(8,128)S(1)} %copy-done.2, bf16[2048,512]{1,0:T(8,128)(2,1)S(1)} %get-tuple-element.43.d_ref, ...), custom_call_target="tpu_custom_call" | custom-call | flops 536870912 | bytes 7340032 | tf_op jit(solution)/shard_map/project_grad/pallas_call | solution.py:554
  90.4 0.0 collective-permute-done.4
  90.4 0.0 collective-permute-done.5
  90.4 7.8 %depth_grad.1 = (bf16[2048,512]{1,0:T(8,128)(2,1)S(1)}, bf16[2048,128]{1,0:T(8,128)(2,1)S(1)}) custom-call(bf16[34,64,512]{2,1,0:T(8,128)(2,1)S(1)} %bitcast.38, bf16[2,48,128]{2,1,0:T(8,128)(2,1)S(1)} %fusion.9.strip_ref, bf16[2,48,512]{2,1,0:T(8,128)(2,1)S(1)} %get-tuple-element.46.ss_ref, f32[512,128]{1,0:T(8,128)S(1)} %copy-done.2, ...), custom_call_target="tpu_custom_call" | custom-call | flops 331350016 | bytes 9437184 | tf_op jit(solution)/shard_map/depth_grad/pallas_call | solution.py:645
  98.3 0.0 copy-start.5
  98.3 1.3 copy-done.5
  99.6 23.9 %all_to_all.22.refs_0_ = bf16[128,16,128]{2,1,0:T(8,128)(2,1)S(1)} all-to-all(bf16[128,16,128]{2,1,0:T(8,128)(2,1)S(1)} %bitcast.40), channel_id=1, replica_groups=mesh['rows'=4,'group'=8,'plane'=4] {'rows','group','plane'}, dimensions={0} | all-to-all | bytes 1048576 | tf_op jit(solution)/shard_map/all_to_all | solution.py:841
  123.5 0.0 copy-start.1
  123.6 0.0 copy-start.4
  123.6 0.0 copy-start.11
  123.6 1.7 %sum_parts.1 = bf16[128,16,128]{2,1,0:T(8,128)(2,1)} custom-call(bf16[128,16,128]{2,1,0:T(8,128)(2,1)S(1)} %all_to_all.22.refs_0_), custom_call_target="tpu_custom_call" | custom-call | flops 524288 | bytes 1048576 | tf_op jit(solution)/shard_map/sum_parts/pallas_call | solution.py:715
  125.3 4.3 %all-to-all-start.3 = ((bf16[128,16,128]{2,1,0:T(8,128)(2,1)}), bf16[128,16,128]{2,1,0:T(8,128)(2,1)S(1)}, u32[]{:S(2)}, u32[]{:S(2)}) async-start(bf16[128,16,128]{2,1,0:T(8,128)(2,1)} %sum_parts.1), calls=%async_computation.3 | async-start | bytes 1048576 | tf_op jit(solution)/shard_map/all_to_all | solution.py:845
  129.6 1.4 from_columns.1
  131.1 0.0 copy-done.1
  131.1 0.0 copy-done.4
  131.1 0.0 copy-done.11
  131.1 0.0 copy-start.6
  131.1 1.6 %copy-done.6 = bf16[2048,512]{1,0:T(8,128)(2,1)S(1)} copy-done((bf16[2048,512]{1,0:T(8,128)(2,1)S(1)}, bf16[2048,512]{1,0:T(8,128)(2,1)}, u32[]{:S(2)}) %copy-start.6) | copy-done | bytes 2097176
  132.7 3.4 %image_grad.1 = bf16[2048,128]{1,0:T(8,128)(2,1)} custom-call(bf16[2048,512]{1,0:T(8,128)(2,1)S(1)} %copy-done.6, f32[128,512]{1,0:T(8,128)S(1)} %copy-done.4, f32[1,128]{1,0:T(1,128)S(1)} %bitcast.43, bf16[2048,128]{1,0:T(8,128)(2,1)S(1)} %bitcast.37, bf16[2048,128]{1,0:T(8,128)(2,1)S(1)} %get-tuple-element.56.m_ref), custom_call_target="tpu_custom_call" | custom-call | flops 268435456 | bytes 3670016 | tf_op jit(solution)/shard_map/image_grad/pallas_call | solution.py:684
  136.0 7.6 %all-to-all-done.3 = bf16[128,16,128]{2,1,0:T(8,128)(2,1)S(1)} async-done(((bf16[128,16,128]{2,1,0:T(8,128)(2,1)}), bf16[128,16,128]{2,1,0:T(8,128)(2,1)S(1)}, u32[]{:S(2)}, u32[]{:S(2)}) %all-to-all-start.3) | async-done | bytes 524320 | tf_op jit(solution)/shard_map/all_to_all | solution.py:845
  143.6 1.1 unpack.1
  (20 shorter events, 0.2 us)
Async XLA Ops:
  0.6 17.9 %copy-start.2 = (f32[512,128]{1,0:T(8,128)S(1)}, f32[512,128]{1,0:T(8,128)}, u32[]{:S(2)}) copy-start(f32[512,128]{1,0:T(8,128)} %w2_ref.3) | copy-start | bytes 786436
  0.7 17.9 %copy-start.9 = (f32[9,512]{1,0:T(8,128)S(1)}, f32[9,512]{1,0:T(8,128)}, u32[]{:S(2)}) copy-start(f32[9,512]{1,0:T(8,128)} %dw_ref.3) | copy-start | bytes 55300
  1.5 7.2 %collective-permute-start.1 = (bf16[128,128]{1,0:T(8,128)(2,1)S(1)}, bf16[128,128]{1,0:T(8,128)(2,1)S(1)}, u32[]{:S(2)}, u32[]{:S(2)}) collective-permute-start(bf16[128,128]{1,0:T(8,128)(2,1)S(1)} %bitcast.53), channel_id=1, source_target_pairs={{32,64},{64,32},{33,65},{65,33},{34,66},{66,34},{35,67},{67,35},{3... | collective-permute-start | bytes 98312 | tf_op jit(solution)/shard_map/ppermute | solution.py:792
  6.0 2.7 %collective-permute-start = (bf16[128,128]{1,0:T(8,128)(2,1)S(1)}, bf16[128,128]{1,0:T(8,128)(2,1)S(1)}, u32[]{:S(2)}, u32[]{:S(2)}) collective-permute-start(bf16[128,128]{1,0:T(8,128)(2,1)S(1)} %bitcast.52), channel_id=1, source_target_pairs={{0,32},{32,0},{64,96},{96,64},{1,33},{33,1},{65,97},{97,65},{2,34}... | collective-permute-start | bytes 98312 | tf_op jit(solution)/shard_map/ppermute | solution.py:791
  7.0 1.0 copy-start.7
  8.9 2.9 %collective-permute-start.2 = (bf16[2,36,128]{2,1,0:T(8,128)(2,1)S(1)}, bf16[2,36,128]{2,1,0:T(8,128)(2,1)S(1)}, u32[]{:S(2)}, u32[]{:S(2)}) collective-permute-start(bf16[2,36,128]{2,1,0:T(8,128)(2,1)S(1)} %get-tuple-element.77), channel_id=1, source_target_pairs={{0,1},{1,0},{2,3},{3,2},{4,5},{5,4},{6,7},{7,6},{8,9},{9,8},{10,11... | collective-permute-start | bytes 55304 | tf_op jit(solution)/shard_map/ppermute | solution.py:791
  10.7 7.8 %collective-permute-start.3 = (bf16[2,36,128]{2,1,0:T(8,128)(2,1)S(1)}, bf16[2,36,128]{2,1,0:T(8,128)(2,1)S(1)}, u32[]{:S(2)}, u32[]{:S(2)}) collective-permute-start(bf16[2,36,128]{2,1,0:T(8,128)(2,1)S(1)} %get-tuple-element.76), channel_id=1, source_target_pairs={{1,2},{2,1},{3,4},{4,3},{5,6},{6,5},{7,8},{8,7},{9,10},{10,9},{11,... | collective-permute-start | bytes 55304 | tf_op jit(solution)/shard_map/ppermute | solution.py:792
  11.8 1.0 copy-start
  12.9 0.9 copy-start.3
  13.8 0.7 copy-start.10
  18.6 36.5 %copy-start.8 = (f32[128,384]{1,0:T(8,128)S(1)}, f32[128,384]{1,0:T(8,128)}, u32[]{:S(2)}) copy-start(f32[128,384]{1,0:T(8,128)} %wq_ref.1) | copy-start | bytes 589828
  18.6 36.5 %copy-start.12 = (f32[128]{0:T(128)S(1)}, f32[128]{0:T(128)}, u32[]{:S(2)}) copy-start(f32[128]{0:T(128)} %param.16) | copy-start | bytes 1540
  18.6 36.5 %copy-start.13 = (f32[128,128]{1,0:T(8,128)S(1)}, f32[128,128]{1,0:T(8,128)}, u32[]{:S(2)}) copy-start(f32[128,128]{1,0:T(8,128)} %wof_ref.1) | copy-start | bytes 196612
  18.6 36.5 %copy-start.14 = (f32[4,225]{1,0:T(4,128)S(1)}, f32[4,225]{1,0:T(4,128)}, u32[]{:S(2)}) copy-start(f32[4,225]{1,0:T(4,128)} %table_ref.1) | copy-start | bytes 10804
  86.2 4.2 %collective-permute-start.4 = (bf16[40,128]{1,0:T(8,128)(2,1)S(1)}, bf16[40,128]{1,0:T(8,128)(2,1)S(1)}, u32[]{:S(2)}, u32[]{:S(2)}) collective-permute-start(bf16[40,128]{1,0:T(8,128)(2,1)S(1)} %get-tuple-element.66), channel_id=1, source_target_pairs={{0,1},{1,0},{2,3},{3,2},{4,5},{5,4},{6,7},{7,6},{8,9},{9,8},{10,11... | collective-permute-start | bytes 30728 | tf_op jit(solution)/shard_map/ppermute | solution.py:791
  86.8 3.6 %collective-permute-start.5 = (bf16[40,128]{1,0:T(8,128)(2,1)S(1)}, bf16[40,128]{1,0:T(8,128)(2,1)S(1)}, u32[]{:S(2)}, u32[]{:S(2)}) collective-permute-start(bf16[40,128]{1,0:T(8,128)(2,1)S(1)} %get-tuple-element.67), channel_id=1, source_target_pairs={{1,2},{2,1},{3,4},{4,3},{5,6},{6,5},{7,8},{8,7},{9,10},{10,9},{11,... | collective-permute-start | bytes 30728 | tf_op jit(solution)/shard_map/ppermute | solution.py:792
  98.3 1.4 copy-start.5
  123.5 7.5 %copy-start.1 = (bf16[32,64,128]{2,1,0:T(8,128)(2,1)S(1)}, bf16[32,64,128]{2,1,0:T(8,128)(2,1)}, u32[]{:S(2)}) copy-start(bf16[32,64,128]{2,1,0:T(8,128)(2,1)} %param.10) | copy-start | bytes 1572868
  123.6 7.5 %copy-start.4 = (f32[128,512]{1,0:T(8,128)S(1)}, f32[128,512]{1,0:T(8,128)}, u32[]{:S(2)}) copy-start(f32[128,512]{1,0:T(8,128)} %w1_ref.3) | copy-start | bytes 786436
  123.6 7.5 %copy-start.11 = (f32[128]{0:T(128)S(1)}, f32[128]{0:T(128)}, u32[]{:S(2)}) copy-start(f32[128]{0:T(128)} %param.12) | copy-start | bytes 1540
  125.3 18.3 %all-to-all-start.3 = ((bf16[128,16,128]{2,1,0:T(8,128)(2,1)}), bf16[128,16,128]{2,1,0:T(8,128)(2,1)S(1)}, u32[]{:S(2)}, u32[]{:S(2)}) async-start(bf16[128,16,128]{2,1,0:T(8,128)(2,1)} %sum_parts.1), calls=%async_computation.3 | async-start | bytes 1048576 | tf_op jit(solution)/shard_map/all_to_all | solution.py:845
  131.1 1.6 %copy-start.6 = (bf16[2048,512]{1,0:T(8,128)(2,1)S(1)}, bf16[2048,512]{1,0:T(8,128)(2,1)}, u32[]{:S(2)}) copy-start(bf16[2048,512]{1,0:T(8,128)(2,1)} %copy-done.5) | copy-start | bytes 6291460

commit v4 on v3

--- a/solution.py
+++ b/solution.py
@@ -35,7 +35,7 @@
 ROWS_USED = 1616
 PACK_ROWS = 2048
 
-PAIRS = 8
+PAIRS = 16
 
 HBM = pl.BlockSpec(memory_space=pltpu.HBM)
 ANY = pl.BlockSpec()
@@ -54,6 +54,7 @@
 
 
 def gelu_pair(t):
+    t = t.astype(bf16)
     t2 = t * t
     u = jnp.tanh(t * (t2 * (0.044715 * gelu_coef) + gelu_coef))
     h = 0.5 * u + 0.5
@@ -139,8 +140,9 @@
         at = pl.ds(pl.multiple_of(i * 256, 256), 256)
         normed = (normalise(x_ref[at, :].astype(f32))[1] * gain_ref[...]).astype(bf16)
         n_ref[at, :] = normed
+        wide = dot(normed, w)
         for g in range(GROUPS):
-            value, slope = gelu_pair(dot(normed, w[:, lane_group(g)]))
+            value, slope = gelu_pair(wide[:, lane_group(g)])
             e_ref[at, lane_group(g)] = value.astype(bf16)
             s_ref[at, lane_group(g)] = slope.astype(bf16)
         return carry
@@ -225,11 +227,18 @@
 
     fill(0)
 
+    def project(i):
+        four = pl.ds(pl.multiple_of(i * 4 * CD, 4 * CD), 4 * CD)
+        mid[four, :] = x_ref[four, :].astype(f32) + dot(d_ref[four, :], w2_ref[...])
+
+    d_ref[0 : 4 * CD, :] = jnp.zeros((4 * CD, E), bf16)
+
     def block(i, carry):
         @pl.when(i < RD // 4 - 1)
         def _():
             fill(i + 1)
 
+        project(jnp.maximum(i - 1, 0))
         for k in range(4):
             row = i * 4 + k
             at = pl.ds(pl.multiple_of(row * CD, CD), CD)
@@ -238,11 +247,10 @@
                 value, slope = gelu_pair(conv_row(ext, taps_of(g), g, row + 1))
                 d_ref[at, lane_group(g)] = value.astype(bf16)
                 s_ref[ring, lane_group(g)] = slope.astype(bf16)
-        four = pl.ds(pl.multiple_of(i * 4 * CD, 4 * CD), 4 * CD)
-        mid[four, :] = x_ref[four, :].astype(f32) + dot(d_ref[four, :], w2_ref[...])
         return carry
 
     lax.fori_loop(0, RD // 4, block, 0)
+    project(RD // 4 - 1)
     for col in range(CD):
         part = mid[pl.ds(col, RD, stride=CD), :]
         send_ref[col // 2, (col % 2) * RD : (col % 2 + 1) * RD, :] = part.astype(bf16)
@@ -605,28 +613,41 @@
     sums[...] = jnp.zeros(sums.shape, f32)
     total[...] = jnp.zeros(total.shape, f32)
 
+    def add_grad(i, weight=1.0):
+        four = pl.ds(pl.multiple_of(i * 4 * CD, 4 * CD), 4 * CD)
+        wide = dot(n_ref[four, :], x_ref[four, :], TN) * weight
+        for g in range(GROUPS):
+            total[lane_group(g), :] += wide[:, lane_group(g)]
+
+    x_ref[0 : 4 * CD, :] = jnp.zeros((4 * CD, E), bf16)
+
     def block(i, carry):
         fill(i * 4 + 2, 4)
+        add_grad(jnp.maximum(i - 1, 0), jnp.where(i > 0, 1.0, 0.0))
         for k in range(4):
             row = i * 4 + k
             at = pl.ds(pl.multiple_of(row * CD, CD), CD)
             for g in range(GROUPS):
-                own = e_ref[at, lane_group(g)].astype(f32)
-                running = None
+                held = [sums[g, t] for t in range(9)]
+                for q in range(0, CD, 16):
+                    here = pl.ds(pl.multiple_of(row * CD + q, 16), 16)
+                    own = e_ref[here, lane_group(g)].astype(f32)
+                    running = None
+                    for t in range(9):
+                        left = 15 + t % 3 + q
+                        window = ext[g, row + t // 3, left : left + 16, :]
+                        term = dw_ref[8 - t : 9 - t, lane_group(g)] * window
+                        running = term if running is None else running + term
+                        part = own * window
+                        held[8 - t] = held[8 - t] + (part[0:8] + part[8:16])
+                    wide = running * s_ref[here, lane_group(g)].astype(f32)
+                    x_ref[here, lane_group(g)] = wide.astype(bf16)
                 for t in range(9):
-                    window = ext[g, row + t // 3, 15 + t % 3 : 15 + t % 3 + CD, :]
-                    term = dw_ref[8 - t : 9 - t, lane_group(g)] * window
-                    running = term if running is None else running + term
-                    sums[g, 8 - t] += jnp.sum((own * window).reshape(CD // 8, 8, LANES), axis=0)
-                wide = running * s_ref[at, lane_group(g)].astype(f32)
-                x_ref[at, lane_group(g)] = wide.astype(bf16)
-        four = pl.ds(pl.multiple_of(i * 4 * CD, 4 * CD), 4 * CD)
-        normed = n_ref[four, :]
-        for g in range(GROUPS):
-            total[lane_group(g), :] += dot(normed, x_ref[four, lane_group(g)], TN)
+                    sums[g, t] = held[t]
         return carry
 
     lax.fori_loop(0, RD // 4, block, 0)
+    add_grad(RD // 4 - 1)
     pack_ref[ROW_EXPAND : ROW_EXPAND + E, :] = total[...].astype(bf16)
     pack_ref[ROW_PROJECT : ROW_PROJECT + E, :] = gp_ref[...].astype(bf16)
     pack_ref[ROW_QKV : ROW_QKV + 3 * C, :] = gq_ref[...].astype(bf16)

time: 145 us -> 142 us (0.979)
  Pallas kernels: 39.8 us -> 35.8 us
    pallas_call x1, Pallas kernels: 8.25 us -> 6.67 us  [depth(): pl.pallas_call(depth_kernel, out_shape=[jax.ShapeDtypeStruct((CD // 2, 4...]
where the time goes in v4:
time: 142 us; the launch traced here: 141 us
  blocking collectives  75.2 us (53%)
  Pallas kernels  35.8 us (25%)
  starting transfers between devices  12.5 us (9%)
  waiting for transfers between devices  8.04 us (6%)
  local copies, waits for them, and re-layouts  7.62 us (5%)
    all_to_all x1, blocking collectives, per_device(): windows = lax.all_to_all(send, PLANE, 0, 0, tiled=True)  28.1 us
    all_to_all x1, blocking collectives, per_device(): parts = lax.all_to_all(pack.reshape(128, 16, C), ALL, 0, 0, tiled=True)  24.6 us
    all_to_all x1, blocking collectives, per_device(): back = lax.all_to_all(back, PLANE, 0, 0, tiled=True)  22.4 us
    pallas_call x1, Pallas kernels, attend(): pl.pallas_call(attend_kernel, out_shape=[jax.ShapeDtypeStruct((32, 144, C...  8.17 us
    all_to_all x1, waiting for transfers between devices, per_device(): whole = lax.all_to_all(sum_parts(parts, factor), ALL, 0, 0, tiled=True)  7.56 us
    pallas_call x1, Pallas kernels, depth_grad(): pl.pallas_call(depth_grad_kernel, out_shape=[jax.ShapeDtypeStruct((tokens...  6.69 us
    unnamed x36, local copies, waits for them, and re-layouts  6.69 us
    pallas_call x1, Pallas kernels, depth(): pl.pallas_call(depth_kernel, out_shape=[jax.ShapeDtypeStruct((CD // 2, 4...  6.67 us
  transfers between devices with their start and end apart: 7, of which 2 were waited for; matrix products, arithmetic and copies ran while one was open for 1% of the time, Pallas kernels for 8%

profile of v4, /device:TPU:1, one launch (start us, length us, event | category | flops | bytes accessed | tf_op | source)
XLA Modules:
  0.0 141.1 jit_solution(284083722802009859)
XLA Ops:
  0.6 0.0 copy-start.2
  0.7 0.0 copy-start.9
  0.7 0.8 broadcast_select_fusion.1
  1.5 4.5 %collective-permute-start.1 = (bf16[128,128]{1,0:T(8,128)(2,1)S(1)}, bf16[128,128]{1,0:T(8,128)(2,1)S(1)}, u32[]{:S(2)}, u32[]{:S(2)}) collective-permute-start(bf16[128,128]{1,0:T(8,128)(2,1)S(1)} %bitcast.53), channel_id=1, source_target_pairs={{32,64},{64,32},{33,65},{65,33},{34,66},{66,34},{35,67},{67,35},{3... | collective-permute-start | bytes 98312 | tf_op jit(solution)/shard_map/ppermute | solution.py:813
  6.0 0.1 collective-permute-start
  6.1 0.9 fusion.10
  7.0 0.0 copy-start.7
  7.1 1.0 copy-done.7
  8.1 0.6 to_columns.1.c_ref
  8.7 0.0 collective-permute-done.1
  8.7 0.0 collective-permute-done
  8.9 1.7 %collective-permute-start.2 = (bf16[2,36,128]{2,1,0:T(8,128)(2,1)S(1)}, bf16[2,36,128]{2,1,0:T(8,128)(2,1)S(1)}, u32[]{:S(2)}, u32[]{:S(2)}) collective-permute-start(bf16[2,36,128]{2,1,0:T(8,128)(2,1)S(1)} %get-tuple-element.77), channel_id=1, source_target_pairs={{0,1},{1,0},{2,3},{3,2},{4,5},{5,4},{6,7},{7,6},{8,9},{9,8},{10,11... | collective-permute-start | bytes 55304 | tf_op jit(solution)/shard_map/ppermute | solution.py:812
  10.7 0.7 collective-permute-start.3
  11.3 0.5 collective-permute-done.2
  11.8 0.0 copy-start
  11.8 1.0 copy-done
  12.9 0.0 copy-start.3
  12.9 0.9 copy-done.3
  13.8 0.0 copy-start.10
  13.8 0.7 copy-done.10
  14.5 3.3 %expand.1 = (bf16[2048,512]{1,0:T(8,128)(2,1)S(1)}, bf16[2048,512]{1,0:T(8,128)(2,1)S(1)}, bf16[2048,128]{1,0:T(8,128)(2,1)S(1)}) custom-call(bf16[2048,128]{1,0:T(8,128)(2,1)S(1)} %bitcast.35, f32[1,128]{1,0:T(1,128)S(1)} %bitcast.41, f32[128,512]{1,0:T(8,128)S(1)} %copy-done.3), custom_call_target="tpu_custom_call" | custom-call | flops 289406976 | bytes 5242880 | tf_op jit(solution)/shard_map/expand/pallas_call | solution.py:155
  17.7 0.0 collective-permute-done.3
  17.8 0.0 copy-done.2
  17.8 0.0 copy-done.9
  17.8 0.0 copy-start.8
  17.8 0.0 copy-start.12
  17.8 0.0 copy-start.13
  17.8 0.0 copy-start.14
  17.9 6.7 %depth.1 = (bf16[32,128,128]{2,1,0:T(8,128)(2,1)S(1)}, bf16[2048,512]{1,0:T(8,128)(2,1)S(1)}, bf16[2176,512]{1,0:T(8,128)(2,1)S(1)}, bf16[2,48,512]{2,1,0:T(8,128)(2,1)S(1)}) custom-call(bf16[32,64,512]{2,1,0:T(8,128)(2,1)S(1)} %bitcast.34, bf16[2048,128]{1,0:T(8,128)(2,1)S(1)} %bitcast.36, bf16[32,64,128]{2,1,0:T(8,128)(2,1)S(1)} %to_columns.1.c_ref, ...), custom_call_target="tpu_custom_call" | custom-call | flops 310378496 | bytes 7340032 | tf_op jit(solution)/shard_map/depth/pallas_call | solution.py:273
  24.5 28.1 %all_to_all.20.x_ref = bf16[32,128,128]{2,1,0:T(8,128)(2,1)S(1)} all-to-all(bf16[32,128,128]{2,1,0:T(8,128)(2,1)S(1)} %get-tuple-element.41), channel_id=1, replica_groups=mesh['rows'=4,'group'=8,'plane'=4] {'rows','group'}, dimensions={0} | all-to-all | bytes 2097152 | tf_op jit(solution)/shard_map/all_to_all | solution.py:852
  52.7 0.0 copy-done.8
  52.7 0.0 copy-done.12
  52.7 0.0 copy-done.13
  52.7 0.0 copy-done.14
  52.7 8.2 %attend.1 = (bf16[32,144,128]{2,1,0:T(8,128)(2,1)S(1)}, f32[384,128]{1,0:T(8,128)S(1)}, f32[128,128]{1,0:T(8,128)S(1)}, f32[8,256]{1,0:T(8,128)S(1)}) custom-call(bf16[32,128,128]{2,1,0:T(8,128)(2,1)S(1)} %all_to_all.20.x_ref, f32[1,128]{1,0:T(1,128)S(1)} %bitcast.45, f32[128,384]{1,0:T(8,128)S(1)} %copy-done.8, f32[128,128]{1,0:T(8,128)S(1)} %copy-done.13, ...), custom_call_target="tpu_custom_call" | custom-call | flops 1342177280 | bytes 2097152 | tf_op jit(solution)/shard_map/attend/pallas_call | solution.py:495
  60.9 22.4 %all_to_all.21.x_ref.g_ref = bf16[32,144,128]{2,1,0:T(8,128)(2,1)S(1)} all-to-all(bf16[32,144,128]{2,1,0:T(8,128)(2,1)S(1)} %get-tuple-element.42), channel_id=1, replica_groups=mesh['rows'=4,'group'=8,'plane'=4] {'rows','group'}, dimensions={0} | all-to-all | bytes 2359296 | tf_op jit(solution)/shard_map/all_to_all | solution.py:854
  83.3 0.6 collective-permute-start.4
  83.9 0.7 collective-permute-start.5
  84.5 2.8 %project_grad.1 = (bf16[2176,512]{1,0:T(8,128)(2,1)S(1)}, f32[512,128]{1,0:T(8,128)S(1)}, bf16[2048,128]{1,0:T(8,128)(2,1)S(1)}) custom-call(bf16[32,144,128]{2,1,0:T(8,128)(2,1)S(1)} %all_to_all.21.x_ref.g_ref, f32[512,128]{1,0:T(8,128)S(1)} %copy-done.2, bf16[2048,512]{1,0:T(8,128)(2,1)S(1)} %get-tuple-element.43.d_ref, ...), custom_call_target="tpu_custom_call" | custom-call | flops 536870912 | bytes 7340032 | tf_op jit(solution)/shard_map/project_grad/pallas_call | solution.py:562
  87.3 0.0 collective-permute-done.4
  87.3 0.0 collective-permute-done.5
  87.3 6.7 %depth_grad.1 = (bf16[2048,512]{1,0:T(8,128)(2,1)S(1)}, bf16[2048,128]{1,0:T(8,128)(2,1)S(1)}) custom-call(bf16[34,64,512]{2,1,0:T(8,128)(2,1)S(1)} %bitcast.38, bf16[2,48,128]{2,1,0:T(8,128)(2,1)S(1)} %fusion.9.strip_ref, bf16[2,48,512]{2,1,0:T(8,128)(2,1)S(1)} %get-tuple-element.46.ss_ref, f32[512,128]{1,0:T(8,128)S(1)} %copy-done.2, ...), custom_call_target="tpu_custom_call" | custom-call | flops 331350016 | bytes 9437184 | tf_op jit(solution)/shard_map/depth_grad/pallas_call | solution.py:666
  94.0 0.0 copy-start.5
  94.0 1.3 copy-done.5
  95.4 24.6 %all_to_all.22.refs_0_ = bf16[128,16,128]{2,1,0:T(8,128)(2,1)S(1)} all-to-all(bf16[128,16,128]{2,1,0:T(8,128)(2,1)S(1)} %bitcast.40), channel_id=1, replica_groups=mesh['rows'=4,'group'=8,'plane'=4] {'rows','group','plane'}, dimensions={0} | all-to-all | bytes 1048576 | tf_op jit(solution)/shard_map/all_to_all | solution.py:862
  120.0 0.0 copy-start.1
  120.0 0.0 copy-start.4
  120.0 0.0 copy-start.11
  120.0 1.7 %sum_parts.1 = bf16[128,16,128]{2,1,0:T(8,128)(2,1)} custom-call(bf16[128,16,128]{2,1,0:T(8,128)(2,1)S(1)} %all_to_all.22.refs_0_), custom_call_target="tpu_custom_call" | custom-call | flops 524288 | bytes 1048576 | tf_op jit(solution)/shard_map/sum_parts/pallas_call | solution.py:736
  121.8 4.3 %all-to-all-start.3 = ((bf16[128,16,128]{2,1,0:T(8,128)(2,1)}), bf16[128,16,128]{2,1,0:T(8,128)(2,1)S(1)}, u32[]{:S(2)}, u32[]{:S(2)}) async-start(bf16[128,16,128]{2,1,0:T(8,128)(2,1)} %sum_parts.1), calls=%async_computation.3 | async-start | bytes 1048576 | tf_op jit(solution)/shard_map/all_to_all | solution.py:866
  126.1 1.4 %from_columns.1 = bf16[32,64,128]{2,1,0:T(8,128)(2,1)} custom-call(bf16[32,144,128]{2,1,0:T(8,128)(2,1)S(1)} %all_to_all.21.x_ref.g_ref), custom_call_target="tpu_custom_call" | custom-call | bytes 1048576 | tf_op jit(solution)/shard_map/from_columns/pallas_call | solution.py:126
  127.6 0.0 copy-done.1
  127.6 0.0 copy-done.4
  127.6 0.0 copy-done.11
  127.6 0.0 copy-start.6
  127.6 1.6 %copy-done.6 = bf16[2048,512]{1,0:T(8,128)(2,1)S(1)} copy-done((bf16[2048,512]{1,0:T(8,128)(2,1)S(1)}, bf16[2048,512]{1,0:T(8,128)(2,1)}, u32[]{:S(2)}) %copy-start.6) | copy-done | bytes 2097176
  129.2 3.4 %image_grad.1 = bf16[2048,128]{1,0:T(8,128)(2,1)} custom-call(bf16[2048,512]{1,0:T(8,128)(2,1)S(1)} %copy-done.6, f32[128,512]{1,0:T(8,128)S(1)} %copy-done.4, f32[1,128]{1,0:T(1,128)S(1)} %bitcast.43, bf16[2048,128]{1,0:T(8,128)(2,1)S(1)} %bitcast.37, bf16[2048,128]{1,0:T(8,128)(2,1)S(1)} %get-tuple-element.56.m_ref), custom_call_target="tpu_custom_call" | custom-call | flops 268435456 | bytes 3670016 | tf_op jit(solution)/shard_map/image_grad/pallas_call | solution.py:705
  132.5 7.6 %all-to-all-done.3 = bf16[128,16,128]{2,1,0:T(8,128)(2,1)S(1)} async-done(((bf16[128,16,128]{2,1,0:T(8,128)(2,1)}), bf16[128,16,128]{2,1,0:T(8,128)(2,1)S(1)}, u32[]{:S(2)}, u32[]{:S(2)}) %all-to-all-start.3) | async-done | bytes 524320 | tf_op jit(solution)/shard_map/all_to_all | solution.py:866
  140.1 1.1 unpack.1
  (20 shorter events, 0.2 us)
Async XLA Ops:
  0.6 17.1 %copy-start.2 = (f32[512,128]{1,0:T(8,128)S(1)}, f32[512,128]{1,0:T(8,128)}, u32[]{:S(2)}) copy-start(f32[512,128]{1,0:T(8,128)} %w2_ref.3) | copy-start | bytes 786436
  0.7 17.1 %copy-start.9 = (f32[9,512]{1,0:T(8,128)S(1)}, f32[9,512]{1,0:T(8,128)}, u32[]{:S(2)}) copy-start(f32[9,512]{1,0:T(8,128)} %dw_ref.3) | copy-start | bytes 55300
  1.5 7.2 %collective-permute-start.1 = (bf16[128,128]{1,0:T(8,128)(2,1)S(1)}, bf16[128,128]{1,0:T(8,128)(2,1)S(1)}, u32[]{:S(2)}, u32[]{:S(2)}) collective-permute-start(bf16[128,128]{1,0:T(8,128)(2,1)S(1)} %bitcast.53), channel_id=1, source_target_pairs={{32,64},{64,32},{33,65},{65,33},{34,66},{66,34},{35,67},{67,35},{3... | collective-permute-start | bytes 98312 | tf_op jit(solution)/shard_map/ppermute | solution.py:813
  6.0 2.7 %collective-permute-start = (bf16[128,128]{1,0:T(8,128)(2,1)S(1)}, bf16[128,128]{1,0:T(8,128)(2,1)S(1)}, u32[]{:S(2)}, u32[]{:S(2)}) collective-permute-start(bf16[128,128]{1,0:T(8,128)(2,1)S(1)} %bitcast.52), channel_id=1, source_target_pairs={{0,32},{32,0},{64,96},{96,64},{1,33},{33,1},{65,97},{97,65},{2,34}... | collective-permute-start | bytes 98312 | tf_op jit(solution)/shard_map/ppermute | solution.py:812
  7.0 1.0 copy-start.7
  8.9 2.9 %collective-permute-start.2 = (bf16[2,36,128]{2,1,0:T(8,128)(2,1)S(1)}, bf16[2,36,128]{2,1,0:T(8,128)(2,1)S(1)}, u32[]{:S(2)}, u32[]{:S(2)}) collective-permute-start(bf16[2,36,128]{2,1,0:T(8,128)(2,1)S(1)} %get-tuple-element.77), channel_id=1, source_target_pairs={{0,1},{1,0},{2,3},{3,2},{4,5},{5,4},{6,7},{7,6},{8,9},{9,8},{10,11... | collective-permute-start | bytes 55304 | tf_op jit(solution)/shard_map/ppermute | solution.py:812
  10.7 7.1 %collective-permute-start.3 = (bf16[2,36,128]{2,1,0:T(8,128)(2,1)S(1)}, bf16[2,36,128]{2,1,0:T(8,128)(2,1)S(1)}, u32[]{:S(2)}, u32[]{:S(2)}) collective-permute-start(bf16[2,36,128]{2,1,0:T(8,128)(2,1)S(1)} %get-tuple-element.76), channel_id=1, source_target_pairs={{1,2},{2,1},{3,4},{4,3},{5,6},{6,5},{7,8},{8,7},{9,10},{10,9},{11,... | collective-permute-start | bytes 55304 | tf_op jit(solution)/shard_map/ppermute | solution.py:813
  11.8 1.0 copy-start
  12.9 0.9 copy-start.3
  13.8 0.7 copy-start.10
  17.8 34.9 %copy-start.8 = (f32[128,384]{1,0:T(8,128)S(1)}, f32[128,384]{1,0:T(8,128)}, u32[]{:S(2)}) copy-start(f32[128,384]{1,0:T(8,128)} %wq_ref.1) | copy-start | bytes 589828
  17.8 34.9 %copy-start.12 = (f32[128]{0:T(128)S(1)}, f32[128]{0:T(128)}, u32[]{:S(2)}) copy-start(f32[128]{0:T(128)} %param.16) | copy-start | bytes 1540
  17.8 34.8 %copy-start.13 = (f32[128,128]{1,0:T(8,128)S(1)}, f32[128,128]{1,0:T(8,128)}, u32[]{:S(2)}) copy-start(f32[128,128]{1,0:T(8,128)} %wof_ref.1) | copy-start | bytes 196612
  17.8 34.8 %copy-start.14 = (f32[4,225]{1,0:T(4,128)S(1)}, f32[4,225]{1,0:T(4,128)}, u32[]{:S(2)}) copy-start(f32[4,225]{1,0:T(4,128)} %table_ref.1) | copy-start | bytes 10804
  83.3 4.0 %collective-permute-start.4 = (bf16[40,128]{1,0:T(8,128)(2,1)S(1)}, bf16[40,128]{1,0:T(8,128)(2,1)S(1)}, u32[]{:S(2)}, u32[]{:S(2)}) collective-permute-start(bf16[40,128]{1,0:T(8,128)(2,1)S(1)} %get-tuple-element.66), channel_id=1, source_target_pairs={{0,1},{1,0},{2,3},{3,2},{4,5},{5,4},{6,7},{7,6},{8,9},{9,8},{10,11... | collective-permute-start | bytes 30728 | tf_op jit(solution)/shard_map/ppermute | solution.py:812
  83.9 3.4 %collective-permute-start.5 = (bf16[40,128]{1,0:T(8,128)(2,1)S(1)}, bf16[40,128]{1,0:T(8,128)(2,1)S(1)}, u32[]{:S(2)}, u32[]{:S(2)}) collective-permute-start(bf16[40,128]{1,0:T(8,128)(2,1)S(1)} %get-tuple-element.67), channel_id=1, source_target_pairs={{1,2},{2,1},{3,4},{4,3},{5,6},{6,5},{7,8},{8,7},{9,10},{10,9},{11,... | collective-permute-start | bytes 30728 | tf_op jit(solution)/shard_map/ppermute | solution.py:813
  94.0 1.4 copy-start.5
  120.0 7.5 %copy-start.1 = (bf16[32,64,128]{2,1,0:T(8,128)(2,1)S(1)}, bf16[32,64,128]{2,1,0:T(8,128)(2,1)}, u32[]{:S(2)}) copy-start(bf16[32,64,128]{2,1,0:T(8,128)(2,1)} %param.10) | copy-start | bytes 1572868
  120.0 7.5 %copy-start.4 = (f32[128,512]{1,0:T(8,128)S(1)}, f32[128,512]{1,0:T(8,128)}, u32[]{:S(2)}) copy-start(f32[128,512]{1,0:T(8,128)} %w1_ref.3) | copy-start | bytes 786436
  120.0 7.5 %copy-start.11 = (f32[128]{0:T(128)S(1)}, f32[128]{0:T(128)}, u32[]{:S(2)}) copy-start(f32[128]{0:T(128)} %param.12) | copy-start | bytes 1540
  121.8 18.3 %all-to-all-start.3 = ((bf16[128,16,128]{2,1,0:T(8,128)(2,1)}), bf16[128,16,128]{2,1,0:T(8,128)(2,1)S(1)}, u32[]{:S(2)}, u32[]{:S(2)}) async-start(bf16[128,16,128]{2,1,0:T(8,128)(2,1)} %sum_parts.1), calls=%async_computation.3 | async-start | bytes 1048576 | tf_op jit(solution)/shard_map/all_to_all | solution.py:866
  127.6 1.6 %copy-start.6 = (bf16[2048,512]{1,0:T(8,128)(2,1)S(1)}, bf16[2048,512]{1,0:T(8,128)(2,1)}, u32[]{:S(2)}) copy-start(bf16[2048,512]{1,0:T(8,128)(2,1)} %copy-done.5) | copy-start | bytes 6291460

commit v5 on v4

--- a/solution.py
+++ b/solution.py
@@ -34,8 +34,6 @@
 ROW_BIAS = 1600
 ROWS_USED = 1616
 PACK_ROWS = 2048
-
-PAIRS = 16
 
 HBM = pl.BlockSpec(memory_space=pltpu.HBM)
 ANY = pl.BlockSpec()
@@ -375,9 +373,8 @@
                 k = 2 * c + il
                 dst[at, :] = x[k * 32 : (k + 1) * 32]
 
-    def pairs(i, carry):
-        each = range(PAIRS)
-        r0s = [i * PAIRS + p for p in each]
+    def pairs(r0s):
+        each = range(len(r0s))
         ms = [windows(mid, r0, 64, 0) for r0 in r0s]
         cts = [windows(cot, r0, 64, 0) for r0 in r0s]
         ctbs = [ct.astype(bf16) for ct in cts]
@@ -412,7 +409,7 @@
         gn = [dot(x, wq_ref[...], NT).astype(bf16).astype(f32) for x in gx]
         mixed = [dot(x, wo_ref[...]) for x in att]
         for p in each:
-            at = pl.ds(pl.multiple_of(r0s[p] * 128, 128), 128)
+            at = pl.ds(r0s[p] * 128, 128)
             inverse, unit = scales[p]
             scaled = gn[p] * gain
             mean = jnp.mean(scaled * unit, axis=-1, keepdims=True)
@@ -422,9 +419,8 @@
             atts[at, :] = att[p]
             cots[at, :] = ctbs[p]
             mixes[at, :] = gx[p]
-        return carry
-
-    lax.fori_loop(0, 16 // PAIRS, pairs, 0)
+
+    pairs(range(16))
     for c in range(2):
         low = grad[pl.ds(c * 40 + 32, 24, stride=80), :]
         high = grad[pl.ds(c * 40 + 1 + 8 * 80, 24, stride=80), :]

time: 142 us -> 142 us (level)
  no operation moved by 1% of the time
where the time goes in v5:
time: 142 us; the launch traced here: 141 us
  blocking collectives  75.2 us (53%)
  Pallas kernels  35.8 us (25%)
  starting transfers between devices  12.5 us (9%)
  waiting for transfers between devices  8.04 us (6%)
  local copies, waits for them, and re-layouts  7.62 us (5%)
    all_to_all x1, blocking collectives, per_device(): windows = lax.all_to_all(send, PLANE, 0, 0, tiled=True)  28.1 us
    all_to_all x1, blocking collectives, per_device(): parts = lax.all_to_all(pack.reshape(128, 16, C), ALL, 0, 0, tiled=True)  24.6 us
    all_to_all x1, blocking collectives, per_device(): back = lax.all_to_all(back, PLANE, 0, 0, tiled=True)  22.4 us
    pallas_call x1, Pallas kernels, attend(): pl.pallas_call(attend_kernel, out_shape=[jax.ShapeDtypeStruct((32, 144, C...  8.17 us
    all_to_all x1, waiting for transfers between devices, per_device(): whole = lax.all_to_all(sum_parts(parts, factor), ALL, 0, 0, tiled=True)  7.56 us
    pallas_call x1, Pallas kernels, depth_grad(): pl.pallas_call(depth_grad_kernel, out_shape=[jax.ShapeDtypeStruct((tokens...  6.69 us
    unnamed x36, local copies, waits for them, and re-layouts  6.69 us
    pallas_call x1, Pallas kernels, depth(): pl.pallas_call(depth_kernel, out_shape=[jax.ShapeDtypeStruct((CD // 2, 4...  6.67 us
  transfers between devices with their start and end apart: 7, of which 2 were waited for; matrix products, arithmetic and copies ran while one was open for 1% of the time, Pallas kernels for 8%

profile of v5, /device:TPU:1, one launch (start us, length us, event | category | flops | bytes accessed | tf_op | source)
XLA Modules:
  0.0 141.1 jit_solution(284083722802009859)
XLA Ops:
  0.6 0.0 copy-start.2
  0.7 0.0 copy-start.9
  0.7 0.8 broadcast_select_fusion.1
  1.5 4.5 %collective-permute-start.1 = (bf16[128,128]{1,0:T(8,128)(2,1)S(1)}, bf16[128,128]{1,0:T(8,128)(2,1)S(1)}, u32[]{:S(2)}, u32[]{:S(2)}) collective-permute-start(bf16[128,128]{1,0:T(8,128)(2,1)S(1)} %bitcast.53), channel_id=1, source_target_pairs={{32,64},{64,32},{33,65},{65,33},{34,66},{66,34},{35,67},{67,35},{3... | collective-permute-start | bytes 98312 | tf_op jit(solution)/shard_map/ppermute | solution.py:809
  6.0 0.1 collective-permute-start
  6.1 0.9 fusion.10
  7.0 0.0 copy-start.7
  7.1 1.0 copy-done.7
  8.1 0.6 to_columns.1.c_ref
  8.7 0.0 collective-permute-done.1
  8.7 0.0 collective-permute-done
  8.9 1.7 %collective-permute-start.2 = (bf16[2,36,128]{2,1,0:T(8,128)(2,1)S(1)}, bf16[2,36,128]{2,1,0:T(8,128)(2,1)S(1)}, u32[]{:S(2)}, u32[]{:S(2)}) collective-permute-start(bf16[2,36,128]{2,1,0:T(8,128)(2,1)S(1)} %get-tuple-element.77), channel_id=1, source_target_pairs={{0,1},{1,0},{2,3},{3,2},{4,5},{5,4},{6,7},{7,6},{8,9},{9,8},{10,11... | collective-permute-start | bytes 55304 | tf_op jit(solution)/shard_map/ppermute | solution.py:808
  10.7 0.7 collective-permute-start.3
  11.3 0.5 collective-permute-done.2
  11.8 0.0 copy-start
  11.8 1.0 copy-done
  12.9 0.0 copy-start.3
  12.9 0.9 copy-done.3
  13.8 0.0 copy-start.10
  13.8 0.7 copy-done.10
  14.5 3.3 %expand.1 = (bf16[2048,512]{1,0:T(8,128)(2,1)S(1)}, bf16[2048,512]{1,0:T(8,128)(2,1)S(1)}, bf16[2048,128]{1,0:T(8,128)(2,1)S(1)}) custom-call(bf16[2048,128]{1,0:T(8,128)(2,1)S(1)} %bitcast.35, f32[1,128]{1,0:T(1,128)S(1)} %bitcast.41, f32[128,512]{1,0:T(8,128)S(1)} %copy-done.3), custom_call_target="tpu_custom_call" | custom-call | flops 289406976 | bytes 5242880 | tf_op jit(solution)/shard_map/expand/pallas_call | solution.py:153
  17.7 0.0 collective-permute-done.3
  17.8 0.0 copy-done.2
  17.8 0.0 copy-done.9
  17.8 0.0 copy-start.8
  17.8 0.0 copy-start.12
  17.8 0.0 copy-start.13
  17.8 0.0 copy-start.14
  17.9 6.7 %depth.1 = (bf16[32,128,128]{2,1,0:T(8,128)(2,1)S(1)}, bf16[2048,512]{1,0:T(8,128)(2,1)S(1)}, bf16[2176,512]{1,0:T(8,128)(2,1)S(1)}, bf16[2,48,512]{2,1,0:T(8,128)(2,1)S(1)}) custom-call(bf16[32,64,512]{2,1,0:T(8,128)(2,1)S(1)} %bitcast.34, bf16[2048,128]{1,0:T(8,128)(2,1)S(1)} %bitcast.36, bf16[32,64,128]{2,1,0:T(8,128)(2,1)S(1)} %to_columns.1.c_ref, ...), custom_call_target="tpu_custom_call" | custom-call | flops 310378496 | bytes 7340032 | tf_op jit(solution)/shard_map/depth/pallas_call | solution.py:271
  24.5 28.1 %all_to_all.20.x_ref = bf16[32,128,128]{2,1,0:T(8,128)(2,1)S(1)} all-to-all(bf16[32,128,128]{2,1,0:T(8,128)(2,1)S(1)} %get-tuple-element.41), channel_id=1, replica_groups=mesh['rows'=4,'group'=8,'plane'=4] {'rows','group'}, dimensions={0} | all-to-all | bytes 2097152 | tf_op jit(solution)/shard_map/all_to_all | solution.py:848
  52.7 0.0 copy-done.8
  52.7 0.0 copy-done.12
  52.7 0.0 copy-done.13
  52.7 0.0 copy-done.14
  52.7 8.2 %attend.1 = (bf16[32,144,128]{2,1,0:T(8,128)(2,1)S(1)}, f32[384,128]{1,0:T(8,128)S(1)}, f32[128,128]{1,0:T(8,128)S(1)}, f32[8,256]{1,0:T(8,128)S(1)}) custom-call(bf16[32,128,128]{2,1,0:T(8,128)(2,1)S(1)} %all_to_all.20.x_ref, f32[1,128]{1,0:T(1,128)S(1)} %bitcast.45, f32[128,384]{1,0:T(8,128)S(1)} %copy-done.8, f32[128,128]{1,0:T(8,128)S(1)} %copy-done.13, ...), custom_call_target="tpu_custom_call" | custom-call | flops 1342177280 | bytes 2097152 | tf_op jit(solution)/shard_map/attend/pallas_call | solution.py:491
  60.9 22.4 %all_to_all.21.x_ref.g_ref = bf16[32,144,128]{2,1,0:T(8,128)(2,1)S(1)} all-to-all(bf16[32,144,128]{2,1,0:T(8,128)(2,1)S(1)} %get-tuple-element.42), channel_id=1, replica_groups=mesh['rows'=4,'group'=8,'plane'=4] {'rows','group'}, dimensions={0} | all-to-all | bytes 2359296 | tf_op jit(solution)/shard_map/all_to_all | solution.py:850
  83.3 0.6 collective-permute-start.4
  83.9 0.7 collective-permute-start.5
  84.5 2.8 %project_grad.1 = (bf16[2176,512]{1,0:T(8,128)(2,1)S(1)}, f32[512,128]{1,0:T(8,128)S(1)}, bf16[2048,128]{1,0:T(8,128)(2,1)S(1)}) custom-call(bf16[32,144,128]{2,1,0:T(8,128)(2,1)S(1)} %all_to_all.21.x_ref.g_ref, f32[512,128]{1,0:T(8,128)S(1)} %copy-done.2, bf16[2048,512]{1,0:T(8,128)(2,1)S(1)} %get-tuple-element.43.d_ref, ...), custom_call_target="tpu_custom_call" | custom-call | flops 536870912 | bytes 7340032 | tf_op jit(solution)/shard_map/project_grad/pallas_call | solution.py:558
  87.3 0.0 collective-permute-done.4
  87.3 0.0 collective-permute-done.5
  87.3 6.7 %depth_grad.1 = (bf16[2048,512]{1,0:T(8,128)(2,1)S(1)}, bf16[2048,128]{1,0:T(8,128)(2,1)S(1)}) custom-call(bf16[34,64,512]{2,1,0:T(8,128)(2,1)S(1)} %bitcast.38, bf16[2,48,128]{2,1,0:T(8,128)(2,1)S(1)} %fusion.9.strip_ref, bf16[2,48,512]{2,1,0:T(8,128)(2,1)S(1)} %get-tuple-element.46.ss_ref, f32[512,128]{1,0:T(8,128)S(1)} %copy-done.2, ...), custom_call_target="tpu_custom_call" | custom-call | flops 331350016 | bytes 9437184 | tf_op jit(solution)/shard_map/depth_grad/pallas_call | solution.py:662
  94.0 0.0 copy-start.5
  94.0 1.3 copy-done.5
  95.4 24.6 %all_to_all.22.refs_0_ = bf16[128,16,128]{2,1,0:T(8,128)(2,1)S(1)} all-to-all(bf16[128,16,128]{2,1,0:T(8,128)(2,1)S(1)} %bitcast.40), channel_id=1, replica_groups=mesh['rows'=4,'group'=8,'plane'=4] {'rows','group','plane'}, dimensions={0} | all-to-all | bytes 1048576 | tf_op jit(solution)/shard_map/all_to_all | solution.py:858
  120.0 0.0 copy-start.1
  120.0 0.0 copy-start.4
  120.0 0.0 copy-start.11
  120.0 1.7 %sum_parts.1 = bf16[128,16,128]{2,1,0:T(8,128)(2,1)} custom-call(bf16[128,16,128]{2,1,0:T(8,128)(2,1)S(1)} %all_to_all.22.refs_0_), custom_call_target="tpu_custom_call" | custom-call | flops 524288 | bytes 1048576 | tf_op jit(solution)/shard_map/sum_parts/pallas_call | solution.py:732
  121.8 4.3 %all-to-all-start.3 = ((bf16[128,16,128]{2,1,0:T(8,128)(2,1)}), bf16[128,16,128]{2,1,0:T(8,128)(2,1)S(1)}, u32[]{:S(2)}, u32[]{:S(2)}) async-start(bf16[128,16,128]{2,1,0:T(8,128)(2,1)} %sum_parts.1), calls=%async_computation.3 | async-start | bytes 1048576 | tf_op jit(solution)/shard_map/all_to_all | solution.py:862
  126.1 1.4 %from_columns.1 = bf16[32,64,128]{2,1,0:T(8,128)(2,1)} custom-call(bf16[32,144,128]{2,1,0:T(8,128)(2,1)S(1)} %all_to_all.21.x_ref.g_ref), custom_call_target="tpu_custom_call" | custom-call | bytes 1048576 | tf_op jit(solution)/shard_map/from_columns/pallas_call | solution.py:124
  127.6 0.0 copy-done.1
  127.6 0.0 copy-done.4
  127.6 0.0 copy-done.11
  127.6 0.0 copy-start.6
  127.6 1.6 %copy-done.6 = bf16[2048,512]{1,0:T(8,128)(2,1)S(1)} copy-done((bf16[2048,512]{1,0:T(8,128)(2,1)S(1)}, bf16[2048,512]{1,0:T(8,128)(2,1)}, u32[]{:S(2)}) %copy-start.6) | copy-done | bytes 2097176
  129.2 3.4 %image_grad.1 = bf16[2048,128]{1,0:T(8,128)(2,1)} custom-call(bf16[2048,512]{1,0:T(8,128)(2,1)S(1)} %copy-done.6, f32[128,512]{1,0:T(8,128)S(1)} %copy-done.4, f32[1,128]{1,0:T(1,128)S(1)} %bitcast.43, bf16[2048,128]{1,0:T(8,128)(2,1)S(1)} %bitcast.37, bf16[2048,128]{1,0:T(8,128)(2,1)S(1)} %get-tuple-element.56.m_ref), custom_call_target="tpu_custom_call" | custom-call | flops 268435456 | bytes 3670016 | tf_op jit(solution)/shard_map/image_grad/pallas_call | solution.py:701
  132.5 7.6 %all-to-all-done.3 = bf16[128,16,128]{2,1,0:T(8,128)(2,1)S(1)} async-done(((bf16[128,16,128]{2,1,0:T(8,128)(2,1)}), bf16[128,16,128]{2,1,0:T(8,128)(2,1)S(1)}, u32[]{:S(2)}, u32[]{:S(2)}) %all-to-all-start.3) | async-done | bytes 524320 | tf_op jit(solution)/shard_map/all_to_all | solution.py:862
  140.1 1.1 unpack.1
  (20 shorter events, 0.2 us)
Async XLA Ops:
  0.6 17.1 %copy-start.2 = (f32[512,128]{1,0:T(8,128)S(1)}, f32[512,128]{1,0:T(8,128)}, u32[]{:S(2)}) copy-start(f32[512,128]{1,0:T(8,128)} %w2_ref.3) | copy-start | bytes 786436
  0.7 17.1 %copy-start.9 = (f32[9,512]{1,0:T(8,128)S(1)}, f32[9,512]{1,0:T(8,128)}, u32[]{:S(2)}) copy-start(f32[9,512]{1,0:T(8,128)} %dw_ref.3) | copy-start | bytes 55300
  1.5 7.2 %collective-permute-start.1 = (bf16[128,128]{1,0:T(8,128)(2,1)S(1)}, bf16[128,128]{1,0:T(8,128)(2,1)S(1)}, u32[]{:S(2)}, u32[]{:S(2)}) collective-permute-start(bf16[128,128]{1,0:T(8,128)(2,1)S(1)} %bitcast.53), channel_id=1, source_target_pairs={{32,64},{64,32},{33,65},{65,33},{34,66},{66,34},{35,67},{67,35},{3... | collective-permute-start | bytes 98312 | tf_op jit(solution)/shard_map/ppermute | solution.py:809
  6.0 2.7 %collective-permute-start = (bf16[128,128]{1,0:T(8,128)(2,1)S(1)}, bf16[128,128]{1,0:T(8,128)(2,1)S(1)}, u32[]{:S(2)}, u32[]{:S(2)}) collective-permute-start(bf16[128,128]{1,0:T(8,128)(2,1)S(1)} %bitcast.52), channel_id=1, source_target_pairs={{0,32},{32,0},{64,96},{96,64},{1,33},{33,1},{65,97},{97,65},{2,34}... | collective-permute-start | bytes 98312 | tf_op jit(solution)/shard_map/ppermute | solution.py:808
  7.0 1.0 copy-start.7
  8.9 2.9 %collective-permute-start.2 = (bf16[2,36,128]{2,1,0:T(8,128)(2,1)S(1)}, bf16[2,36,128]{2,1,0:T(8,128)(2,1)S(1)}, u32[]{:S(2)}, u32[]{:S(2)}) collective-permute-start(bf16[2,36,128]{2,1,0:T(8,128)(2,1)S(1)} %get-tuple-element.77), channel_id=1, source_target_pairs={{0,1},{1,0},{2,3},{3,2},{4,5},{5,4},{6,7},{7,6},{8,9},{9,8},{10,11... | collective-permute-start | bytes 55304 | tf_op jit(solution)/shard_map/ppermute | solution.py:808
  10.7 7.1 %collective-permute-start.3 = (bf16[2,36,128]{2,1,0:T(8,128)(2,1)S(1)}, bf16[2,36,128]{2,1,0:T(8,128)(2,1)S(1)}, u32[]{:S(2)}, u32[]{:S(2)}) collective-permute-start(bf16[2,36,128]{2,1,0:T(8,128)(2,1)S(1)} %get-tuple-element.76), channel_id=1, source_target_pairs={{1,2},{2,1},{3,4},{4,3},{5,6},{6,5},{7,8},{8,7},{9,10},{10,9},{11,... | collective-permute-start | bytes 55304 | tf_op jit(solution)/shard_map/ppermute | solution.py:809
  11.8 1.0 copy-start
  12.9 0.9 copy-start.3
  13.8 0.7 copy-start.10
  17.8 34.9 %copy-start.8 = (f32[128,384]{1,0:T(8,128)S(1)}, f32[128,384]{1,0:T(8,128)}, u32[]{:S(2)}) copy-start(f32[128,384]{1,0:T(8,128)} %wq_ref.1) | copy-start | bytes 589828
  17.8 34.9 %copy-start.12 = (f32[128]{0:T(128)S(1)}, f32[128]{0:T(128)}, u32[]{:S(2)}) copy-start(f32[128]{0:T(128)} %param.16) | copy-start | bytes 1540
  17.8 34.8 %copy-start.13 = (f32[128,128]{1,0:T(8,128)S(1)}, f32[128,128]{1,0:T(8,128)}, u32[]{:S(2)}) copy-start(f32[128,128]{1,0:T(8,128)} %wof_ref.1) | copy-start | bytes 196612
  17.8 34.8 %copy-start.14 = (f32[4,225]{1,0:T(4,128)S(1)}, f32[4,225]{1,0:T(4,128)}, u32[]{:S(2)}) copy-start(f32[4,225]{1,0:T(4,128)} %table_ref.1) | copy-start | bytes 10804
  83.3 4.0 %collective-permute-start.4 = (bf16[40,128]{1,0:T(8,128)(2,1)S(1)}, bf16[40,128]{1,0:T(8,128)(2,1)S(1)}, u32[]{:S(2)}, u32[]{:S(2)}) collective-permute-start(bf16[40,128]{1,0:T(8,128)(2,1)S(1)} %get-tuple-element.66), channel_id=1, source_target_pairs={{0,1},{1,0},{2,3},{3,2},{4,5},{5,4},{6,7},{7,6},{8,9},{9,8},{10,11... | collective-permute-start | bytes 30728 | tf_op jit(solution)/shard_map/ppermute | solution.py:808
  83.9 3.4 %collective-permute-start.5 = (bf16[40,128]{1,0:T(8,128)(2,1)S(1)}, bf16[40,128]{1,0:T(8,128)(2,1)S(1)}, u32[]{:S(2)}, u32[]{:S(2)}) collective-permute-start(bf16[40,128]{1,0:T(8,128)(2,1)S(1)} %get-tuple-element.67), channel_id=1, source_target_pairs={{1,2},{2,1},{3,4},{4,3},{5,6},{6,5},{7,8},{8,7},{9,10},{10,9},{11,... | collective-permute-start | bytes 30728 | tf_op jit(solution)/shard_map/ppermute | solution.py:809
  94.0 1.4 copy-start.5
  120.0 7.5 %copy-start.1 = (bf16[32,64,128]{2,1,0:T(8,128)(2,1)S(1)}, bf16[32,64,128]{2,1,0:T(8,128)(2,1)}, u32[]{:S(2)}) copy-start(bf16[32,64,128]{2,1,0:T(8,128)(2,1)} %param.10) | copy-start | bytes 1572868
  120.0 7.5 %copy-start.4 = (f32[128,512]{1,0:T(8,128)S(1)}, f32[128,512]{1,0:T(8,128)}, u32[]{:S(2)}) copy-start(f32[128,512]{1,0:T(8,128)} %w1_ref.3) | copy-start | bytes 786436
  120.0 7.5 %copy-start.11 = (f32[128]{0:T(128)S(1)}, f32[128]{0:T(128)}, u32[]{:S(2)}) copy-start(f32[128]{0:T(128)} %param.12) | copy-start | bytes 1540
  121.8 18.3 %all-to-all-start.3 = ((bf16[128,16,128]{2,1,0:T(8,128)(2,1)}), bf16[128,16,128]{2,1,0:T(8,128)(2,1)S(1)}, u32[]{:S(2)}, u32[]{:S(2)}) async-start(bf16[128,16,128]{2,1,0:T(8,128)(2,1)} %sum_parts.1), calls=%async_computation.3 | async-start | bytes 1048576 | tf_op jit(solution)/shard_map/all_to_all | solution.py:862
  127.6 1.6 %copy-start.6 = (bf16[2048,512]{1,0:T(8,128)(2,1)S(1)}, bf16[2048,512]{1,0:T(8,128)(2,1)}, u32[]{:S(2)}) copy-start(bf16[2048,512]{1,0:T(8,128)(2,1)} %copy-done.5) | copy-start | bytes 6291460
